TPU v7x, 128 devices: a whole 4x4x4 slice. The times are simulated.
128 devices in a mesh: lon: 8 (over z_lo, x), lat: 16 (over y, z_hi, core).
Axes of the slice: x: 4, y: 4, z: 4 (z_hi: 2, z_lo: 2; z = z_hi * 2 + z_lo), core: 2. Of those that a mesh axis runs over, the one named last changes fastest.
Arguments:
- tracers: float32 [2, 16, 256, 2048], P(None, None, 'lat', 'lon'), may hold values from -6 to 6
- east_velocity: float32 [16, 256, 2048], P(None, 'lat', 'lon'), may hold values from -0.3 to 0.3
- north_velocity: float32 [16, 256, 2048], P(None, 'lat', 'lon'), may hold values from -0.3 to 0.3
- ocean_levels: int32 [256, 2048], P('lat', 'lon'), may hold values from 0 to 16
- fold_partner: int32 [2048], P('lon'), may hold values from 0 to 2047, as said below
- atm_flux: float32 [2, 65536], P(None, ('lon', 'lat')), may hold values from -6 to 6
- remap_index: int32 [4, 256, 2048], P(None, 'lat', 'lon'), may hold values from 0 to 65535
- remap_weight: float32 [4, 256, 2048], P(None, 'lat', 'lon'), may hold values from 0 to 0.5
Outputs:
- tracers_out: float32 [2, 16, 256, 2048], P(None, None, 'lat', 'lon')
Inputs may be any that keep to these rules, and one draw needn't show every extreme that they name: `fold_partner`: the partners of the columns of longitude tile t (global column i lies in tile i // 256) lie among the 512 columns of tiles (7 - t) mod 8 and (8 - t) mod 8; both of these tiles hold partners of tile t.
All inputs are finite; a program needn't handle non-finite values.
Results may differ from a plain program's by a relative error of at most 0.0003.
Values sent between devices are 32-bit elements; how exact they have to be, the bound alone decides.
No kernel may reach another device: no remote copies, remote signals or barrier semaphores. Data moves between devices by JAX's collectives and lax.ppermute only.
A program may use at most 128 MiB of HBM per device.

v0:
```python
import jax
import jax.numpy as jnp
from jax import lax
from jax.sharding import PartitionSpec as P

STEPS = 3


def extended_2(cells, sides, width, closed):
    for axis, dim in sides:
        count = lax.axis_size(axis)
        ends = count if closed else count - 1
        head = lax.slice_in_dim(cells, 0, width, axis=dim)
        tail = lax.slice_in_dim(cells, cells.shape[dim] - width, cells.shape[dim], axis=dim)
        cells = jnp.concatenate(
            [
                lax.ppermute(tail, axis, [(i, (i + 1) % count) for i in range(ends)]),
                cells,
                lax.ppermute(head, axis, [((i + 1) % count, i) for i in range(ends)]),
            ],
            axis=dim,
        )
    return cells


def laplace(values_in, east_mask, north_mask):
    east_flux = east_mask * (values_in[..., 1:] - values_in[..., :-1])
    north_flux = north_mask * (values_in[..., 1:, :] - values_in[..., :-1, :])
    return (
        east_flux[..., 1:-1, 1:]
        - east_flux[..., 1:-1, :-1]
        + (north_flux[..., 1:, 1:-1] - north_flux[..., :-1, 1:-1])
    )


def advance(extended, wet_mask, east_ext, north_ext, surface):
    east_mask = wet_mask[..., :-1] * wet_mask[..., 1:]
    north_mask = wet_mask[:, :-1, :] * wet_mask[:, 1:, :]
    lap_once = laplace(extended, east_mask, north_mask)
    inner_east = east_mask[:, 1:-1, 1:-1]
    inner_north = north_mask[:, 1:-1, 1:-1]
    lap_twice = laplace(lap_once, inner_east, inner_north)
    near_cells = extended[..., 1:-1, 1:-1]
    east_flux = (
        east_ext[:, 1:-1, 1:-2] * inner_east * 0.5 * (near_cells[..., :-1] + near_cells[..., 1:])
    )
    north_flux = (
        north_ext[:, 1:-2, 1:-1]
        * inner_north
        * 0.5
        * (near_cells[..., :-1, :] + near_cells[..., 1:, :])
    )
    spread = (
        east_flux[..., 1:-1, 1:]
        - east_flux[..., 1:-1, :-1]
        + (north_flux[..., 1:, 1:-1] - north_flux[..., :-1, 1:-1])
    )
    centre_cells = extended[..., 2:-2, 2:-2]
    wet_cells = wet_mask[:, 2:-2, 2:-2]
    vert_mask = wet_cells[:-1] * wet_cells[1:]
    vert_flux = vert_mask * (centre_cells[:, 1:] - centre_cells[:, :-1])
    zero_level = jnp.zeros_like(centre_cells[:, :1])
    vertical = jnp.concatenate([vert_flux, zero_level], axis=1) - jnp.concatenate(
        [zero_level, vert_flux], axis=1
    )
    forcing = jnp.concatenate([surface[:, None], jnp.zeros_like(centre_cells[:, 1:])], axis=1)
    tendency = (
        -spread
        + 0.08 * lap_once[..., 1:-1, 1:-1]
        - 0.01 * lap_twice
        + 0.1 * vertical
        + 0.5 * forcing
    )
    return centre_cells + wet_cells * tendency


def per_device(
    tracers,
    east_velocity,
    north_velocity,
    ocean_levels,
    fold_partner,
    atm_flux,
    remap_index,
    remap_weight,
):
    levels = tracers.shape[1]
    cols_dev = tracers.shape[3]
    lat_place = lax.axis_index("lat")
    is_top = lat_place == lax.axis_size("lat") - 1
    keep_top = jnp.where(is_top, 0.0, 1.0).astype(jnp.float32)
    north_fixed = north_velocity.at[:, -1, :].multiply(keep_top)
    statics = jnp.concatenate(
        [east_velocity, north_fixed, ocean_levels.astype(jnp.float32)[None]], axis=0
    )
    statics = extended_2(statics, (("lat", 1),), 2, False)
    static_ghost = jnp.concatenate(
        [
            jnp.zeros((2 * levels, 2, cols_dev), jnp.float32),
            jnp.full((1, 2, cols_dev), float(levels), jnp.float32),
        ],
        axis=0,
    )
    static_top = jnp.where(is_top, static_ghost, statics[:, -2:])
    statics = jnp.concatenate([statics[:, :-2], static_top], axis=1)
    statics = extended_2(statics, (("lon", 2),), 2, True)
    east_ext = statics[:levels]
    north_ext = statics[levels : 2 * levels]
    depth_ext = statics[2 * levels]
    level_index = jnp.arange(levels).astype(jnp.float32)
    wet_mask = (level_index[:, None, None] < depth_ext[None]).astype(jnp.float32)
    gathered = lax.all_gather(atm_flux, ("lon", "lat"), axis=1, tiled=True)
    surface = jnp.sum(remap_weight[None] * jnp.take(gathered, remap_index, axis=1), axis=1)
    tracer = tracers
    for repeat in range(STEPS):
        ghost_rows = jnp.stack([tracer[:, :, -1], tracer[:, :, -2]], axis=2)
        whole_rows = lax.all_gather(ghost_rows, "lon", axis=3, tiled=True)
        ghost_rows = jnp.take(whole_rows, fold_partner, axis=3)
        extended = extended_2(tracer, (("lat", 2),), 2, False)
        top_rows = jnp.where(is_top, ghost_rows, extended[:, :, -2:])
        extended = jnp.concatenate([extended[:, :, :-2], top_rows], axis=2)
        extended = extended_2(extended, (("lon", 3),), 2, True)
        tracer = advance(extended, wet_mask, east_ext, north_ext, surface)
    return tracer


def solution(mesh):
    return jax.shard_map(
        per_device,
        mesh=mesh,
        in_specs=(
            P(None, None, "lat", "lon"),
            P(None, "lat", "lon"),
            P(None, "lat", "lon"),
            P("lat", "lon"),
            P("lon"),
            P(None, ("lon", "lat")),
            P(None, "lat", "lon"),
            P(None, "lat", "lon"),
        ),
        out_specs=P(None, None, "lat", "lon"),
        check_vma=False,
    )
```

profile of v0, /device:TPU:1, one launch (start us, length us, event | category | flops | bytes accessed | tf_op | source)
XLA Modules:
  0.0 800.2 jit_solution(17099343849323046629)
XLA Ops:
  0.0 0.9 copy.141
  1.0 1.3 copy.128
  3.0 3.3 collective-permute-start.5
  6.3 5.5 collective-permute-start.4
  12.6 1.7 pad_maximum_fusion.38
  14.3 1.9 collective-permute-start.1
  16.2 5.1 collective-permute-start
  22.8 0.8 compare_select_fusion
  23.6 0.9 compare_and_fusion
  24.5 2.0 slice_subtract_fusion.32
  26.8 43.8 %all_gather.12 = f32[2,16,2,2048]{1,2,3,0:T(2,128)} all-gather(f32[2,16,2,256]{1,2,3,0:T(2,128)S(1)} %copy.114), channel_id=1, replica_groups=mesh['lon'=8,'lat'=16] {'lon'}, dimensions={3}, use_global_device_ids=true | all-gather | bytes 589824 | tf_op jit(solution)/shard_map/all_gather | solution.py:117
  70.6 3.5 gather_fusion.1
  74.6 448.2 %all_gather.13 = f32[2,65536]{0,1:T(8,128)} all-gather(f32[2,512]{0,1:T(8,128)S(1)} %copy.125), channel_id=1, replica_groups=mesh['lon'=8,'lat'=16] {'lon','lat'}, dimensions={1}, use_global_device_ids=true | all-gather | bytes 528384 | tf_op jit(solution)/shard_map/all_gather | solution.py:112
  522.9 65.2 %gather_fusion = f32[16384,2]{1,0:T(8,128)} fusion(f32[2,65536]{0,1:T(8,128)} %all_gather.13, s32[16384]{0:T(1024)S(1)} %broadcast_clamp_fusion), kind=kCustom, calls=%fused_computation.3 | custom fusion | bytes 327680 | tf_op jit(solution)/shard_map/jit(_take)/gather | solution.py:113
  588.1 7.0 multiply_reduce_fusion
  595.7 0.9 bitcast_select_fusion.2
  596.8 39.5 %collective-permute-start.7 = (f32[2,16,20,2]{3,1,2,0:T(8,128)S(1)}, f32[2,16,20,2]{3,1,2,0:T(8,128)S(1)}, u32[]{:S(2)}, u32[]{:S(2)}) collective-permute-start(f32[2,16,20,2]{3,1,2,0:T(8,128)S(1)} %get-tuple-element.25), channel_id=1, source_target_pairs={{16,0},{32,16},{48,32},{64,48},{80,64},{96,80},{112,96},{0,112},{1... | collective-permute-start | bytes 15368 | tf_op jit(solution)/shard_map/ppermute | solution.py:19
  636.3 0.9 broadcast_select_fusion
  637.6 3.6 collective-permute-start.3
  641.2 2.1 collective-permute-done.7
  643.3 4.6 collective-permute-done.6
  648.3 4.3 collective-permute-done.3
  652.6 4.0 collective-permute-done.2
  660.1 0.8 fusion.15
  662.8 1.0 fusion.56
  663.8 3.2 collective-permute-start.9
  667.1 25.3 %all_gather.14 = f32[2,16,2,2048]{3,1,2,0:T(8,128)} all-gather(f32[2,16,2,256]{3,1,2,0:T(8,128)S(1)} %pad_maximum_fusion.40), channel_id=1, replica_groups=mesh['lon'=8,'lat'=16] {'lon'}, dimensions={3}, use_global_device_ids=true | all-gather | bytes 589824 | tf_op jit(solution)/shard_map/all_gather | solution.py:117
  692.4 6.0 copy.129
  698.5 4.3 gather_fusion.2
  702.7 1.2 copy.130
  703.9 9.6 %collective-permute-start.8 = (f32[2,16,2,256]{3,1,2,0:T(8,128)S(1)}, f32[2,16,2,256]{3,1,2,0:T(8,128)S(1)}, u32[]{:S(2)}, u32[]{:S(2)}) collective-permute-start(f32[2,16,2,256]{3,1,2,0:T(8,128)S(1)} %get-tuple-element.36), channel_id=1, source_target_pairs={{0,1},{1,2},{2,3},{3,4},{4,5},{5,6},{6,7},{7,8},{8,9},{9,10},{10,1... | collective-permute-start | bytes 196616 | tf_op jit(solution)/shard_map/ppermute | solution.py:17
  713.6 6.7 collective-permute-done.8
  720.5 1.5 collective-permute-start.10
  722.1 4.4 collective-permute-done.11
  726.4 2.4 collective-permute-done.10
  731.8 1.0 fusion.46
  733.5 1.9 collective-permute-start.13
  735.4 25.0 %all_gather.15 = f32[2,16,2,2048]{3,1,2,0:T(8,128)} all-gather(f32[2,16,2,256]{3,1,2,0:T(8,128)S(1)} %pad_maximum_fusion.41), channel_id=1, replica_groups=mesh['lon'=8,'lat'=16] {'lon'}, dimensions={3}, use_global_device_ids=true | all-gather | bytes 589824 | tf_op jit(solution)/shard_map/all_gather | solution.py:117
  760.4 6.0 copy.131
  766.4 4.3 gather_fusion.3
  770.7 1.2 copy.132
  771.9 13.2 %collective-permute-start.12 = (f32[2,16,2,256]{3,1,2,0:T(8,128)}, f32[2,16,2,256]{3,1,2,0:T(8,128)S(1)}, u32[]{:S(2)}, u32[]{:S(2)}) collective-permute-start(f32[2,16,2,256]{3,1,2,0:T(8,128)} %get-tuple-element.32), channel_id=1, source_target_pairs={{0,1},{1,2},{2,3},{3,4},{4,5},{5,6},{6,7},{7,8},{8,9},{9,10},{10,1... | collective-permute-start | bytes 196616 | tf_op jit(solution)/shard_map/ppermute | solution.py:17
  785.2 1.6 collective-permute-done.12
  787.1 1.5 collective-permute-start.14
  788.6 4.4 collective-permute-done.15
  793.0 2.2 collective-permute-done.14
  798.1 1.0 fusion.35
  799.1 1.1 copy.133
  (114 shorter events, 17.5 us)
Async XLA Ops:
  3.0 592.8 %collective-permute-start.5 = (f32[2,16,2,256]{3,1,2,0:T(8,128)}, f32[2,16,2,256]{3,1,2,0:T(8,128)}, u32[]{:S(2)}, u32[]{:S(2)}) collective-permute-start(f32[2,16,2,256]{3,1,2,0:T(8,128)} %get-tuple-element.41), channel_id=1, source_target_pairs={{1,0},{2,1},{3,2},{4,3},{5,4},{6,5},{7,6},{8,7},{9,8},{10,9},{11,1... | collective-permute-start | bytes 196616 | tf_op jit(solution)/shard_map/ppermute | solution.py:19
  6.3 590.3 %collective-permute-start.4 = (f32[2,16,2,256]{3,1,2,0:T(8,128)}, f32[2,16,2,256]{3,1,2,0:T(8,128)S(1)}, u32[]{:S(2)}, u32[]{:S(2)}) collective-permute-start(f32[2,16,2,256]{3,1,2,0:T(8,128)} %get-tuple-element.40), channel_id=1, source_target_pairs={{0,1},{1,2},{2,3},{3,4},{4,5},{5,6},{6,7},{7,8},{8,9},{9,10},{10,1... | collective-permute-start | bytes 196616 | tf_op jit(solution)/shard_map/ppermute | solution.py:17
  12.6 61.8 %copy-start.15 = (f32[2,512]{1,0:T(2,128)S(1)}, f32[2,512]{1,0:T(2,128)}, u32[]{:S(2)}) copy-start(f32[2,512]{1,0:T(2,128)} %param.17) | copy-start | bytes 12292
  14.3 622.0 %collective-permute-start.1 = (f32[33,2,256]{2,1,0:T(2,128)}, f32[33,2,256]{2,1,0:T(2,128)}, u32[]{:S(2)}, u32[]{:S(2)}) collective-permute-start(f32[33,2,256]{2,1,0:T(2,128)} %get-tuple-element.31), channel_id=1, source_target_pairs={{1,0},{2,1},{3,2},{4,3},{5,4},{6,5},{7,6},{8,7},{9,8},{10,9},{11,1... | collective-permute-start | bytes 202760 | tf_op jit(solution)/shard_map/ppermute | solution.py:19
  16.2 621.0 %collective-permute-start = (f32[33,2,256]{2,1,0:T(2,128)}, f32[33,2,256]{2,1,0:T(2,128)S(1)}, u32[]{:S(2)}, u32[]{:S(2)}) collective-permute-start(f32[33,2,256]{2,1,0:T(2,128)} %get-tuple-element.30), channel_id=1, source_target_pairs={{0,1},{1,2},{2,3},{3,4},{4,5},{5,6},{6,7},{7,8},{8,9},{9,10},{10,1... | collective-permute-start | bytes 202760 | tf_op jit(solution)/shard_map/ppermute | solution.py:17
  74.6 513.5 %copy-start.14 = (f32[4,16,256]{2,1,0:T(8,128)S(1)}, f32[4,16,256]{2,1,0:T(8,128)}, u32[]{:S(2)}) copy-start(f32[4,16,256]{2,1,0:T(8,128)} %param.19) | copy-start | bytes 196612
  595.1 41.2 %copy-start.13 = (f32[33,2,256]{2,1,0:T(2,128)S(1)}, f32[33,2,256]{2,1,0:T(2,128)}, u32[]{:S(2)}) copy-start(f32[33,2,256]{2,1,0:T(2,128)} %constant.69.clone.1) | copy-start | bytes 202756
  595.1 42.2 %copy-start.4 = (f32[16,16,256]{2,1,0:T(8,128)S(1)}, f32[16,16,256]{2,1,0:T(8,128)}, u32[]{:S(2)}) copy-start(f32[16,16,256]{2,1,0:T(8,128)} %param.13) | copy-start | bytes 786436
  596.8 46.5 %collective-permute-start.7 = (f32[2,16,20,2]{3,1,2,0:T(8,128)S(1)}, f32[2,16,20,2]{3,1,2,0:T(8,128)S(1)}, u32[]{:S(2)}, u32[]{:S(2)}) collective-permute-start(f32[2,16,20,2]{3,1,2,0:T(8,128)S(1)} %get-tuple-element.25), channel_id=1, source_target_pairs={{16,0},{32,16},{48,32},{64,48},{80,64},{96,80},{112,96},{0,112},{1... | collective-permute-start | bytes 15368 | tf_op jit(solution)/shard_map/ppermute | solution.py:19
  636.3 11.6 %collective-permute-start.6 = (f32[2,16,20,2]{3,1,2,0:T(8,128)S(1)}, f32[2,16,20,2]{3,1,2,0:T(8,128)S(1)}, u32[]{:S(2)}, u32[]{:S(2)}) collective-permute-start(f32[2,16,20,2]{3,1,2,0:T(8,128)S(1)} %get-tuple-element.24), channel_id=1, source_target_pairs={{0,16},{16,32},{32,48},{48,64},{64,80},{80,96},{96,112},{112,0},{1... | collective-permute-start | bytes 15368 | tf_op jit(solution)/shard_map/ppermute | solution.py:17
  637.6 15.0 %collective-permute-start.3 = (f32[33,20,2]{2,1,0:T(8,128)S(1)}, f32[33,20,2]{2,1,0:T(8,128)S(1)}, u32[]{:S(2)}, u32[]{:S(2)}) collective-permute-start(f32[33,20,2]{2,1,0:T(8,128)S(1)} %get-tuple-element.19), channel_id=1, source_target_pairs={{16,0},{32,16},{48,32},{64,48},{80,64},{96,80},{112,96},{0,112},{1... | collective-permute-start | bytes 15848 | tf_op jit(solution)/shard_map/ppermute | solution.py:19
  641.2 15.4 %collective-permute-start.2 = (f32[33,20,2]{2,1,0:T(8,128)S(1)}, f32[33,20,2]{2,1,0:T(8,128)S(1)}, u32[]{:S(2)}, u32[]{:S(2)}) collective-permute-start(f32[33,20,2]{2,1,0:T(8,128)S(1)} %get-tuple-element.18), channel_id=1, source_target_pairs={{0,16},{16,32},{32,48},{48,64},{64,80},{80,96},{96,112},{112,0},{1... | collective-permute-start | bytes 15848 | tf_op jit(solution)/shard_map/ppermute | solution.py:17
  657.8 1.2 copy-start.5
  658.9 2.3 copy-start.1
  659.6 1.3 copy-start.12
  659.9 0.9 copy-start.9
  660.1 2.3 copy-start.6
  661.7 1.0 copy-start
  663.8 49.7 %collective-permute-start.9 = (f32[2,16,2,256]{3,1,2,0:T(8,128)S(1)}, f32[2,16,2,256]{3,1,2,0:T(8,128)S(1)}, u32[]{:S(2)}, u32[]{:S(2)}) collective-permute-start(f32[2,16,2,256]{3,1,2,0:T(8,128)S(1)} %get-tuple-element.37), channel_id=1, source_target_pairs={{1,0},{2,1},{3,2},{4,3},{5,4},{6,5},{7,6},{8,7},{9,8},{10,9},{11,1... | collective-permute-start | bytes 196616 | tf_op jit(solution)/shard_map/ppermute | solution.py:19
  692.4 29.6 %copy-start.10 = (f32[15,16,256]{2,0,1:T(8,128)S(1)}, f32[15,16,256]{2,0,1:T(8,128)}, u32[]{:S(2)}) copy-start(f32[15,16,256]{2,0,1:T(8,128)} %copy-done.9) | copy-start | bytes 737284
  703.9 16.3 %collective-permute-start.8 = (f32[2,16,2,256]{3,1,2,0:T(8,128)S(1)}, f32[2,16,2,256]{3,1,2,0:T(8,128)S(1)}, u32[]{:S(2)}, u32[]{:S(2)}) collective-permute-start(f32[2,16,2,256]{3,1,2,0:T(8,128)S(1)} %get-tuple-element.36), channel_id=1, source_target_pairs={{0,1},{1,2},{2,3},{3,4},{4,5},{5,6},{6,7},{7,8},{8,9},{9,10},{10,1... | collective-permute-start | bytes 196616 | tf_op jit(solution)/shard_map/ppermute | solution.py:17
  720.5 6.0 collective-permute-start.11
  720.5 8.3 %collective-permute-start.10 = (f32[2,16,20,2]{3,1,2,0:T(8,128)S(1)}, f32[2,16,20,2]{3,1,2,0:T(8,128)S(1)}, u32[]{:S(2)}, u32[]{:S(2)}) collective-permute-start(f32[2,16,20,2]{3,1,2,0:T(8,128)S(1)} %get-tuple-element.22), channel_id=1, source_target_pairs={{0,16},{16,32},{32,48},{48,64},{64,80},{80,96},{96,112},{112,0},{1... | collective-permute-start | bytes 15368 | tf_op jit(solution)/shard_map/ppermute | solution.py:17
  729.4 1.1 copy-start.2
  730.6 1.2 copy-start.7
  733.5 51.7 %collective-permute-start.13 = (f32[2,16,2,256]{3,1,2,0:T(8,128)S(1)}, f32[2,16,2,256]{3,1,2,0:T(8,128)S(1)}, u32[]{:S(2)}, u32[]{:S(2)}) collective-permute-start(f32[2,16,2,256]{3,1,2,0:T(8,128)S(1)} %get-tuple-element.33), channel_id=1, source_target_pairs={{1,0},{2,1},{3,2},{4,3},{5,4},{6,5},{7,6},{8,7},{9,8},{10,9},{11,1... | collective-permute-start | bytes 196616 | tf_op jit(solution)/shard_map/ppermute | solution.py:19
  760.4 28.1 %copy-start.11 = (f32[15,16,256]{2,0,1:T(8,128)S(1)}, f32[15,16,256]{2,0,1:T(8,128)}, u32[]{:S(2)}) copy-start(f32[15,16,256]{2,0,1:T(8,128)} %copy-done.9) | copy-start | bytes 737284
  771.9 14.8 %collective-permute-start.12 = (f32[2,16,2,256]{3,1,2,0:T(8,128)}, f32[2,16,2,256]{3,1,2,0:T(8,128)S(1)}, u32[]{:S(2)}, u32[]{:S(2)}) collective-permute-start(f32[2,16,2,256]{3,1,2,0:T(8,128)} %get-tuple-element.32), channel_id=1, source_target_pairs={{0,1},{1,2},{2,3},{3,4},{4,5},{5,6},{6,7},{7,8},{8,9},{9,10},{10,1... | collective-permute-start | bytes 196616 | tf_op jit(solution)/shard_map/ppermute | solution.py:17
  787.0 6.0 collective-permute-start.15
  787.1 8.1 %collective-permute-start.14 = (f32[2,16,20,2]{3,1,2,0:T(8,128)S(1)}, f32[2,16,20,2]{3,1,2,0:T(8,128)S(1)}, u32[]{:S(2)}, u32[]{:S(2)}) collective-permute-start(f32[2,16,20,2]{3,1,2,0:T(8,128)S(1)} %get-tuple-element.20), channel_id=1, source_target_pairs={{0,16},{16,32},{32,48},{48,64},{64,80},{80,96},{96,112},{112,0},{1... | collective-permute-start | bytes 15368 | tf_op jit(solution)/shard_map/ppermute | solution.py:17
  795.7 1.1 copy-start.3
  796.9 1.2 copy-start.8
where the time goes:
time: 802 us; the launch traced here: 800 us
  blocking collectives  542 us (68%)
  local copies, waits for them, and re-layouts  100 us (12%)
  starting transfers between devices  90 us (11%)
  waiting for transfers between devices  36.6 us (5%)
  other arithmetic  30.6 us (4%)
    all_gather x1, blocking collectives, per_device(): gathered = lax.all_gather(atm_flux, ('lon', 'lat'), axis=1, tiled=True)  448 us
    all_gather x3, blocking collectives, per_device(): whole_rows = lax.all_gather(ghost_rows, 'lon', axis=3, tiled=True)  94.2 us
    gather x1, local copies, waits for them, and re-layouts, per_device(): jnp.take(gathered, remap_index, axis=1)  65.2 us
    ppermute x8, starting transfers between devices, extended_2(): lax.ppermute(head, axis, [((i + 1) % count, i) for i in range(ends)])  53.6 us
    ppermute x8, starting transfers between devices, extended_2(): lax.ppermute(tail, axis, [(i, (i + 1) % count) for i in range(ends)])  36.3 us
    ppermute x8, waiting for transfers between devices, extended_2(): lax.ppermute(tail, axis, [(i, (i + 1) % count) for i in range(ends)])  21.5 us
  transfers between devices with their start and end apart: 16, of which 10 were waited for; matrix products, arithmetic and copies ran while one was open for 14% of the time, Pallas kernels for 0%

commit v1 on v0

v1 whole, which is shorter than its diff:
```python
import functools

import jax
import jax.numpy as jnp
from jax import lax
from jax.experimental import pallas as pl
from jax.experimental.pallas import tpu as pltpu
from jax.sharding import PartitionSpec as P

STEPS = 3
H = 8
VMEM = pl.BlockSpec(memory_space=pltpu.VMEM)
SMEM = pl.BlockSpec(memory_space=pltpu.SMEM)
PARAMS = pltpu.CompilerParams(vmem_limit_bytes=48 * 2**20)
F32 = jnp.float32
LANE_GATHER = lax.GatherDimensionNumbers(
    offset_dims=(),
    collapsed_slice_dims=(1,),
    start_index_map=(1,),
    operand_batching_dims=(0,),
    start_indices_batching_dims=(0,),
)


def lane_gather(values, lanes):
    return lax.gather(
        values, lanes[..., None], LANE_GATHER, (1, 1), mode=lax.GatherScatterMode.PROMISE_IN_BOUNDS
    )


def pick_columns(partner, sources):
    lanes = jnp.bitwise_and(partner, 127)
    place = jnp.right_shift(partner, 7)
    result = jnp.zeros((8, 128), F32)
    for tile, rows in sources:
        for half in range(2):
            got = lane_gather(rows[:, 128 * half : 128 * half + 128], lanes)
            result = jnp.where(place == 2 * tile + half, got, result)
    return result


def iota(shape, axis):
    return lax.broadcasted_iota(jnp.int32, shape, axis)


def pack_kernel(info, tracers, east, north, levels, weights, indices, partner, from_south, from_north, fold_a, fold_b, ghosts, to_west, to_east):
    tile, is_top = info[0], info[1] == 1
    wanted = jnp.broadcast_to(partner[...], (8, 256))
    for block in range(8):
        rows = pl.ds(8 * block, 8)
        sources = [(info[2], fold_a[rows, :]), (info[3], fold_b[rows, :])]
        for half in range(2):
            cut = slice(128 * half, 128 * half + 128)
            ghosts[rows, cut] = pick_columns(wanted[:, cut], sources)
    lane = iota((32, 128), 1)
    row = iota((32, 128), 0)
    ghost_first = jnp.logical_and(row == 24, is_top)
    ghost_second = jnp.logical_and(row == 25, is_top)
    last_north = jnp.logical_and(row == 23, is_top)
    beyond = jnp.logical_and(row >= 24, is_top)
    west_cut, east_cut = slice(0, 128), slice(128, 256)

    def whole(plane, centre, cut):
        return jnp.concatenate([from_south[plane, :, cut], centre, from_north[plane, :, cut]], axis=0)

    def value(plane, cut):
        if plane < 32:
            got = whole(plane, tracers[plane // 16, plane % 16, :, cut], cut)
            got = jnp.where(ghost_first, ghosts[plane : plane + 1, cut], got)
            return jnp.where(ghost_second, ghosts[32 + plane : 33 + plane, cut], got)
        if plane < 48:
            return whole(plane, east[plane - 32, :, cut], cut)
        if plane < 64:
            return jnp.where(last_north, 0.0, whole(plane, north[plane - 48, :, cut], cut))
        if plane < 68:
            return whole(plane, weights[plane - 64, :, cut], cut)
        if plane < 72:
            return whole(plane, indices[plane - 68, :, cut].astype(F32), cut)
        if plane == 72:
            return jnp.where(beyond, 16.0, whole(plane, levels[:, cut].astype(F32), cut))
        return jnp.broadcast_to(partner[:, cut].astype(F32), (32, 128))

    for group in range(5):
        first = jnp.zeros((32, 128), F32)
        last = jnp.zeros((32, 128), F32)
        for slot in range(16 if group < 4 else 10):
            mine = jnp.logical_and(lane >= 8 * slot, lane < 8 * slot + 8)
            plane = 16 * group + slot
            near = value(plane, west_cut)
            far = value(plane, east_cut)
            first = jnp.where(mine, pltpu.roll(near, 8 * slot, 1) if slot else near, first)
            last = jnp.where(mine, pltpu.roll(far, (8 * slot + 8) % 128, 1) if slot != 15 else far, last)
        to_west[group] = first
        to_east[group] = last


def one_hot_lookup(split_table, high, low, count):
    chosen = (iota((512, count), 0) == high).astype(F32).astype(jnp.bfloat16)
    got = jnp.dot(split_table[...], chosen, preferred_element_type=F32)
    lanes = iota((128, count), 0) == low
    first = jnp.sum(jnp.where(lanes, got[:128] + got[128:256], 0.0), axis=0, keepdims=True)
    second = jnp.sum(jnp.where(lanes, got[256:384] + got[384:], 0.0), axis=0, keepdims=True)
    return first, second


def split_place(index):
    high = jnp.bitwise_and(jnp.right_shift(index, 7), 3) * 128 + jnp.right_shift(index, 9)
    return high, jnp.bitwise_and(index, 127)


def lookup_kernel(table, weights, indices, from_south, from_north, surface, split_table, high, low, weight):
    for tracer in range(2):
        for quarter in range(4):
            block = table[:, tracer * 4 + quarter, :].T
            top = block.astype(jnp.bfloat16)
            rest = (block - top.astype(F32)).astype(jnp.bfloat16)
            cut = slice(128 * quarter, 128 * quarter + 128)
            split_table[tracer * 256 : tracer * 256 + 128, cut] = top
            split_table[tracer * 256 + 128 : tracer * 256 + 256, cut] = rest
    for j in range(4):
        index = jnp.concatenate(
            [from_south[68 + j].astype(jnp.int32), indices[j], from_north[68 + j].astype(jnp.int32)], axis=0
        )
        high[j], low[j] = split_place(index)
        weight[j] = jnp.concatenate([from_south[64 + j], weights[j], from_north[64 + j]], axis=0)
    surface[...] = jnp.zeros((2, 32, 256), F32)

    def body(step, carry):
        group, j = step // 4, step % 4
        rows = [pl.ds(4 + 4 * group + i, 1) for i in range(4)]
        join = lambda ref: jnp.concatenate([ref[j, r, :] for r in rows], axis=1)
        pair = one_hot_lookup(split_table, join(high), join(low), 1024)
        for i, r in enumerate(rows):
            scale = weight[j, r, :]
            for tracer in range(2):
                surface[tracer, r, :] += scale * pair[tracer][:, 256 * i : 256 * i + 256]
        return carry

    lax.fori_loop(0, 24, body, 0)


def spread_rows(halo, row_of, lane):
    moved = jnp.where(lane < 8, pltpu.roll(halo, 4, 1), jnp.zeros_like(halo))
    for shift in (8, 16, 32, 64):
        moved = moved + pltpu.roll(moved, shift, 1)
    return jnp.sum(jnp.where(lane // 8 == row_of, moved, jnp.zeros_like(moved)), axis=0, keepdims=True)


def gather_rows(packed, row_of, lane):
    moved = jnp.where(lane // 8 == row_of, jnp.broadcast_to(packed, (16, 128)), 0.0)
    for shift in (8, 16, 32, 64):
        moved = moved + pltpu.roll(moved, shift, 1)
    return pltpu.roll(moved, 124, 1)


def east_of(f):
    return pltpu.roll(f, f.shape[1] - 1, 1)


def west_of(f):
    return pltpu.roll(f, 1, 1)


def north_of(f):
    return pltpu.roll(f, f.shape[0] - 1, 0)


def south_of(f):
    return pltpu.roll(f, 1, 0)


def level_step(k, cells, upper, below_flux, coefficients, forcing):
    wet, vert_mask, east_mask, north_mask, east_near, east_far, north_near, north_far = coefficients
    cells_east, cells_north = east_of(cells), north_of(cells)
    grad_east = east_mask * (cells_east - cells)
    grad_north = north_mask * (cells_north - cells)
    lap = grad_east - west_of(grad_east) + (grad_north - south_of(grad_north))
    flux_east = east_far * cells_east - east_near * cells - (0.01 * east_mask) * (east_of(lap) - lap)
    flux_north = north_far * cells_north - north_near * cells - (0.01 * north_mask) * (north_of(lap) - lap)
    vert_flux = vert_mask * (upper - cells)
    tendency = flux_east - west_of(flux_east) + (flux_north - south_of(flux_north)) + 0.1 * (vert_flux - below_flux)
    if forcing is not None:
        tendency = tendency + forcing
    return cells + wet * tendency, vert_flux


def coefficients_of(k, depth, east_depth, north_depth, east, north):
    level = k.astype(F32) if hasattr(k, "astype") else float(k)
    one = lambda mask: mask.astype(F32)
    wet, vert_mask = one(level < depth), one(level + 1.0 < depth)
    east_mask, north_mask = one(level < east_depth), one(level < north_depth)
    half_east, half_north = 0.5 * east, 0.5 * north
    return (
        wet,
        vert_mask,
        east_mask,
        north_mask,
        east_mask * (0.08 + half_east),
        east_mask * (0.08 - half_east),
        north_mask * (0.08 + half_north),
        north_mask * (0.08 - half_north),
    )


def run_levels(load, depth, east_all, north_all, surface, store):
    east_depth = jnp.minimum(depth, east_of(depth))
    north_depth = jnp.minimum(depth, north_of(depth))
    shape = depth.shape

    def body(k, fluxes):
        coefficients = coefficients_of(k, depth, east_depth, north_depth, east_all[k], north_all[k])
        at_surface = jnp.where(k == 0, 0.5, 0.0).astype(F32)
        results = []
        for tracer in range(2):
            cells = load(tracer, k)
            upper = load(tracer, jnp.minimum(k + 1, 15))
            fresh, flux = level_step(k, cells, upper, fluxes[tracer], coefficients, at_surface * surface[tracer])
            store(tracer, k, fresh)
            results.append(flux)
        return tuple(results)

    lax.fori_loop(0, 16, body, (jnp.zeros(shape, F32), jnp.zeros(shape, F32)))


def first_kernel(
    info, tracers, east, north, levels, weights, indices, partner, from_south, from_north, ghosts, from_east, from_west,
    surface_main, split_table, cells_out, fold_out, east_ext, north_ext, depth_ext, surface_ext, partner_ext, start,
):
    is_top = info[1] == 1
    lane = iota((32, 128), 1)
    row = iota((32, 256), 0)
    last_north = jnp.logical_and(row == 23, is_top)

    def halo(group, slot):
        shift = (lambda v: v % 128) if isinstance(slot, int) else (lambda v: lax.rem(v, 128))
        near = pltpu.roll(from_east[group], shift(128 - 8 * slot), 1)
        far = pltpu.roll(from_west[group], shift(248 - 8 * slot), 1)
        return jnp.where(lane < 8, near, jnp.where(lane >= 120, far, 0.0))

    def whole(plane, centre):
        return jnp.concatenate([from_south[plane], centre, from_north[plane]], axis=0)

    def fill(k, carry):
        for tracer in range(2):
            start[tracer, k, :, 0:256] = whole(tracer * 16 + k, tracers[tracer, k])
            start[tracer, k, :, 256:384] = halo(tracer, k)
        east_ext[k, :, 0:256] = whole(32 + k, east[k])
        east_ext[k, :, 256:384] = halo(2, k)
        north_ext[k, :, 0:256] = jnp.where(last_north, 0.0, whole(48 + k, north[k]))
        north_ext[k, :, 256:384] = halo(3, k)
        return carry

    lax.fori_loop(0, 16, fill, 0)

    @pl.when(is_top)
    def _():
        def place(k, carry):
            for tracer in range(2):
                for r in range(2):
                    start[tracer, k, 24 + r : 25 + r, 0:256] = ghosts[pl.ds(32 * r + 16 * tracer + k, 1), :]
            return carry

        lax.fori_loop(0, 16, place, 0)

    depth_ext[:, 0:256] = jnp.where(
        jnp.logical_and(row >= 24, is_top), 16.0, whole(72, levels[...].astype(F32))
    )
    depth_ext[:, 256:384] = halo(4, 8)
    partner_ext[:, 0:256] = jnp.broadcast_to(partner[...], (8, 256))
    partner_ext[:, 256:384] = halo(4, 9)[0:8].astype(jnp.int32)

    small_lane, small_row = iota((16, 128), 1), iota((16, 128), 0)
    places, scales = [], []
    for j in range(4):
        index, weight = halo(4, 4 + j), halo(4, j)
        for part in range(2):
            cut = slice(16 * part, 16 * part + 16)
            places.append(spread_rows(index[cut], small_row, small_lane).astype(jnp.int32))
            scales.append(spread_rows(weight[cut], small_row, small_lane))
    high, low = split_place(jnp.concatenate(places, axis=1))
    pair = one_hot_lookup(split_table, high, low, 1024)
    surface_ext[:, :, 0:256] = surface_main[...]
    for tracer in range(2):
        for part in range(2):
            total = jnp.zeros((1, 128), F32)
            for j in range(4):
                at = 2 * j + part
                total += scales[at] * pair[tracer][:, 128 * at : 128 * at + 128]
            surface_ext[tracer, 16 * part : 16 * part + 16, 256:384] = gather_rows(total, small_row, small_lane)

    def store(tracer, k, fresh):
        cells_out[tracer, k] = fresh
        for r in range(2):
            fold_out[pl.ds(32 * r + 16 * tracer + k, 1), :] = fresh[23 - r : 24 - r, 0:256]

    surfaces = [surface_ext[0], surface_ext[1]]
    run_levels(lambda tracer, k: start[tracer, k], depth_ext[...], east_ext, north_ext, surfaces, store)


def next_kernel(last, info, cells, east_ext, north_ext, depth_ext, surface_ext, partner_ext, fold_a, fold_b, fold_c, fold_d, *outs):
    if last:
        cells_out, ghosts = outs
    else:
        cells_out, fold_out, ghosts = outs
    is_top = info[1] == 1

    @pl.when(is_top)
    def _():
        def block_body(block, carry):
            rows = pl.ds(pl.multiple_of(8 * block, 8), 8)
            near = [(info[2], fold_a[rows, :]), (info[3], fold_b[rows, :])]
            wide = near + [(info[4], fold_c[rows, :]), (info[5], fold_d[rows, :])]
            for part, sources in enumerate((near, near, wide)):
                cut = slice(128 * part, 128 * part + 128)
                ghosts[rows, cut] = pick_columns(partner_ext[:, cut], sources)
            return carry

        lax.fori_loop(0, 8, block_body, 0)

    row = iota((32, 384), 0)
    ghost_first = jnp.logical_and(row == 24, is_top)
    ghost_second = jnp.logical_and(row == 25, is_top)

    def load(tracer, k):
        plane = 16 * tracer + k
        got = cells[tracer, k]
        got = jnp.where(ghost_first, ghosts[pl.ds(plane, 1), :], got)
        return jnp.where(ghost_second, ghosts[pl.ds(32 + plane, 1), :], got)

    def store(tracer, k, fresh):
        if last:
            cells_out[tracer, k] = fresh[8:24, 0:256]
        else:
            cells_out[tracer, k] = fresh
            for r in range(2):
                fold_out[pl.ds(32 * r + 16 * tracer + k, 1), :] = fresh[23 - r : 24 - r, 0:256]

    surfaces = [surface_ext[0], surface_ext[1]]
    run_levels(load, depth_ext[...], east_ext, north_ext, surfaces, store)


def call(kernel, ins, outs, scratch=(), cost=None):
    return pl.pallas_call(
        kernel,
        out_shape=tuple(jax.ShapeDtypeStruct(s, d) for s, d in outs),
        in_specs=[SMEM if i == 0 and v.shape == (6,) else VMEM for i, v in enumerate(ins)],
        out_specs=tuple(VMEM for _ in outs),
        scratch_shapes=list(scratch),
        compiler_params=PARAMS,
        cost_estimate=cost,
    )(*ins)


def per_device(tracers, east, north, levels, partner, atm_flux, indices, weights):
    nlon, nlat = lax.axis_size("lon"), lax.axis_size("lat")
    both = ("lon", "lat")
    t, lat = lax.axis_index("lon"), lax.axis_index("lat")
    is_top = (lat == nlat - 1).astype(jnp.int32)
    tiles = [jnp.remainder(nlon - 1 - t + d, nlon) for d in (0, 1, -1, 2)]
    info = jnp.stack([t, is_top] + tiles).astype(jnp.int32)
    top = nlat - 1

    def fold_permutes(rows, shifts):
        return [
            lax.ppermute(rows, both, [(i * nlat + top, ((nlon - 1 + d - i) % nlon) * nlat + top) for i in range(nlon)])
            for d in shifts
        ]

    def cut(a, rows):
        return a[..., rows, :].reshape((-1, H, a.shape[-1])).astype(F32)

    pieces = (tracers, east, north, weights, indices, levels)
    northward = jnp.concatenate([cut(a, slice(8, 16)) for a in pieces], axis=0)
    southward = jnp.concatenate([cut(a, slice(0, 8)) for a in pieces], axis=0)
    from_south = lax.ppermute(northward, "lat", [(i, i + 1) for i in range(nlat - 1)])
    from_north = lax.ppermute(southward, "lat", [(i + 1, i) for i in range(nlat - 1)])
    fold_rows = jnp.concatenate(
        [tracers[:, :, 15].reshape(32, -1), tracers[:, :, 14].reshape(32, -1)], axis=0
    )
    fold_a, fold_b = fold_permutes(fold_rows, (0, 1))

    block = atm_flux.reshape(8, 128)
    slots = jnp.broadcast_to(block[None], (nlon * nlat, 8, 128))
    table = lax.all_to_all(slots, both, 0, 0, tiled=True)

    partner_row = partner.reshape(1, -1)
    ghosts, to_west, to_east = call(
        pack_kernel,
        (info, tracers, east, north, levels, weights, indices, partner_row, from_south, from_north, fold_a, fold_b),
        [((64, 256), F32), ((5, 32, 128), F32), ((5, 32, 128), F32)],
    )
    from_east = lax.ppermute(to_west, "lon", [((i + 1) % nlon, i) for i in range(nlon)])
    from_west = lax.ppermute(to_east, "lon", [(i, (i + 1) % nlon) for i in range(nlon)])

    surface, split_table = call(
        lookup_kernel,
        (table, weights, indices, from_south, from_north),
        [((2, 32, 256), F32), ((512, 512), jnp.bfloat16)],
        [pltpu.VMEM((4, 32, 256), jnp.int32), pltpu.VMEM((4, 32, 256), jnp.int32), pltpu.VMEM((4, 32, 256), F32)],
        pl.CostEstimate(flops=2 * 512 * 512 * 24576, bytes_accessed=4 * 2**20, transcendentals=0),
    )

    wide = (2, 16, 32, 384)
    cells, fold_rows, east_ext, north_ext, depth_ext, surface_ext, partner_ext = call(
        first_kernel,
        (info, tracers, east, north, levels, weights, indices, partner_row, from_south, from_north, ghosts, from_east,
         from_west, surface, split_table),
        [(wide, F32), ((64, 256), F32), (wide[1:], F32), (wide[1:], F32), ((32, 384), F32), ((2, 32, 384), F32),
         ((8, 384), jnp.int32)],
        [pltpu.VMEM(wide, F32)],
    )
    for step in range(1, STEPS):
        last = step == STEPS - 1
        received = fold_permutes(fold_rows, (0, 1, -1, 2))
        outs = call(
            functools.partial(next_kernel, last),
            (info, cells, east_ext, north_ext, depth_ext, surface_ext, partner_ext, *received),
            [(tracers.shape, F32)] if last else [(wide, F32), ((64, 256), F32)],
            [pltpu.VMEM((64, 384), F32)],
        )
        if last:
            return outs[0]
        cells, fold_rows = outs


def solution(mesh):
    return jax.shard_map(
        per_device,
        mesh=mesh,
        in_specs=(
            P(None, None, "lat", "lon"),
            P(None, "lat", "lon"),
            P(None, "lat", "lon"),
            P("lat", "lon"),
            P("lon"),
            P(None, ("lon", "lat")),
            P(None, "lat", "lon"),
            P(None, "lat", "lon"),
        ),
        out_specs=P(None, None, "lat", "lon"),
        check_vma=False,
    )
```

time: 802 us -> 118 us (0.15)
  the two profiles are of different devices: /device:TPU:1 before, /device:TPU:121 now
where the time goes in v1:
time: 118 us; the launch traced here: 116 us
  starting transfers between devices  55.6 us (47%)
  Pallas kernels  45.4 us (38%)
  waiting for transfers between devices  6.78 us (6%)
  local copies, waits for them, and re-layouts  6.45 us (5%)
  other arithmetic  1.26 us (1%)
    pallas_call x5, Pallas kernels, call(): pl.pallas_call(kernel, out_shape=tuple((jax.ShapeDtypeStruct(s, d) for s,...  45.4 us
    ppermute x10, starting transfers between devices, fold_permutes(): lax.ppermute(rows, both, [(i * nlat + top, (nlon - 1 + d - i) % nlon * nl...  34.6 us
    all_to_all x1, starting transfers between devices, per_device(): table = lax.all_to_all(slots, both, 0, 0, tiled=True)  13.5 us
    ppermute x10, waiting for transfers between devices, fold_permutes(): lax.ppermute(rows, both, [(i * nlat + top, (nlon - 1 + d - i) % nlon * nl...  6.77 us
    unnamed x24, local copies, waits for them, and re-layouts  4.35 us
    ppermute x1, starting transfers between devices, per_device(): lax.ppermute(to_west, 'lon', [((i + 1) % nlon, i) for i in range(nlon)])  3.63 us
    ppermute x1, starting transfers between devices, per_device(): lax.ppermute(southward, 'lat', [(i + 1, i) for i in range(nlat - 1)])  2.6 us
  transfers between devices with their start and end apart: 15, of which 3 were waited for; matrix products, arithmetic and copies ran while one was open for 1% of the time, Pallas kernels for 18%

profile of v1, /device:TPU:121, one launch (start us, length us, event | category | flops | bytes accessed | tf_op | source)
XLA Modules:
  0.0 115.9 jit_solution(6134136604472198314)
XLA Ops:
  0.0 0.0 copy-start.5
  0.0 0.0 copy-start.6
  0.0 1.1 fusion.1
  1.2 0.8 constant_dynamic-update-slice_fusion.1
  2.0 0.7 slice_dynamic-update-slice_fusion.1
  2.7 0.7 slice_dynamic-update-slice_fusion
  3.5 0.6 slice_dynamic-update-slice_fusion.4
  4.1 0.6 convert_dynamic-update-slice_fusion
  4.7 0.6 constant_dynamic-update-slice_fusion.2
  5.3 2.6 %collective-permute-start.1 = (f32[73,8,256]{2,1,0:T(8,128)}, f32[73,8,256]{2,1,0:T(8,128)S(1)}, u32[]{:S(2)}, u32[]{:S(2)}) collective-permute-start(f32[73,8,256]{2,1,0:T(8,128)} %get-tuple-element.45), channel_id=1, source_target_pairs={{1,0},{2,1},{3,2},{4,3},{5,4},{6,5},{7,6},{8,7},{9,8},{10,9},{11,1... | collective-permute-start | bytes 1794056 | tf_op jit(solution)/shard_map/ppermute | solution.py:376
  8.0 1.3 %collective-permute-start = (f32[73,8,256]{2,1,0:T(8,128)}, f32[73,8,256]{2,1,0:T(8,128)S(1)}, u32[]{:S(2)}, u32[]{:S(2)}) collective-permute-start(f32[73,8,256]{2,1,0:T(8,128)} %get-tuple-element.46), channel_id=1, source_target_pairs={{0,1},{1,2},{2,3},{3,4},{4,5},{5,6},{6,7},{7,8},{8,9},{9,10},{10,1... | collective-permute-start | bytes 1794056 | tf_op jit(solution)/shard_map/ppermute | solution.py:375
  9.3 0.8 broadcast_in_dim.8
  10.1 13.5 %all-to-all-start = ((f32[128,8,128]{2,1,0:T(8,128)}), f32[128,8,128]{2,1,0:T(8,128)S(1)}, u32[]{:S(2)}, u32[]{:S(2)}) async-start(f32[128,8,128]{2,1,0:T(8,128)} %broadcast_in_dim.8), calls=%async_computation | async-start | bytes 1048576 | tf_op jit(solution)/shard_map/all_to_all | solution.py:384
  23.6 0.1 fusion
  23.7 0.7 collective-permute-start.3
  24.4 7.6 %collective-permute-start.2 = (f32[64,256]{1,0:T(8,128)S(1)}, f32[64,256]{1,0:T(8,128)S(1)}, u32[]{:S(2)}, u32[]{:S(2)}) collective-permute-start(f32[64,256]{1,0:T(8,128)S(1)} %pad_maximum_fusion), channel_id=1, source_target_pairs={{15,127},{31,111},{47,95},{63,79},{79,63},{95,47},{111,31},{127,15}} | collective-permute-start | bytes 196616 | tf_op jit(solution)/shard_map/ppermute | solution.py:365
  32.1 0.1 stack.31.info
  32.2 0.0 collective-permute-done.3.fold_b
  32.2 1.5 %collective-permute-done.2.fold_a = f32[64,256]{1,0:T(8,128)S(1)} collective-permute-done((f32[64,256]{1,0:T(8,128)S(1)}, f32[64,256]{1,0:T(8,128)S(1)}, u32[]{:S(2)}, u32[]{:S(2)}) %collective-permute-start.2) | collective-permute-done | bytes 65568 | tf_op jit(solution)/shard_map/ppermute | solution.py:365
  33.7 0.0 collective-permute-done.1.from_north
  33.7 0.0 collective-permute-done.from_south
  33.7 1.4 %shard_map.82 = (f32[64,256]{1,0:T(8,128)S(1)}, f32[5,32,128]{2,1,0:T(8,128)S(1)}, f32[5,32,128]{2,1,0:T(8,128)S(1)}) custom-call(s32[6]{0:T(128)S(1)} %stack.31.info, f32[2,16,16,256]{3,2,1,0:T(8,128)S(1)} %copy-done, f32[16,16,256]{2,1,0:T(8,128)S(1)} %copy-done.1, f32[16,16,256]{2,1,0:T(8,128)S(1)} %copy-done.2, s32[16,256]{1,0:T(8,128)S(1)} %copy-done.6, ...), custom_call_target="tpu_custom_call" | custom-call | tf_op jit(solution)/shard_map/pallas_call | solution.py:343
  35.1 3.6 %collective-permute-start.4 = (f32[5,32,128]{2,1,0:T(8,128)S(1)}, f32[5,32,128]{2,1,0:T(8,128)S(1)}, u32[]{:S(2)}, u32[]{:S(2)}) collective-permute-start(f32[5,32,128]{2,1,0:T(8,128)S(1)} %get-tuple-element.20), channel_id=1, source_target_pairs={{16,0},{32,16},{48,32},{64,48},{80,64},{96,80},{112,96},{0,112},{1... | collective-permute-start | bytes 245768 | tf_op jit(solution)/shard_map/ppermute | solution.py:392
  38.7 0.0 collective-permute-start.5
  38.7 0.0 all-to-all-done.table
  38.7 19.0 %shard_map.83 = (f32[2,32,256]{2,1,0:T(8,128)S(1)}, bf16[512,512]{1,0:T(8,128)(2,1)S(1)}) custom-call(f32[128,8,128]{2,1,0:T(8,128)S(1)} %all-to-all-done.table, f32[4,16,256]{2,1,0:T(8,128)S(1)} %copy-done.4, s32[4,16,256]{2,1,0:T(8,128)S(1)} %copy-done.5, f32[73,8,256]{2,1,0:T(8,128)S(1)} %collective-permute-done.from_south, ...), custom_call_target="tpu_custom_call" | custom-call | flops 12884901888 | bytes 4194304 | tf_op jit(solution)/shard_map/pallas_call | solution.py:343
  57.8 0.0 collective-permute-done.4.from_east
  57.8 0.0 collective-permute-done.5.from_west
  57.8 10.7 %shard_map.84 = (f32[2,16,32,384]{3,2,1,0:T(8,128)}, f32[64,256]{1,0:T(8,128)S(1)}, f32[16,32,384]{2,1,0:T(8,128)S(1)}, f32[16,32,384]{2,1,0:T(8,128)S(1)}, f32[...) custom-call(s32[6]{0:T(128)S(1)} %stack.31.info, f32[2,16,16,256]{3,2,1,0:T(8,128)S(1)} %copy-done, ...), custom_call_target="tpu_custom_call" | custom-call | tf_op jit(solution)/shard_map/pallas_call | solution.py:343
  68.5 1.9 %collective-permute-start.9 = (f32[64,256]{1,0:T(8,128)S(1)}, f32[64,256]{1,0:T(8,128)S(1)}, u32[]{:S(2)}, u32[]{:S(2)}) collective-permute-start(f32[64,256]{1,0:T(8,128)S(1)} %get-tuple-element.30), channel_id=1, source_target_pairs={{15,31},{31,15},{47,127},{63,111},{79,95},{95,79},{111,63},{127,47}} | collective-permute-start | bytes 196616 | tf_op jit(solution)/shard_map/ppermute | solution.py:365
  70.4 6.7 %collective-permute-start.8 = (f32[64,256]{1,0:T(8,128)S(1)}, f32[64,256]{1,0:T(8,128)S(1)}, u32[]{:S(2)}, u32[]{:S(2)}) collective-permute-start(f32[64,256]{1,0:T(8,128)S(1)} %get-tuple-element.30), channel_id=1, source_target_pairs={{15,111},{31,95},{47,79},{63,63},{79,47},{95,31},{111,15},{127,127}} | collective-permute-start | bytes 196616 | tf_op jit(solution)/shard_map/ppermute | solution.py:365
  77.1 0.7 collective-permute-start.7
  77.8 3.4 %collective-permute-start.6 = (f32[64,256]{1,0:T(8,128)S(1)}, f32[64,256]{1,0:T(8,128)S(1)}, u32[]{:S(2)}, u32[]{:S(2)}) collective-permute-start(f32[64,256]{1,0:T(8,128)S(1)} %get-tuple-element.30), channel_id=1, source_target_pairs={{15,127},{31,111},{47,95},{63,79},{79,63},{95,47},{111,31},{127,15}} | collective-permute-start | bytes 196616 | tf_op jit(solution)/shard_map/ppermute | solution.py:365
  81.3 0.0 collective-permute-done.9.fold_d
  81.3 0.0 collective-permute-done.8.fold_c
  81.3 0.0 collective-permute-done.7.fold_b
  81.3 3.6 %collective-permute-done.6.fold_a = f32[64,256]{1,0:T(8,128)S(1)} collective-permute-done((f32[64,256]{1,0:T(8,128)S(1)}, f32[64,256]{1,0:T(8,128)S(1)}, u32[]{:S(2)}, u32[]{:S(2)}) %collective-permute-start.6) | collective-permute-done | bytes 65568 | tf_op jit(solution)/shard_map/ppermute | solution.py:365
  84.9 1.4 %copy-done.3 = f32[2,16,32,384]{3,2,1,0:T(8,128)S(1)} copy-done((f32[2,16,32,384]{3,2,1,0:T(8,128)S(1)}, f32[2,16,32,384]{3,2,1,0:T(8,128)}, u32[]{:S(2)}) %copy-start.3) | copy-done | bytes 1572888
  86.3 7.1 %shard_map.85 = (f32[2,16,32,384]{3,2,1,0:T(8,128)S(1)}, f32[64,256]{1,0:T(8,128)S(1)}) custom-call(s32[6]{0:T(128)S(1)} %stack.31.info, f32[2,16,32,384]{3,2,1,0:T(8,128)S(1)} %copy-done.3, f32[16,32,384]{2,1,0:T(8,128)S(1)} %get-tuple-element.25.east_ext, f32[16,32,384]{2,1,0:T(8,128)S(1)} %get-tuple-element.26.north_ext, ...), custom_call_target="tpu_custom_call" | custom-call | tf_op jit(solution)/shard_map/pallas_call | solution.py:343
  93.4 1.9 %collective-permute-start.13 = (f32[64,256]{1,0:T(8,128)S(1)}, f32[64,256]{1,0:T(8,128)S(1)}, u32[]{:S(2)}, u32[]{:S(2)}) collective-permute-start(f32[64,256]{1,0:T(8,128)S(1)} %get-tuple-element.32), channel_id=1, source_target_pairs={{15,31},{31,15},{47,127},{63,111},{79,95},{95,79},{111,63},{127,47}} | collective-permute-start | bytes 196616 | tf_op jit(solution)/shard_map/ppermute | solution.py:365
  95.3 5.4 %collective-permute-start.12 = (f32[64,256]{1,0:T(8,128)S(1)}, f32[64,256]{1,0:T(8,128)S(1)}, u32[]{:S(2)}, u32[]{:S(2)}) collective-permute-start(f32[64,256]{1,0:T(8,128)S(1)} %get-tuple-element.32), channel_id=1, source_target_pairs={{15,111},{31,95},{47,79},{63,63},{79,47},{95,31},{111,15},{127,127}} | collective-permute-start | bytes 196616 | tf_op jit(solution)/shard_map/ppermute | solution.py:365
  100.8 0.7 collective-permute-start.11
  101.5 5.5 %collective-permute-start.10 = (f32[64,256]{1,0:T(8,128)S(1)}, f32[64,256]{1,0:T(8,128)S(1)}, u32[]{:S(2)}, u32[]{:S(2)}) collective-permute-start(f32[64,256]{1,0:T(8,128)S(1)} %get-tuple-element.32), channel_id=1, source_target_pairs={{15,127},{31,111},{47,95},{63,79},{79,63},{95,47},{111,31},{127,15}} | collective-permute-start | bytes 196616 | tf_op jit(solution)/shard_map/ppermute | solution.py:365
  107.0 0.0 collective-permute-done.13.fold_d
  107.0 0.0 collective-permute-done.12.fold_c
  107.0 0.0 collective-permute-done.11.fold_b
  107.0 1.6 %collective-permute-done.10.fold_a = f32[64,256]{1,0:T(8,128)S(1)} collective-permute-done((f32[64,256]{1,0:T(8,128)S(1)}, f32[64,256]{1,0:T(8,128)S(1)}, u32[]{:S(2)}, u32[]{:S(2)}) %collective-permute-start.10) | collective-permute-done | bytes 65568 | tf_op jit(solution)/shard_map/ppermute | solution.py:365
  108.6 7.3 %shard_map.86 = f32[2,16,16,256]{3,2,1,0:T(8,128)} custom-call(s32[6]{0:T(128)S(1)} %stack.31.info, f32[2,16,32,384]{3,2,1,0:T(8,128)S(1)} %get-tuple-element.31.cells, f32[16,32,384]{2,1,0:T(8,128)S(1)} %get-tuple-element.25.east_ext, f32[16,32,384]{2,1,0:T(8,128)S(1)} %get-tuple-element.26.north_ext, f32[32,384]{1,0:T(8,128)S(1)} %get-tuple-element.27.depth_ext, ...), custom_call_target="tpu_custom_call" | custom-call | tf_op jit(solution)/shard_map/pallas_call | solution.py:343
  (19 shorter events, 0.1 us)
Async XLA Ops:
  0.0 2.0 %copy-start.1 = (f32[16,16,256]{2,1,0:T(8,128)S(1)}, f32[16,16,256]{2,1,0:T(8,128)}, u32[]{:S(2)}) copy-start(f32[16,16,256]{2,1,0:T(8,128)} %east.3) | copy-start | bytes 786436
  0.0 2.7 %copy-start.2 = (f32[16,16,256]{2,1,0:T(8,128)S(1)}, f32[16,16,256]{2,1,0:T(8,128)}, u32[]{:S(2)}) copy-start(f32[16,16,256]{2,1,0:T(8,128)} %north.3) | copy-start | bytes 786436
  0.0 3.5 %copy-start.4 = (f32[4,16,256]{2,1,0:T(8,128)S(1)}, f32[4,16,256]{2,1,0:T(8,128)}, u32[]{:S(2)}) copy-start(f32[4,16,256]{2,1,0:T(8,128)} %weights.5) | copy-start | bytes 196612
  0.0 4.1 %copy-start.5 = (s32[4,16,256]{2,1,0:T(8,128)S(1)}, s32[4,16,256]{2,1,0:T(8,128)}, u32[]{:S(2)}) copy-start(s32[4,16,256]{2,1,0:T(8,128)} %indices.5) | copy-start | bytes 196612
  0.0 4.7 %copy-start.6 = (s32[16,256]{1,0:T(8,128)S(1)}, s32[16,256]{1,0:T(8,128)}, u32[]{:S(2)}) copy-start(s32[16,256]{1,0:T(8,128)} %levels.3) | copy-start | bytes 49156
  0.0 9.2 %copy-start.8 = (f32[2,512]{1,0:T(2,128)S(1)}, f32[2,512]{1,0:T(2,128)}, u32[]{:S(2)}) copy-start(f32[2,512]{1,0:T(2,128)} %param.13) | copy-start | bytes 12292
  2.0 21.6 %copy-start = (f32[2,16,16,256]{3,2,1,0:T(8,128)S(1)}, f32[2,16,16,256]{3,2,1,0:T(8,128)}, u32[]{:S(2)}) copy-start(f32[2,16,16,256]{3,2,1,0:T(8,128)} %tracers.3) | copy-start | bytes 1572868
  2.7 31.0 %copy-start.7 = (s32[256]{0:T(256)S(1)}, s32[256]{0:T(256)}, u32[]{:S(2)}) copy-start(s32[256]{0:T(256)} %param.12) | copy-start | bytes 3076
  5.3 28.4 %collective-permute-start.1 = (f32[73,8,256]{2,1,0:T(8,128)}, f32[73,8,256]{2,1,0:T(8,128)S(1)}, u32[]{:S(2)}, u32[]{:S(2)}) collective-permute-start(f32[73,8,256]{2,1,0:T(8,128)} %get-tuple-element.45), channel_id=1, source_target_pairs={{1,0},{2,1},{3,2},{4,3},{5,4},{6,5},{7,6},{8,7},{9,8},{10,9},{11,1... | collective-permute-start | bytes 1794056 | tf_op jit(solution)/shard_map/ppermute | solution.py:376
  8.0 25.8 %collective-permute-start = (f32[73,8,256]{2,1,0:T(8,128)}, f32[73,8,256]{2,1,0:T(8,128)S(1)}, u32[]{:S(2)}, u32[]{:S(2)}) collective-permute-start(f32[73,8,256]{2,1,0:T(8,128)} %get-tuple-element.46), channel_id=1, source_target_pairs={{0,1},{1,2},{2,3},{3,4},{4,5},{5,6},{6,7},{7,8},{8,9},{9,10},{10,1... | collective-permute-start | bytes 1794056 | tf_op jit(solution)/shard_map/ppermute | solution.py:375
  10.1 28.6 %all-to-all-start = ((f32[128,8,128]{2,1,0:T(8,128)}), f32[128,8,128]{2,1,0:T(8,128)S(1)}, u32[]{:S(2)}, u32[]{:S(2)}) async-start(f32[128,8,128]{2,1,0:T(8,128)} %broadcast_in_dim.8), calls=%async_computation | async-start | bytes 1048576 | tf_op jit(solution)/shard_map/all_to_all | solution.py:384
  23.7 8.5 %collective-permute-start.3 = (f32[64,256]{1,0:T(8,128)S(1)}, f32[64,256]{1,0:T(8,128)S(1)}, u32[]{:S(2)}, u32[]{:S(2)}) collective-permute-start(f32[64,256]{1,0:T(8,128)S(1)} %pad_maximum_fusion), channel_id=1, source_target_pairs={{15,15},{31,127},{47,111},{63,95},{79,79},{95,63},{111,47},{127,31}} | collective-permute-start | bytes 196616 | tf_op jit(solution)/shard_map/ppermute | solution.py:365
  24.4 9.3 %collective-permute-start.2 = (f32[64,256]{1,0:T(8,128)S(1)}, f32[64,256]{1,0:T(8,128)S(1)}, u32[]{:S(2)}, u32[]{:S(2)}) collective-permute-start(f32[64,256]{1,0:T(8,128)S(1)} %pad_maximum_fusion), channel_id=1, source_target_pairs={{15,127},{31,111},{47,95},{63,79},{79,63},{95,47},{111,31},{127,15}} | collective-permute-start | bytes 196616 | tf_op jit(solution)/shard_map/ppermute | solution.py:365
  35.1 22.7 %collective-permute-start.4 = (f32[5,32,128]{2,1,0:T(8,128)S(1)}, f32[5,32,128]{2,1,0:T(8,128)S(1)}, u32[]{:S(2)}, u32[]{:S(2)}) collective-permute-start(f32[5,32,128]{2,1,0:T(8,128)S(1)} %get-tuple-element.20), channel_id=1, source_target_pairs={{16,0},{32,16},{48,32},{64,48},{80,64},{96,80},{112,96},{0,112},{1... | collective-permute-start | bytes 245768 | tf_op jit(solution)/shard_map/ppermute | solution.py:392
  38.7 19.1 %collective-permute-start.5 = (f32[5,32,128]{2,1,0:T(8,128)S(1)}, f32[5,32,128]{2,1,0:T(8,128)S(1)}, u32[]{:S(2)}, u32[]{:S(2)}) collective-permute-start(f32[5,32,128]{2,1,0:T(8,128)S(1)} %get-tuple-element.21), channel_id=1, source_target_pairs={{0,16},{16,32},{32,48},{48,64},{64,80},{80,96},{96,112},{112,0},{1... | collective-permute-start | bytes 245768 | tf_op jit(solution)/shard_map/ppermute | solution.py:393
  68.5 12.8 %collective-permute-start.9 = (f32[64,256]{1,0:T(8,128)S(1)}, f32[64,256]{1,0:T(8,128)S(1)}, u32[]{:S(2)}, u32[]{:S(2)}) collective-permute-start(f32[64,256]{1,0:T(8,128)S(1)} %get-tuple-element.30), channel_id=1, source_target_pairs={{15,31},{31,15},{47,127},{63,111},{79,95},{95,79},{111,63},{127,47}} | collective-permute-start | bytes 196616 | tf_op jit(solution)/shard_map/ppermute | solution.py:365
  70.4 10.8 %collective-permute-start.8 = (f32[64,256]{1,0:T(8,128)S(1)}, f32[64,256]{1,0:T(8,128)S(1)}, u32[]{:S(2)}, u32[]{:S(2)}) collective-permute-start(f32[64,256]{1,0:T(8,128)S(1)} %get-tuple-element.30), channel_id=1, source_target_pairs={{15,111},{31,95},{47,79},{63,63},{79,47},{95,31},{111,15},{127,127}} | collective-permute-start | bytes 196616 | tf_op jit(solution)/shard_map/ppermute | solution.py:365
  77.1 4.1 %collective-permute-start.7 = (f32[64,256]{1,0:T(8,128)S(1)}, f32[64,256]{1,0:T(8,128)S(1)}, u32[]{:S(2)}, u32[]{:S(2)}) collective-permute-start(f32[64,256]{1,0:T(8,128)S(1)} %get-tuple-element.30), channel_id=1, source_target_pairs={{15,15},{31,127},{47,111},{63,95},{79,79},{95,63},{111,47},{127,31}} | collective-permute-start | bytes 196616 | tf_op jit(solution)/shard_map/ppermute | solution.py:365
  77.8 7.1 %collective-permute-start.6 = (f32[64,256]{1,0:T(8,128)S(1)}, f32[64,256]{1,0:T(8,128)S(1)}, u32[]{:S(2)}, u32[]{:S(2)}) collective-permute-start(f32[64,256]{1,0:T(8,128)S(1)} %get-tuple-element.30), channel_id=1, source_target_pairs={{15,127},{31,111},{47,95},{63,79},{79,63},{95,47},{111,31},{127,15}} | collective-permute-start | bytes 196616 | tf_op jit(solution)/shard_map/ppermute | solution.py:365
  84.9 1.4 %copy-start.3 = (f32[2,16,32,384]{3,2,1,0:T(8,128)S(1)}, f32[2,16,32,384]{3,2,1,0:T(8,128)}, u32[]{:S(2)}) copy-start(f32[2,16,32,384]{3,2,1,0:T(8,128)} %get-tuple-element.24.cells) | copy-start | bytes 4718596
  93.4 13.6 %collective-permute-start.13 = (f32[64,256]{1,0:T(8,128)S(1)}, f32[64,256]{1,0:T(8,128)S(1)}, u32[]{:S(2)}, u32[]{:S(2)}) collective-permute-start(f32[64,256]{1,0:T(8,128)S(1)} %get-tuple-element.32), channel_id=1, source_target_pairs={{15,31},{31,15},{47,127},{63,111},{79,95},{95,79},{111,63},{127,47}} | collective-permute-start | bytes 196616 | tf_op jit(solution)/shard_map/ppermute | solution.py:365
  95.3 11.7 %collective-permute-start.12 = (f32[64,256]{1,0:T(8,128)S(1)}, f32[64,256]{1,0:T(8,128)S(1)}, u32[]{:S(2)}, u32[]{:S(2)}) collective-permute-start(f32[64,256]{1,0:T(8,128)S(1)} %get-tuple-element.32), channel_id=1, source_target_pairs={{15,111},{31,95},{47,79},{63,63},{79,47},{95,31},{111,15},{127,127}} | collective-permute-start | bytes 196616 | tf_op jit(solution)/shard_map/ppermute | solution.py:365
  100.8 6.2 %collective-permute-start.11 = (f32[64,256]{1,0:T(8,128)S(1)}, f32[64,256]{1,0:T(8,128)S(1)}, u32[]{:S(2)}, u32[]{:S(2)}) collective-permute-start(f32[64,256]{1,0:T(8,128)S(1)} %get-tuple-element.32), channel_id=1, source_target_pairs={{15,15},{31,127},{47,111},{63,95},{79,79},{95,63},{111,47},{127,31}} | collective-permute-start | bytes 196616 | tf_op jit(solution)/shard_map/ppermute | solution.py:365
  101.5 7.2 %collective-permute-start.10 = (f32[64,256]{1,0:T(8,128)S(1)}, f32[64,256]{1,0:T(8,128)S(1)}, u32[]{:S(2)}, u32[]{:S(2)}) collective-permute-start(f32[64,256]{1,0:T(8,128)S(1)} %get-tuple-element.32), channel_id=1, source_target_pairs={{15,127},{31,111},{47,95},{63,79},{79,63},{95,47},{111,31},{127,15}} | collective-permute-start | bytes 196616 | tf_op jit(solution)/shard_map/ppermute | solution.py:365

commit v2 on v1

v2 whole, which is shorter than its diff:
```python
import functools

import jax
import jax.numpy as jnp
from jax import lax
from jax.experimental import pallas as pl
from jax.experimental.pallas import tpu as pltpu
from jax.sharding import PartitionSpec as P

H = 8
VMEM = pl.BlockSpec(memory_space=pltpu.VMEM)
SMEM = pl.BlockSpec(memory_space=pltpu.SMEM)
PARAMS = pltpu.CompilerParams(vmem_limit_bytes=20 * 2**20)
F32 = jnp.float32
LANE_GATHER = lax.GatherDimensionNumbers(
    offset_dims=(),
    collapsed_slice_dims=(1,),
    start_index_map=(1,),
    operand_batching_dims=(0,),
    start_indices_batching_dims=(0,),
)


def lane_gather(values, lanes):
    return lax.gather(
        values, lanes[..., None], LANE_GATHER, (1, 1), mode=lax.GatherScatterMode.PROMISE_IN_BOUNDS
    )


def pick_columns(partner, sources):
    lanes = jnp.bitwise_and(partner, 127)
    place = jnp.right_shift(partner, 7)
    result = jnp.zeros((8, 128), F32)
    for tile, rows in sources:
        for half in range(2):
            got = lane_gather(rows[:, 128 * half : 128 * half + 128], lanes)
            result = jnp.where(place == 2 * tile + half, got, result)
    return result


def iota(shape, axis):
    return lax.broadcasted_iota(jnp.int32, shape, axis)


def build_kernel(info, *refs):
    sources, (first, second, fold_rows, slots), held, done = refs[:7], refs[7:11], refs[11:18], refs[18]
    copies = [pltpu.make_async_copy(a, b, done.at[i]) for i, (a, b) in enumerate(zip(sources, held))]
    for copy in copies:
        copy.start()
    for copy in copies:
        copy.wait()
    tracers, east, north, levels, weights, indices, flux = held
    for tracer in range(2):
        for quarter in range(4):
            cut = flux[tracer : tracer + 1, 128 * quarter : 128 * quarter + 128]
            slots[:, 4 * tracer + quarter, :] = jnp.broadcast_to(cut, (128, 128))

    def write(out, rows):
        for tracer in range(2):
            out[16 * tracer : 16 * tracer + 16] = tracers[tracer, :, rows, :]
        out[32:48] = east[:, rows, :]
        out[48:64] = north[:, rows, :]
        out[64:68] = weights[:, rows, :]
        out[68:72] = indices[:, rows, :].astype(F32)
        out[72] = levels[rows, :].astype(F32)

    is_odd = info[6] == 1

    @pl.when(is_odd)
    def _():
        write(first, slice(0, 8))
        write(second, slice(8, 16))

    @pl.when(jnp.logical_not(is_odd))
    def _():
        write(first, slice(8, 16))
        write(second, slice(0, 8))

    for r in range(2):
        for tracer in range(2):
            at = 4 * r + 2 * tracer
            for part in range(2):
                fold_rows[at + part] = tracers[tracer, 8 * part : 8 * part + 8, 15 - r, :]
        wet = levels[15 - r : 16 - r, :] > 0
        for j in range(4):
            weight = weights[j, 15 - r : 16 - r, :]
            fold_rows[8 + r, j : j + 1, :] = jnp.where(wet, weight, jnp.zeros_like(weight))
            fold_rows[8 + r, 4 + j : 5 + j, :] = indices[j, 15 - r : 16 - r, :].astype(F32)

    @pl.when(info[1] == 1)
    def _():
        second[0:10] = fold_rows[...]


class Sides:
    def __init__(self, info, first, second):
        self.odd, self.top = info[6] == 1, info[1] == 1
        self.first, self.second = first, second

    def south(self, plane, cut=slice(None)):
        return jnp.where(self.odd, self.first[plane, :, cut], self.second[plane, :, cut])

    def north(self, plane, cut=slice(None)):
        got = jnp.where(self.odd, self.second[plane, :, cut], self.first[plane, :, cut])
        return jnp.where(self.top, 0.0, got)

    def whole(self, plane, centre, cut=slice(None)):
        return jnp.concatenate([self.south(plane, cut), centre, self.north(plane, cut)], axis=0)


def pack_kernel(info, tracers, east, north, levels, weights, indices, partner, first, second, fold_b, ghosts, to_west, to_east):
    is_top = info[1] == 1
    wanted = jnp.broadcast_to(partner[...], (8, 256))
    for block in range(10):
        rows = pl.ds(8 * block, 8)
        sources = [(info[2], second[block]), (info[3], fold_b[block])]
        for half in range(2):
            cut = slice(128 * half, 128 * half + 128)
            ghosts[rows, cut] = pick_columns(wanted[:, cut], sources)
    lane = iota((32, 128), 1)
    row = iota((32, 128), 0)
    ghost_first = jnp.logical_and(row == 24, is_top)
    ghost_second = jnp.logical_and(row == 25, is_top)
    last_north = jnp.logical_and(row == 23, is_top)
    beyond = jnp.logical_and(row >= 24, is_top)
    west_cut, east_cut = slice(0, 128), slice(128, 256)

    whole = Sides(info, first, second).whole

    def value(plane, cut):
        if plane < 32:
            got = whole(plane, tracers[plane // 16, plane % 16, :, cut], cut)
            got = jnp.where(ghost_first, ghosts[plane : plane + 1, cut], got)
            return jnp.where(ghost_second, ghosts[32 + plane : 33 + plane, cut], got)
        if plane < 48:
            return whole(plane, east[plane - 32, :, cut], cut)
        if plane < 64:
            return jnp.where(last_north, 0.0, whole(plane, north[plane - 48, :, cut], cut))
        if plane < 72:
            centre = weights[plane - 64, :, cut] if plane < 68 else indices[plane - 68, :, cut].astype(F32)
            got = jnp.where(ghost_first, ghosts[plane : plane + 1, cut], whole(plane, centre, cut))
            return jnp.where(ghost_second, ghosts[plane + 8 : plane + 9, cut], got)
        if plane == 72:
            return jnp.where(beyond, 16.0, whole(plane, levels[:, cut].astype(F32), cut))
        return jnp.broadcast_to(partner[:, cut].astype(F32), (32, 128))

    for group in range(5):
        westward = jnp.zeros((32, 128), F32)
        eastward = jnp.zeros((32, 128), F32)
        for slot in range(16 if group < 4 else 10):
            mine = jnp.logical_and(lane >= 8 * slot, lane < 8 * slot + 8)
            plane = 16 * group + slot
            near = value(plane, west_cut)
            far = value(plane, east_cut)
            westward = jnp.where(mine, pltpu.roll(near, 8 * slot, 1) if slot else near, westward)
            eastward = jnp.where(mine, pltpu.roll(far, (8 * slot + 8) % 128, 1) if slot != 15 else far, eastward)
        to_west[group] = westward
        to_east[group] = eastward


def one_hot_lookup(split_table, high, low, count):
    chosen = (iota((512, count), 0) == high).astype(F32).astype(jnp.bfloat16)
    got = jnp.dot(split_table[...], chosen, preferred_element_type=F32)
    lanes = iota((128, count), 0) == low
    first = jnp.sum(jnp.where(lanes, got[:128] + got[128:256], 0.0), axis=0, keepdims=True)
    second = jnp.sum(jnp.where(lanes, got[256:384] + got[384:], 0.0), axis=0, keepdims=True)
    return first, second


def split_place(index):
    high = jnp.bitwise_and(jnp.right_shift(index, 7), 3) * 128 + jnp.right_shift(index, 9)
    return high, jnp.bitwise_and(index, 127)


def split_kernel_table(table, split_table):
    for tracer in range(2):
        for quarter in range(4):
            block = table[:, tracer * 4 + quarter, :].T
            top = block.astype(jnp.bfloat16)
            rest = (block - top.astype(F32)).astype(jnp.bfloat16)
            cut = slice(128 * quarter, 128 * quarter + 128)
            split_table[tracer * 256 : tracer * 256 + 128, cut] = top
            split_table[tracer * 256 + 128 : tracer * 256 + 256, cut] = rest


def halo_tile(from_east, from_west, lane, group, slot):
    shift = (lambda v: v % 128) if isinstance(slot, int) else (lambda v: lax.rem(v, 128))
    near = pltpu.roll(from_east[group], shift(128 - 8 * slot), 1)
    far = pltpu.roll(from_west[group], shift(248 - 8 * slot), 1)
    return jnp.where(lane < 8, near, jnp.where(lane >= 120, far, 0.0))


def lookup_kernel(groups, splits, last, info, table, weights, indices, first, second, ghosts, *rest):
    if last:
        from_east, from_west, surface, halo_surface, high, low, weight = rest
    elif splits:
        surface, split_table, high, low, weight = rest
    else:
        surface, high, low, weight = rest
    if splits:
        split_kernel_table(table, split_table)
    else:
        split_table = table
    is_top = info[1] == 1
    whole = Sides(info, first, second).whole
    row = iota((32, 256), 0)
    for j in range(4):
        index = whole(68 + j, indices[j].astype(F32))
        scale = whole(64 + j, weights[j])
        for r in range(2):
            ghost = jnp.logical_and(row == 24 + r, is_top)
            scale = jnp.where(ghost, ghosts[64 + 8 * r + j : 65 + 8 * r + j, :], scale)
            index = jnp.where(ghost, ghosts[68 + 8 * r + j : 69 + 8 * r + j, :], index)
        high[j], low[j] = split_place(index.astype(jnp.int32))
        weight[j] = scale
    surface[...] = jnp.zeros(surface.shape, F32)
    start = 4 * groups[0]

    def body(step, carry):
        group, j = step // 4, step % 4
        rows = [4 * group + i for i in range(4)]
        join = lambda ref: jnp.concatenate([ref[j, pl.ds(start + r, 1), :] for r in rows], axis=1)
        pair = one_hot_lookup(split_table, join(high), join(low), 1024)
        for i, r in enumerate(rows):
            scale = weight[j, pl.ds(start + r, 1), :]
            for tracer in range(2):
                surface[tracer, pl.ds(r, 1), :] += scale * pair[tracer][:, 256 * i : 256 * i + 256]
        return carry

    lax.fori_loop(0, 4 * len(groups), body, 0, unroll=2)
    if last:
        lane = iota((32, 128), 1)
        small_lane, small_row = iota((16, 128), 1), iota((16, 128), 0)
        places, scales = [], []
        for j in range(4):
            index = halo_tile(from_east, from_west, lane, 4, 4 + j)
            scale = halo_tile(from_east, from_west, lane, 4, j)
            for part in range(2):
                cut = slice(16 * part, 16 * part + 16)
                places.append(spread_rows(index[cut], small_row, small_lane).astype(jnp.int32))
                scales.append(spread_rows(scale[cut], small_row, small_lane))
        halo_high, halo_low = split_place(jnp.concatenate(places, axis=1))
        pair = one_hot_lookup(split_table, halo_high, halo_low, 1024)
        for tracer in range(2):
            for part in range(2):
                total = jnp.zeros((1, 128), F32)
                for j in range(4):
                    at = 2 * j + part
                    total += scales[at] * pair[tracer][:, 128 * at : 128 * at + 128]
                halo_surface[tracer, 16 * part : 16 * part + 16, :] = gather_rows(total, small_row, small_lane)


def spread_rows(halo, row_of, lane):
    moved = jnp.where(lane < 8, pltpu.roll(halo, 4, 1), jnp.zeros_like(halo))
    for shift in (8, 16, 32, 64):
        moved = moved + pltpu.roll(moved, shift, 1)
    return jnp.sum(jnp.where(lane // 8 == row_of, moved, jnp.zeros_like(moved)), axis=0, keepdims=True)


def gather_rows(packed, row_of, lane):
    moved = jnp.where(lane // 8 == row_of, jnp.broadcast_to(packed, (16, 128)), 0.0)
    for shift in (8, 16, 32, 64):
        moved = moved + pltpu.roll(moved, shift, 1)
    return pltpu.roll(moved, 124, 1)


def east_of(f):
    return pltpu.roll(f, f.shape[1] - 1, 1)


def west_of(f):
    return pltpu.roll(f, 1, 1)


def north_of(f):
    return pltpu.roll(f, f.shape[0] - 1, 0)


def south_of(f):
    return pltpu.roll(f, 1, 0)


def run_levels(cells, half_east, half_north, depth, surface, store, window=slice(0, 32), keep=slice(0, 32), tracers=(0, 1)):
    depth = depth[window, :]
    east_depth = jnp.minimum(depth, east_of(depth))
    north_depth = jnp.minimum(depth, north_of(depth))
    kept = slice(window.start + keep.start, window.start + keep.stop)

    def body(k, carry):
        level = k.astype(F32)
        east_open, north_open, wet = level < east_depth, level < north_depth, level < depth[keep]
        deeper = level + 1.0 < depth[keep]
        east, north = half_east[k, window, :], half_north[k, window, :]
        above, under = jnp.minimum(k + 1, 15), jnp.maximum(k - 1, 0)
        at_surface = jnp.where(k == 0, 0.5, 0.0).astype(F32)
        for tracer in tracers:
            here = cells[tracer, k]
            to_east, to_north = east_of(here), north_of(here)
            grad_east = jnp.where(east_open, to_east - here, 0.0)
            grad_north = jnp.where(north_open, to_north - here, 0.0)
            lap = grad_east - west_of(grad_east) + (grad_north - south_of(grad_north))
            flat = 0.08 * here - 0.01 * lap
            flux_east = jnp.where(east_open, east_of(flat) - flat - east * (to_east + here), 0.0)
            flux_north = jnp.where(north_open, north_of(flat) - flat - north * (to_north + here), 0.0)
            total = (flux_east - west_of(flux_east) + (flux_north - south_of(flux_north)))[keep]
            centre = here[keep]
            vertical = jnp.where(deeper, cells[tracer, above, keep, :] - centre, 0.0)
            total += 0.1 * (vertical - (centre - cells[tracer, under, keep, :]))
            if surface is not None:
                total += at_surface * surface[tracer, kept, :]
            store(tracer, k, centre + jnp.where(wet, total, 0.0))
        return carry

    lax.fori_loop(0, 16, body, 0)


def keep_step(cells_out, fold_out):
    def store(tracer, k, fresh):
        cells_out[tracer, k] = fresh
        for r in range(2):
            fold_out[pl.ds(32 * r + 16 * tracer + k, 1), :] = fresh[23 - r : 24 - r, 0:256]

    return store


def place_ghosts(cells, ghosts, columns, row=24):
    def place(k, carry):
        for tracer in range(2):
            for r in range(2):
                cells[tracer, k, row + r : row + r + 1, 0:columns] = ghosts[pl.ds(32 * r + 16 * tracer + k, 1), :]
        return carry

    lax.fori_loop(0, 16, place, 0)


def first_kernel(
    info, tracers, east, north, levels, partner, first, second, ghosts, from_east, from_west,
    cells_out, fold_out, east_ext, north_ext, depth_ext, partner_ext, start,
):
    is_top = info[1] == 1
    lane = iota((32, 128), 1)
    row = iota((32, 256), 0)
    last_north = jnp.logical_and(row == 23, is_top)
    halo = functools.partial(halo_tile, from_east, from_west, lane)

    whole = Sides(info, first, second).whole

    def fill(k, carry):
        for tracer in range(2):
            start[tracer, k, :, 0:256] = whole(tracer * 16 + k, tracers[tracer, k])
            start[tracer, k, :, 256:384] = halo(tracer, k)
        east_ext[k, :, 0:256] = 0.5 * whole(32 + k, east[k])
        east_ext[k, :, 256:384] = 0.5 * halo(2, k)
        north_ext[k, :, 0:256] = jnp.where(last_north, 0.0, 0.5 * whole(48 + k, north[k]))
        north_ext[k, :, 256:384] = 0.5 * halo(3, k)
        return carry

    lax.fori_loop(0, 16, fill, 0)

    @pl.when(is_top)
    def _():
        place_ghosts(start, ghosts, 256)

    depth_ext[:, 0:256] = jnp.where(
        jnp.logical_and(row >= 24, is_top), 16.0, whole(72, levels[...].astype(F32))
    )
    depth_ext[:, 256:384] = halo(4, 8)
    partner_ext[:, 0:256] = jnp.broadcast_to(partner[...], (8, 256))
    partner_ext[:, 256:384] = halo(4, 9)[0:8].astype(jnp.int32)
    run_levels(start, east_ext, north_ext, depth_ext, None, keep_step(cells_out, fold_out))


def fold_ghosts(info, partner_ext, received, ghosts):
    def block_body(block, carry):
        rows = pl.ds(pl.multiple_of(8 * block, 8), 8)
        all_sources = [(info[2 + i], ref[rows, :]) for i, ref in enumerate(received)]
        for part, sources in enumerate((all_sources[:2], all_sources[:2], all_sources)):
            cut = slice(128 * part, 128 * part + 128)
            ghosts[rows, cut] = pick_columns(partner_ext[:, cut], sources)
        return carry

    lax.fori_loop(0, 8, block_body, 0)


def second_kernel(
    info, cells, east_ext, north_ext, depth_ext, partner_ext, fold_a, fold_b, fold_c, fold_d, surface_a, surface_b, surface_c, surface_d,
    surface_e, halo_surface, cells_out, fold_out, surface_ext, ghosts, start,
):
    def fill(k, carry):
        for tracer in range(2):
            start[tracer, k] = cells[tracer, k]
        return carry

    lax.fori_loop(0, 16, fill, 0)

    @pl.when(info[1] == 1)
    def _():
        fold_ghosts(info, partner_ext, (fold_a, fold_b, fold_c, fold_d), ghosts)
        place_ghosts(start, ghosts, 384)

    surface_ext[...] = jnp.zeros((2, 32, 384), F32)
    for tracer in range(2):
        at = 4
        for piece in (surface_a, surface_b, surface_c, surface_d, surface_e):
            surface_ext[tracer, at : at + piece.shape[1], 0:256] = piece[tracer]
            at += piece.shape[1]
        surface_ext[tracer, :, 256:384] = halo_surface[tracer]
        start[tracer, 0] = start[tracer, 0] + jnp.where(depth_ext[...] > 0.0, 0.5 * surface_ext[tracer], 0.0)
    run_levels(start, east_ext, north_ext, depth_ext, surface_ext, keep_step(cells_out, fold_out))


def last_kernel(
    info, cells, east_ext, north_ext, depth_ext, partner_ext, fold_a, fold_b, fold_c, fold_d, surface_ext, result, ghosts, start
):
    def fill(k, carry):
        for tracer in range(2):
            start[tracer, k] = cells[tracer, k]
        return carry

    lax.fori_loop(0, 16, fill, 0)

    @pl.when(info[1] == 1)
    def _():
        fold_ghosts(info, partner_ext, (fold_a, fold_b, fold_c, fold_d), ghosts)
        place_ghosts(start, ghosts, 384)

    def store(tracer, k, fresh):
        result[tracer, k] = fresh[:, 0:256]

    run_levels(start, east_ext, north_ext, depth_ext, surface_ext, store, keep=slice(8, 24))


def call(kernel, ins, outs, scratch=(), cost=None, earlier=(), ins_any=False, outs_any=False, alias=None, params=PARAMS):
    used = len(ins)

    def body(*refs):
        kernel(*refs[:used], *refs[used + len(earlier) :])

    anywhere = pl.BlockSpec(memory_space=pl.ANY)
    hbm = pl.BlockSpec(memory_space=pltpu.HBM)

    def place(i, v):
        if v.ndim == 1:
            return SMEM
        return hbm if ins_any or i == alias else anywhere if i >= used else VMEM

    arrays = tuple(ins) + tuple(earlier)
    return pl.pallas_call(
        body,
        out_shape=tuple(jax.ShapeDtypeStruct(s, d) for s, d in outs),
        in_specs=[place(i, v) for i, v in enumerate(arrays)],
        out_specs=tuple(hbm if outs_any else VMEM for _ in outs),
        scratch_shapes=list(scratch),
        compiler_params=params,
        cost_estimate=cost,
        input_output_aliases={} if alias is None else {alias: 0},
    )(*arrays)


STEP_COST = pl.CostEstimate(flops=10**7, bytes_accessed=16 * 2**20, transcendentals=0)


def lookup_cost(groups):
    return pl.CostEstimate(flops=groups * 2 * 512 * 512 * 4096, bytes_accessed=groups * 2**20, transcendentals=0)


def per_device(tracers, east, north, levels, partner, atm_flux, indices, weights):
    nlon, nlat = lax.axis_size("lon"), lax.axis_size("lat")
    both = ("lon", "lat")
    t, lat = lax.axis_index("lon"), lax.axis_index("lat")
    is_top = (lat == nlat - 1).astype(jnp.int32)
    tiles = [jnp.remainder(nlon - 1 - t + d, nlon) for d in (0, 1, -1, 2)]
    info = jnp.stack([t, is_top] + tiles + [lat % 2]).astype(jnp.int32)
    top = nlat - 1

    def fold_permute(rows, d):
        pairs = [(i * nlat + top, ((nlon - 1 + d - i) % nlon) * nlat + top) for i in range(nlon)]
        return lax.ppermute(rows, both, pairs)

    message = ((73, H, 256), F32)
    whole_inputs = (tracers, east, north, levels, weights, indices)
    build_inputs = (*whole_inputs, atm_flux)
    first, second, fold_rows, slots = call(
        build_kernel,
        (info, *build_inputs),
        [message, message, ((10, 8, 256), F32), ((nlon * nlat, 8, 128), F32)],
        [pltpu.VMEM(a.shape, a.dtype) for a in build_inputs] + [pltpu.SemaphoreType.DMA((7,))],
        ins_any=True,
        params=pltpu.CompilerParams(vmem_limit_bytes=60 * 2**20),
    )
    def after(value, *earlier):
        return lax.optimization_barrier((value, *earlier))[0]

    swaps = [(i, i + 1) for i in range(0, nlat, 2)]
    first = lax.ppermute(first, "lat", swaps + [(j, i) for i, j in swaps])
    swaps = [(i, i + 1) for i in range(1, nlat - 1, 2)]
    swaps = [(c * nlat + i, c * nlat + j) for c in range(nlon) for i, j in swaps + [(j, i) for i, j in swaps]]
    facing = [(c * nlat + top, (nlon - 1 - c) * nlat + top) for c in range(nlon)]
    second = lax.ppermute(second, both, swaps + facing)
    fold_b = fold_permute(fold_rows, 1)

    table = lax.all_to_all(slots, both, 0, 0, tiled=True)

    partner_row = partner.reshape(1, -1)
    ghosts, to_west, to_east = call(
        pack_kernel,
        (info, *whole_inputs, partner_row, first, second, fold_b),
        [((80, 256), F32), ((5, 32, 128), F32), ((5, 32, 128), F32)],
    )
    from_east = lax.ppermute(to_west, "lon", [((i + 1) % nlon, i) for i in range(nlon)])
    from_west = lax.ppermute(to_east, "lon", [(i, (i + 1) % nlon) for i in range(nlon)])

    def lookups(groups, table, splits=False, last=False, earlier=()):
        outs = [((2, 4 * len(groups), 256), F32)]
        outs += [((512, 512), jnp.bfloat16)] if splits else [((2, 32, 128), F32)] if last else []
        words = pltpu.VMEM((4, 32, 256), jnp.int32)
        return call(
            functools.partial(lookup_kernel, groups, splits, last),
            (info, table, weights, indices, first, second, ghosts) + ((from_east, from_west) if last else ()),
            outs,
            [words, words, pltpu.VMEM((4, 32, 256), F32)],
            lookup_cost(len(groups)),
            earlier,
        )

    surface_a, split_table = lookups((1, 2), table, splits=True)

    wide = (2, 16, 32, 384)
    cells, fold_rows, east_ext, north_ext, depth_ext, partner_ext = call(
        first_kernel,
        (info, tracers, east, north, levels, partner_row, first, second, ghosts, from_east, from_west),
        [(wide, F32), ((64, 256), F32), (wide[1:], F32), (wide[1:], F32), ((32, 384), F32), ((8, 384), jnp.int32)],
        [pltpu.VMEM(wide, F32)],
        STEP_COST,
        (surface_a,),
    )
    statics = (east_ext, north_ext, depth_ext)
    received = [fold_permute(fold_rows, 0)]
    (surface_b,) = lookups((3,), split_table, earlier=(fold_rows,))
    received.append(fold_permute(after(fold_rows, surface_b), 1))
    (surface_c,) = lookups((4,), split_table, earlier=(received[0], surface_b))
    received.append(fold_permute(after(fold_rows, surface_c), -1))
    (surface_d,) = lookups((5,), split_table, earlier=(received[1], surface_c))
    received.append(fold_permute(after(fold_rows, surface_d), 2))
    surface_e, halo_surface = lookups((6,), split_table, last=True, earlier=(received[2], surface_d))

    ghost_rows = pltpu.VMEM((64, 384), F32)
    cells, fold_rows, surface_ext = call(
        second_kernel,
        (info, cells, *statics, partner_ext, *received, surface_a, surface_b, surface_c, surface_d, surface_e,
         halo_surface),
        [(wide, F32), ((64, 256), F32), ((2, 32, 384), F32)],
        [ghost_rows, pltpu.VMEM(wide, F32)],
        STEP_COST,
    )
    received = [fold_permute(fold_rows, d) for d in (0, 1, -1, 2)]
    (result,) = call(
        last_kernel,
        (info, cells, *statics, partner_ext, *received, surface_ext),
        [(tracers.shape, F32)],
        [ghost_rows, pltpu.VMEM(wide, F32)],
        STEP_COST,
    )
    return result


def solution(mesh):
    return jax.shard_map(
        per_device,
        mesh=mesh,
        in_specs=(
            P(None, None, "lat", "lon"),
            P(None, "lat", "lon"),
            P(None, "lat", "lon"),
            P("lat", "lon"),
            P("lon"),
            P(None, ("lon", "lat")),
            P(None, "lat", "lon"),
            P(None, "lat", "lon"),
        ),
        out_specs=P(None, None, "lat", "lon"),
        check_vma=False,
    )
```

time: 118 us -> 110 us (0.932); the launches traced: 116 us -> 110 us
  starting transfers between devices: 55.6 us -> 47.3 us
  local copies, waits for them, and re-layouts: 6.45 us -> 0.67 us
  waiting for transfers between devices: 6.78 us -> 11.5 us
  Pallas kernels: 45.4 us -> 49.7 us
  other arithmetic: 1.26 us -> 0 us
    ppermute x12 -> x11, starting transfers between devices: 38.5 us -> 32.4 us  [the longest x9 27.4 us: fold_permute(): return lax.ppermute(rows, both, pairs)]
    all_to_all x1, starting transfers between devices: 13.5 us -> 8.13 us  [per_device(): table = lax.all_to_all(slots, both, 0, 0, tiled=True)]
    unnamed x24 -> x16, local copies, waits for them, and re-layouts: 4.35 us -> 0.04 us
    pallas_call x5 -> x10, Pallas kernels: 45.4 us -> 49.7 us  [call(): pl.pallas_call(body, out_shape=tuple((jax.ShapeDtypeStruct(s, d) for s, d...]
    ppermute x12 -> x11, waiting for transfers between devices: 6.78 us -> 10.4 us  [the longest x1 5.24 us: per_device(): second = lax.ppermute(second, both, swaps + facing)]
    ppermute x1, starting transfers between devices: 3.63 us -> 6.76 us  [per_device(): lax.ppermute(to_west, 'lon', [((i + 1) % nlon, i) for i in range(nlon)])]
  transfers between devices with their start and end apart: 15 -> 14, of which waited for: 3 -> 3; matrix products, arithmetic and copies ran while one was open for 1% -> 0% of each run, Pallas kernels for 18% -> 21%
where the time goes in v2:
time: 110 us
  Pallas kernels  49.7 us (45%)
  starting transfers between devices  47.3 us (43%)
  waiting for transfers between devices  11.5 us (10%)
    pallas_call x10, Pallas kernels, call(): pl.pallas_call(body, out_shape=tuple((jax.ShapeDtypeStruct(s, d) for s, d...  49.7 us
    ppermute x9, starting transfers between devices, fold_permute(): return lax.ppermute(rows, both, pairs)  27.4 us
    all_to_all x1, starting transfers between devices, per_device(): table = lax.all_to_all(slots, both, 0, 0, tiled=True)  8.13 us
    ppermute x1, starting transfers between devices, per_device(): lax.ppermute(to_west, 'lon', [((i + 1) % nlon, i) for i in range(nlon)])  6.76 us
    ppermute x1, waiting for transfers between devices, per_device(): second = lax.ppermute(second, both, swaps + facing)  5.24 us
    ppermute x9, waiting for transfers between devices, fold_permute(): return lax.ppermute(rows, both, pairs)  5.18 us
    ppermute x1, starting transfers between devices, per_device(): second = lax.ppermute(second, both, swaps + facing)  4.21 us
  transfers between devices with their start and end apart: 14, of which 3 were waited for; matrix products, arithmetic and copies ran while one was open for 0% of the time, Pallas kernels for 21%

profile of v2, /device:TPU:121, one launch (start us, length us, event | category | flops | bytes accessed | tf_op | source)
XLA Modules:
  0.0 109.6 jit_solution(7237052168332006856)
XLA Ops:
  0.0 0.0 copy-start.3
  0.0 0.0 copy-start
  0.0 0.0 copy-start.1
  0.0 0.0 copy-start.7
  0.1 0.6 stack.35.refs_0_
  0.7 3.6 %shard_map.82 = (f32[73,8,256]{2,1,0:T(8,128)}, f32[73,8,256]{2,1,0:T(8,128)}, f32[10,8,256]{2,1,0:T(8,128)}, f32[128,8,128]{2,1,0:T(8,128)}) custom-call(s32[7]{0:T(128)} %stack.35.refs_0_, f32[2,16,16,256]{3,2,1,0:T(8,128)} %refs_1_.5, f32[16,16,256]{2,1,0:T(8,128)} %refs_2_.11, f32[16,16,256]{2,1,0:T(8,128)} %refs_3_.11, s32[16,256]{1,0:T(8,128)} %refs_4_.5, ...), custom_call_target="tpu_custom_call" | custom-call | tf_op jit(solution)/shard_map/pallas_call | solution.py:448
  4.4 0.7 collective-permute-start
  5.1 4.2 %collective-permute-start.1 = (f32[73,8,256]{2,1,0:T(8,128)}, f32[73,8,256]{2,1,0:T(8,128)S(1)}, u32[]{:S(2)}, u32[]{:S(2)}) collective-permute-start(f32[73,8,256]{2,1,0:T(8,128)} %get-tuple-element.29), channel_id=1, source_target_pairs={{1,2},{3,4},{5,6},{7,8},{9,10},{11,12},{13,14},{2,1},{4,3},{6,5},{... | collective-permute-start | bytes 1794056 | tf_op jit(solution)/shard_map/ppermute | solution.py:499
  9.3 8.1 %all-to-all-start = ((f32[128,8,128]{2,1,0:T(8,128)}), f32[128,8,128]{2,1,0:T(8,128)S(1)}, u32[]{:S(2)}, u32[]{:S(2)}) async-start(f32[128,8,128]{2,1,0:T(8,128)} %get-tuple-element.34), calls=%async_computation | async-start | bytes 1048576 | tf_op jit(solution)/shard_map/all_to_all | solution.py:502
  17.5 1.5 %collective-permute-start.2 = (f32[10,8,256]{2,1,0:T(8,128)}, f32[10,8,256]{2,1,0:T(8,128)S(1)}, u32[]{:S(2)}, u32[]{:S(2)}) collective-permute-start(f32[10,8,256]{2,1,0:T(8,128)} %get-tuple-element.30), channel_id=1, source_target_pairs={{15,15},{31,127},{47,111},{63,95},{79,79},{95,63},{111,47},{127,31}} | collective-permute-start | bytes 245768 | tf_op jit(solution)/shard_map/ppermute | solution.py:478
  19.0 0.0 collective-permute-done.2.refs_10_
  19.0 0.0 collective-permute-done.refs_8_.refs_4_.refs_6_
  19.0 5.2 %collective-permute-done.1.refs_9_.refs_5_.refs_7_ = f32[73,8,256]{2,1,0:T(8,128)S(1)} collective-permute-done((f32[73,8,256]{2,1,0:T(8,128)}, f32[73,8,256]{2,1,0:T(8,128)S(1)}, u32[]{:S(2)}, u32[]{:S(2)}) %collective-permute-start.1) | collective-permute-done | bytes 598048 | tf_op jit(solution)/shard_map/ppermute | solution.py:499
  24.3 0.0 copy-done.2
  24.3 0.0 copy-done.5
  24.3 0.0 copy-done.4
  24.3 0.0 copy-done.3
  24.3 0.0 copy-done
  24.3 1.4 %shard_map.83 = (f32[80,256]{1,0:T(8,128)S(1)}, f32[5,32,128]{2,1,0:T(8,128)S(1)}, f32[5,32,128]{2,1,0:T(8,128)S(1)}) custom-call(s32[7]{0:T(128)S(1)} %copy-done.6, f32[2,16,16,256]{3,2,1,0:T(8,128)S(1)} %copy-done, f32[16,16,256]{2,1,0:T(8,128)S(1)} %copy-done.1, f32[16,16,256]{2,1,0:T(8,128)S(1)} %copy-done.2, s32[16,256]{1,0:T(8,128)S(1)} %copy-done.5, ...), custom_call_target="tpu_custom_call" | custom-call | tf_op jit(solution)/shard_map/pallas_call | solution.py:448
  25.7 6.8 %collective-permute-start.3 = (f32[5,32,128]{2,1,0:T(8,128)S(1)}, f32[5,32,128]{2,1,0:T(8,128)S(1)}, u32[]{:S(2)}, u32[]{:S(2)}) collective-permute-start(f32[5,32,128]{2,1,0:T(8,128)S(1)} %get-tuple-element.32), channel_id=1, source_target_pairs={{16,0},{32,16},{48,32},{64,48},{80,64},{96,80},{112,96},{0,112},{1... | collective-permute-start | bytes 245768 | tf_op jit(solution)/shard_map/ppermute | solution.py:510
  32.4 0.0 collective-permute-start.4
  32.4 1.1 %all-to-all-done.refs_1_ = f32[128,8,128]{2,1,0:T(8,128)S(1)} async-done(((f32[128,8,128]{2,1,0:T(8,128)}), f32[128,8,128]{2,1,0:T(8,128)S(1)}, u32[]{:S(2)}, u32[]{:S(2)}) %all-to-all-start) | async-done | bytes 524320 | tf_op jit(solution)/shard_map/all_to_all | solution.py:502
  33.5 6.6 %shard_map.84 = (f32[2,8,256]{2,1,0:T(8,128)S(1)}, bf16[512,512]{1,0:T(8,128)(2,1)S(1)}) custom-call(s32[7]{0:T(128)S(1)} %copy-done.6, f32[128,8,128]{2,1,0:T(8,128)S(1)} %all-to-all-done.refs_1_, f32[4,16,256]{2,1,0:T(8,128)S(1)} %copy-done.3, s32[4,16,256]{2,1,0:T(8,128)S(1)} %copy-done.4, f32[73,8,256]{2,1,0:T(8,128)S(1)} %collective-permute-done.refs_8_.refs_4_.refs_6_, ...), custom_call_target="tpu_custom_call" | custom-call | flops 4294967296 | bytes 2097152 | tf_op jit(solution)/shard_map/pallas_call | solution.py:448
  40.2 0.0 collective-permute-done.3.refs_9_.refs_7_
  40.2 0.0 collective-permute-done.4.refs_10_.refs_8_
  40.2 7.9 %shard_map.85 = (f32[2,16,32,384]{3,2,1,0:T(8,128)S(1)}, f32[64,256]{1,0:T(8,128)S(1)}, f32[16,32,384]{2,1,0:T(8,128)S(1)}, f32[16,32,384]{2,1,0:T(8,128)S(1)}, ...) custom-call(s32[7]{0:T(128)S(1)} %copy-done.6, f32[2,16,16,256]{3,2,1,0:T(8,128)S(1)} %copy-done, ...), custom_call_target="tpu_custom_call" | custom-call | flops 10000000 | bytes 16777216 | tf_op jit(solution)/shard_map/pallas_call | solution.py:448
  48.1 7.9 %collective-permute-start.5 = (f32[64,256]{1,0:T(8,128)S(1)}, f32[64,256]{1,0:T(8,128)S(1)}, u32[]{:S(2)}, u32[]{:S(2)}) collective-permute-start(f32[64,256]{1,0:T(8,128)S(1)} %get-tuple-element.45.refs_7_), channel_id=1, source_target_pairs={{15,127},{31,111},{47,95},{63,79},{79,63},{95,47},{111,31},{127,15}} | collective-permute-start | bytes 196616 | tf_op jit(solution)/shard_map/ppermute | solution.py:478
  56.0 3.4 %shard_map.86.refs_8_.refs_11_ = f32[2,4,256]{2,1,0:T(4,128)S(1)} custom-call(s32[7]{0:T(128)S(1)} %copy-done.6, bf16[512,512]{1,0:T(8,128)(2,1)S(1)} %get-tuple-element.42.refs_1_, f32[4,16,256]{2,1,0:T(8,128)S(1)} %copy-done.3, s32[4,16,256]{2,1,0:T(8,128)S(1)} %copy-done.4, f32[73,8,256]{2,1,0:T(8,128)S(1)} %collective-permute-done.refs_8_.refs_4_.refs_6_, ...), custom_call_target="tpu_custom_call" | custom-call | flops 2147483648 | bytes 1048576 | tf_op jit(solution)/shard_map/pallas_call | solution.py:448
  59.5 0.7 collective-permute-start.6
  60.1 0.0 collective-permute-done.5.refs_7_.refs_6_
  60.1 3.5 %shard_map.87.refs_8_.refs_12_ = f32[2,4,256]{2,1,0:T(4,128)S(1)} custom-call(s32[7]{0:T(128)S(1)} %copy-done.6, bf16[512,512]{1,0:T(8,128)(2,1)S(1)} %get-tuple-element.42.refs_1_, f32[4,16,256]{2,1,0:T(8,128)S(1)} %copy-done.3, s32[4,16,256]{2,1,0:T(8,128)S(1)} %copy-done.4, f32[73,8,256]{2,1,0:T(8,128)S(1)} %collective-permute-done.refs_8_.refs_4_.refs_6_, ...), custom_call_target="tpu_custom_call" | custom-call | flops 2147483648 | bytes 1048576 | tf_op jit(solution)/shard_map/pallas_call | solution.py:448
  63.6 4.0 %collective-permute-start.7 = (f32[64,256]{1,0:T(8,128)S(1)}, f32[64,256]{1,0:T(8,128)S(1)}, u32[]{:S(2)}, u32[]{:S(2)}) collective-permute-start(f32[64,256]{1,0:T(8,128)S(1)} %get-tuple-element.45.refs_7_), channel_id=1, source_target_pairs={{15,111},{31,95},{47,79},{63,63},{79,47},{95,31},{111,15},{127,127}} | collective-permute-start | bytes 196616 | tf_op jit(solution)/shard_map/ppermute | solution.py:478
  67.6 0.0 collective-permute-done.6.refs_7_
  67.6 3.4 %shard_map.88.refs_10_.refs_13_ = f32[2,4,256]{2,1,0:T(4,128)S(1)} custom-call(s32[7]{0:T(128)S(1)} %copy-done.6, bf16[512,512]{1,0:T(8,128)(2,1)S(1)} %get-tuple-element.42.refs_1_, f32[4,16,256]{2,1,0:T(8,128)S(1)} %copy-done.3, s32[4,16,256]{2,1,0:T(8,128)S(1)} %copy-done.4, f32[73,8,256]{2,1,0:T(8,128)S(1)} %collective-permute-done.refs_8_.refs_4_.refs_6_, ...), custom_call_target="tpu_custom_call" | custom-call | flops 2147483648 | bytes 1048576 | tf_op jit(solution)/shard_map/pallas_call | solution.py:448
  71.0 1.9 %collective-permute-start.8 = (f32[64,256]{1,0:T(8,128)S(1)}, f32[64,256]{1,0:T(8,128)S(1)}, u32[]{:S(2)}, u32[]{:S(2)}) collective-permute-start(f32[64,256]{1,0:T(8,128)S(1)} %get-tuple-element.45.refs_7_), channel_id=1, source_target_pairs={{15,31},{31,15},{47,127},{63,111},{79,95},{95,79},{111,63},{127,47}} | collective-permute-start | bytes 196616 | tf_op jit(solution)/shard_map/ppermute | solution.py:478
  73.0 0.0 collective-permute-done.7.refs_9_.refs_8_
  73.0 5.1 %shard_map.89 = (f32[2,4,256]{2,1,0:T(4,128)S(1)}, f32[2,32,128]{2,1,0:T(8,128)S(1)}) custom-call(s32[7]{0:T(128)S(1)} %copy-done.6, bf16[512,512]{1,0:T(8,128)(2,1)S(1)} %get-tuple-element.42.refs_1_, f32[4,16,256]{2,1,0:T(8,128)S(1)} %copy-done.3, s32[4,16,256]{2,1,0:T(8,128)S(1)} %copy-done.4, ...), custom_call_target="tpu_custom_call" | custom-call | flops 2147483648 | bytes 1048576 | tf_op jit(solution)/shard_map/pallas_call | solution.py:448
  78.1 0.0 collective-permute-done.8.refs_9_
  78.1 7.3 %shard_map.90 = (f32[2,16,32,384]{3,2,1,0:T(8,128)S(1)}, f32[64,256]{1,0:T(8,128)S(1)}, f32[2,32,384]{2,1,0:T(8,128)S(1)}) custom-call(s32[7]{0:T(128)S(1)} %copy-done.6, f32[2,16,32,384]{3,2,1,0:T(8,128)S(1)} %get-tuple-element.36.refs_1_, f32[16,32,384]{2,1,0:T(8,128)S(1)} %get-tuple-element.37.refs_2_, f32[16,32,384]{2,1,0:T(8,128)S(1)} %get-tuple-element.38.refs_3_, ...), custom_call_target="tpu_custom_call" | custom-call | flops 10000000 | bytes 16777216 | tf_op jit(solution)/shard_map/pallas_call | solution.py:448
  85.4 0.7 collective-permute-start.10
  86.0 5.8 %collective-permute-start.11 = (f32[64,256]{1,0:T(8,128)S(1)}, f32[64,256]{1,0:T(8,128)S(1)}, u32[]{:S(2)}, u32[]{:S(2)}) collective-permute-start(f32[64,256]{1,0:T(8,128)S(1)} %get-tuple-element.49), channel_id=1, source_target_pairs={{15,111},{31,95},{47,79},{63,63},{79,47},{95,31},{111,15},{127,127}} | collective-permute-start | bytes 196616 | tf_op jit(solution)/shard_map/ppermute | solution.py:478
  91.8 3.1 %collective-permute-start.12 = (f32[64,256]{1,0:T(8,128)S(1)}, f32[64,256]{1,0:T(8,128)S(1)}, u32[]{:S(2)}, u32[]{:S(2)}) collective-permute-start(f32[64,256]{1,0:T(8,128)S(1)} %get-tuple-element.49), channel_id=1, source_target_pairs={{15,31},{31,15},{47,127},{63,111},{79,95},{95,79},{111,63},{127,47}} | collective-permute-start | bytes 196616 | tf_op jit(solution)/shard_map/ppermute | solution.py:478
  94.9 1.9 %collective-permute-start.9 = (f32[64,256]{1,0:T(8,128)S(1)}, f32[64,256]{1,0:T(8,128)S(1)}, u32[]{:S(2)}, u32[]{:S(2)}) collective-permute-start(f32[64,256]{1,0:T(8,128)S(1)} %get-tuple-element.49), channel_id=1, source_target_pairs={{15,127},{31,111},{47,95},{63,79},{79,63},{95,47},{111,31},{127,15}} | collective-permute-start | bytes 196616 | tf_op jit(solution)/shard_map/ppermute | solution.py:478
  96.9 0.0 collective-permute-done.10.refs_7_
  96.9 0.0 collective-permute-done.11.refs_8_
  96.9 0.0 collective-permute-done.12.refs_9_
  96.9 5.2 %collective-permute-done.9.refs_6_ = f32[64,256]{1,0:T(8,128)S(1)} collective-permute-done((f32[64,256]{1,0:T(8,128)S(1)}, f32[64,256]{1,0:T(8,128)S(1)}, u32[]{:S(2)}, u32[]{:S(2)}) %collective-permute-start.9) | collective-permute-done | bytes 65568 | tf_op jit(solution)/shard_map/ppermute | solution.py:478
  102.1 7.5 %shard_map.91 = f32[2,16,16,256]{3,2,1,0:T(8,128)} custom-call(s32[7]{0:T(128)S(1)} %copy-done.6, f32[2,16,32,384]{3,2,1,0:T(8,128)S(1)} %get-tuple-element.48.refs_1_, f32[16,32,384]{2,1,0:T(8,128)S(1)} %get-tuple-element.37.refs_2_, f32[16,32,384]{2,1,0:T(8,128)S(1)} %get-tuple-element.38.refs_3_, f32[32,384]{1,0:T(8,128)S(1)} %get-tuple-element.39.refs_4_, ...), custom_call_target="tpu_custom_call" | custom-call | flops 10000000 | bytes 16777216 | tf_op jit(solution)/shard_map/pallas_call | solution.py:448
  (7 shorter events, 0.0 us)
Async XLA Ops:
  0.0 24.3 %copy-start.2 = (f32[16,16,256]{2,1,0:T(8,128)S(1)}, f32[16,16,256]{2,1,0:T(8,128)}, u32[]{:S(2)}) copy-start(f32[16,16,256]{2,1,0:T(8,128)} %refs_3_.11) | copy-start | bytes 786436
  0.0 24.3 %copy-start.5 = (s32[16,256]{1,0:T(8,128)S(1)}, s32[16,256]{1,0:T(8,128)}, u32[]{:S(2)}) copy-start(s32[16,256]{1,0:T(8,128)} %refs_4_.5) | copy-start | bytes 49156
  0.0 24.3 %copy-start.4 = (s32[4,16,256]{2,1,0:T(8,128)S(1)}, s32[4,16,256]{2,1,0:T(8,128)}, u32[]{:S(2)}) copy-start(s32[4,16,256]{2,1,0:T(8,128)} %refs_3_.15) | copy-start | bytes 196612
  0.0 24.3 %copy-start.3 = (f32[4,16,256]{2,1,0:T(8,128)S(1)}, f32[4,16,256]{2,1,0:T(8,128)}, u32[]{:S(2)}) copy-start(f32[4,16,256]{2,1,0:T(8,128)} %refs_2_.15) | copy-start | bytes 196612
  0.0 24.3 %copy-start = (f32[2,16,16,256]{3,2,1,0:T(8,128)S(1)}, f32[2,16,16,256]{3,2,1,0:T(8,128)}, u32[]{:S(2)}) copy-start(f32[2,16,16,256]{3,2,1,0:T(8,128)} %refs_1_.5) | copy-start | bytes 1572868
  0.0 24.3 %copy-start.1 = (f32[16,16,256]{2,1,0:T(8,128)S(1)}, f32[16,16,256]{2,1,0:T(8,128)}, u32[]{:S(2)}) copy-start(f32[16,16,256]{2,1,0:T(8,128)} %refs_2_.11) | copy-start | bytes 786436
  0.0 24.3 %copy-start.7 = (s32[256]{0:T(256)S(1)}, s32[256]{0:T(256)}, u32[]{:S(2)}) copy-start(s32[256]{0:T(256)} %param.12) | copy-start | bytes 3076
  0.7 23.6 %copy-start.6 = (s32[7]{0:T(128)S(1)}, s32[7]{0:T(128)}, u32[]{:S(2)}) copy-start(s32[7]{0:T(128)} %stack.35.refs_0_) | copy-start | bytes 88
  4.4 14.7 %collective-permute-start = (f32[73,8,256]{2,1,0:T(8,128)}, f32[73,8,256]{2,1,0:T(8,128)S(1)}, u32[]{:S(2)}, u32[]{:S(2)}) collective-permute-start(f32[73,8,256]{2,1,0:T(8,128)} %get-tuple-element.28), channel_id=1, source_target_pairs={{0,1},{2,3},{4,5},{6,7},{8,9},{10,11},{12,13},{14,15},{1,0},{3,2},... | collective-permute-start | bytes 1794056 | tf_op jit(solution)/shard_map/ppermute | solution.py:495
  5.1 19.2 %collective-permute-start.1 = (f32[73,8,256]{2,1,0:T(8,128)}, f32[73,8,256]{2,1,0:T(8,128)S(1)}, u32[]{:S(2)}, u32[]{:S(2)}) collective-permute-start(f32[73,8,256]{2,1,0:T(8,128)} %get-tuple-element.29), channel_id=1, source_target_pairs={{1,2},{3,4},{5,6},{7,8},{9,10},{11,12},{13,14},{2,1},{4,3},{6,5},{... | collective-permute-start | bytes 1794056 | tf_op jit(solution)/shard_map/ppermute | solution.py:499
  9.3 24.2 %all-to-all-start = ((f32[128,8,128]{2,1,0:T(8,128)}), f32[128,8,128]{2,1,0:T(8,128)S(1)}, u32[]{:S(2)}, u32[]{:S(2)}) async-start(f32[128,8,128]{2,1,0:T(8,128)} %get-tuple-element.34), calls=%async_computation | async-start | bytes 1048576 | tf_op jit(solution)/shard_map/all_to_all | solution.py:502
  17.5 1.5 %collective-permute-start.2 = (f32[10,8,256]{2,1,0:T(8,128)}, f32[10,8,256]{2,1,0:T(8,128)S(1)}, u32[]{:S(2)}, u32[]{:S(2)}) collective-permute-start(f32[10,8,256]{2,1,0:T(8,128)} %get-tuple-element.30), channel_id=1, source_target_pairs={{15,15},{31,127},{47,111},{63,95},{79,79},{95,63},{111,47},{127,31}} | collective-permute-start | bytes 245768 | tf_op jit(solution)/shard_map/ppermute | solution.py:478
  25.7 14.5 %collective-permute-start.3 = (f32[5,32,128]{2,1,0:T(8,128)S(1)}, f32[5,32,128]{2,1,0:T(8,128)S(1)}, u32[]{:S(2)}, u32[]{:S(2)}) collective-permute-start(f32[5,32,128]{2,1,0:T(8,128)S(1)} %get-tuple-element.32), channel_id=1, source_target_pairs={{16,0},{32,16},{48,32},{64,48},{80,64},{96,80},{112,96},{0,112},{1... | collective-permute-start | bytes 245768 | tf_op jit(solution)/shard_map/ppermute | solution.py:510
  32.4 7.7 %collective-permute-start.4 = (f32[5,32,128]{2,1,0:T(8,128)S(1)}, f32[5,32,128]{2,1,0:T(8,128)S(1)}, u32[]{:S(2)}, u32[]{:S(2)}) collective-permute-start(f32[5,32,128]{2,1,0:T(8,128)S(1)} %get-tuple-element.33), channel_id=1, source_target_pairs={{0,16},{16,32},{32,48},{48,64},{64,80},{80,96},{96,112},{112,0},{1... | collective-permute-start | bytes 245768 | tf_op jit(solution)/shard_map/ppermute | solution.py:511
  48.1 12.0 %collective-permute-start.5 = (f32[64,256]{1,0:T(8,128)S(1)}, f32[64,256]{1,0:T(8,128)S(1)}, u32[]{:S(2)}, u32[]{:S(2)}) collective-permute-start(f32[64,256]{1,0:T(8,128)S(1)} %get-tuple-element.45.refs_7_), channel_id=1, source_target_pairs={{15,127},{31,111},{47,95},{63,79},{79,63},{95,47},{111,31},{127,15}} | collective-permute-start | bytes 196616 | tf_op jit(solution)/shard_map/ppermute | solution.py:478
  59.5 8.1 %collective-permute-start.6 = (f32[64,256]{1,0:T(8,128)S(1)}, f32[64,256]{1,0:T(8,128)S(1)}, u32[]{:S(2)}, u32[]{:S(2)}) collective-permute-start(f32[64,256]{1,0:T(8,128)S(1)} %get-tuple-element.45.refs_7_), channel_id=1, source_target_pairs={{15,15},{31,127},{47,111},{63,95},{79,79},{95,63},{111,47},{127,31}} | collective-permute-start | bytes 196616 | tf_op jit(solution)/shard_map/ppermute | solution.py:478
  63.6 9.4 %collective-permute-start.7 = (f32[64,256]{1,0:T(8,128)S(1)}, f32[64,256]{1,0:T(8,128)S(1)}, u32[]{:S(2)}, u32[]{:S(2)}) collective-permute-start(f32[64,256]{1,0:T(8,128)S(1)} %get-tuple-element.45.refs_7_), channel_id=1, source_target_pairs={{15,111},{31,95},{47,79},{63,63},{79,47},{95,31},{111,15},{127,127}} | collective-permute-start | bytes 196616 | tf_op jit(solution)/shard_map/ppermute | solution.py:478
  71.0 7.0 %collective-permute-start.8 = (f32[64,256]{1,0:T(8,128)S(1)}, f32[64,256]{1,0:T(8,128)S(1)}, u32[]{:S(2)}, u32[]{:S(2)}) collective-permute-start(f32[64,256]{1,0:T(8,128)S(1)} %get-tuple-element.45.refs_7_), channel_id=1, source_target_pairs={{15,31},{31,15},{47,127},{63,111},{79,95},{95,79},{111,63},{127,47}} | collective-permute-start | bytes 196616 | tf_op jit(solution)/shard_map/ppermute | solution.py:478
  85.4 11.5 %collective-permute-start.10 = (f32[64,256]{1,0:T(8,128)S(1)}, f32[64,256]{1,0:T(8,128)S(1)}, u32[]{:S(2)}, u32[]{:S(2)}) collective-permute-start(f32[64,256]{1,0:T(8,128)S(1)} %get-tuple-element.49), channel_id=1, source_target_pairs={{15,15},{31,127},{47,111},{63,95},{79,79},{95,63},{111,47},{127,31}} | collective-permute-start | bytes 196616 | tf_op jit(solution)/shard_map/ppermute | solution.py:478
  86.0 10.8 %collective-permute-start.11 = (f32[64,256]{1,0:T(8,128)S(1)}, f32[64,256]{1,0:T(8,128)S(1)}, u32[]{:S(2)}, u32[]{:S(2)}) collective-permute-start(f32[64,256]{1,0:T(8,128)S(1)} %get-tuple-element.49), channel_id=1, source_target_pairs={{15,111},{31,95},{47,79},{63,63},{79,47},{95,31},{111,15},{127,127}} | collective-permute-start | bytes 196616 | tf_op jit(solution)/shard_map/ppermute | solution.py:478
  91.8 5.1 %collective-permute-start.12 = (f32[64,256]{1,0:T(8,128)S(1)}, f32[64,256]{1,0:T(8,128)S(1)}, u32[]{:S(2)}, u32[]{:S(2)}) collective-permute-start(f32[64,256]{1,0:T(8,128)S(1)} %get-tuple-element.49), channel_id=1, source_target_pairs={{15,31},{31,15},{47,127},{63,111},{79,95},{95,79},{111,63},{127,47}} | collective-permute-start | bytes 196616 | tf_op jit(solution)/shard_map/ppermute | solution.py:478
  94.9 7.1 %collective-permute-start.9 = (f32[64,256]{1,0:T(8,128)S(1)}, f32[64,256]{1,0:T(8,128)S(1)}, u32[]{:S(2)}, u32[]{:S(2)}) collective-permute-start(f32[64,256]{1,0:T(8,128)S(1)} %get-tuple-element.49), channel_id=1, source_target_pairs={{15,127},{31,111},{47,95},{63,79},{79,63},{95,47},{111,31},{127,15}} | collective-permute-start | bytes 196616 | tf_op jit(solution)/shard_map/ppermute | solution.py:478

commit v3 on v2

--- a/solution.py
+++ b/solution.py
@@ -159,7 +159,9 @@
 
 
 def one_hot_lookup(split_table, high, low, count):
-    chosen = (iota((512, count), 0) == high).astype(F32).astype(jnp.bfloat16)
+    short = lambda v: jnp.broadcast_to(v, (512, count)).astype(jnp.int16)
+    matches = lax.broadcasted_iota(jnp.int16, (512, count), 0) == short(high)
+    chosen = jnp.where(matches, jnp.bfloat16(1), jnp.bfloat16(0))
     got = jnp.dot(split_table[...], chosen, preferred_element_type=F32)
     lanes = iota((128, count), 0) == low
     first = jnp.sum(jnp.where(lanes, got[:128] + got[128:256], 0.0), axis=0, keepdims=True)
@@ -190,44 +192,40 @@
     return jnp.where(lane < 8, near, jnp.where(lane >= 120, far, 0.0))
 
 
-def lookup_kernel(groups, splits, last, info, table, weights, indices, first, second, ghosts, *rest):
-    if last:
-        from_east, from_west, surface, halo_surface, high, low, weight = rest
-    elif splits:
-        surface, split_table, high, low, weight = rest
-    else:
-        surface, high, low, weight = rest
+def lookup_kernel(groups, splits, last, info, table, *rest):
     if splits:
+        weights, indices, first, second, ghosts, surface, split_table, high, low, weight = rest
         split_kernel_table(table, split_table)
+        is_top = info[1] == 1
+        whole = Sides(info, first, second).whole
+        row = iota((32, 256), 0)
+        for j in range(4):
+            index = whole(68 + j, indices[j].astype(F32))
+            scale = whole(64 + j, weights[j])
+            for r in range(2):
+                ghost = jnp.logical_and(row == 24 + r, is_top)
+                scale = jnp.where(ghost, ghosts[64 + 8 * r + j : 65 + 8 * r + j, :], scale)
+                index = jnp.where(ghost, ghosts[68 + 8 * r + j : 69 + 8 * r + j, :], index)
+            high[j], low[j] = split_place(index.astype(jnp.int32))
+            weight[j] = scale
     else:
         split_table = table
-    is_top = info[1] == 1
-    whole = Sides(info, first, second).whole
-    row = iota((32, 256), 0)
-    for j in range(4):
-        index = whole(68 + j, indices[j].astype(F32))
-        scale = whole(64 + j, weights[j])
-        for r in range(2):
-            ghost = jnp.logical_and(row == 24 + r, is_top)
-            scale = jnp.where(ghost, ghosts[64 + 8 * r + j : 65 + 8 * r + j, :], scale)
-            index = jnp.where(ghost, ghosts[68 + 8 * r + j : 69 + 8 * r + j, :], index)
-        high[j], low[j] = split_place(index.astype(jnp.int32))
-        weight[j] = scale
-    surface[...] = jnp.zeros(surface.shape, F32)
-    start = 4 * groups[0]
-
-    def body(step, carry):
-        group, j = step // 4, step % 4
-        rows = [4 * group + i for i in range(4)]
-        join = lambda ref: jnp.concatenate([ref[j, pl.ds(start + r, 1), :] for r in rows], axis=1)
-        pair = one_hot_lookup(split_table, join(high), join(low), 1024)
-        for i, r in enumerate(rows):
-            scale = weight[j, pl.ds(start + r, 1), :]
-            for tracer in range(2):
-                surface[tracer, pl.ds(r, 1), :] += scale * pair[tracer][:, 256 * i : 256 * i + 256]
-        return carry
-
-    lax.fori_loop(0, 4 * len(groups), body, 0, unroll=2)
+        if last:
+            high, low, weight, from_east, from_west, surface, halo_surface = rest
+        else:
+            high, low, weight, surface = rest
+    for i, group in enumerate(groups):
+        totals = [[jnp.zeros((1, 256), F32) for _ in range(4)] for _ in range(2)]
+        for j in range(4):
+            rows = [slice(4 * group + q, 4 * group + q + 1) for q in range(4)]
+            join = lambda ref: jnp.concatenate([ref[j, r, :] for r in rows], axis=1)
+            pair = one_hot_lookup(split_table, join(high), join(low), 1024)
+            for q, r in enumerate(rows):
+                for tracer in range(2):
+                    totals[tracer][q] += weight[j, r, :] * pair[tracer][:, 256 * q : 256 * q + 256]
+        for tracer in range(2):
+            for q in range(4):
+                surface[tracer, 4 * i + q : 4 * i + q + 1, :] = totals[tracer][q]
     if last:
         lane = iota((32, 128), 1)
         small_lane, small_row = iota((16, 128), 1), iota((16, 128), 0)
@@ -280,7 +278,7 @@
     return pltpu.roll(f, 1, 0)
 
 
-def run_levels(cells, half_east, half_north, depth, surface, store, window=slice(0, 32), keep=slice(0, 32), tracers=(0, 1)):
+def run_levels(cells, half_east, half_north, depth, surface, store, window=slice(0, 32), keep=slice(0, 32), tracers=(0, 1), unroll=2):
     depth = depth[window, :]
     east_depth = jnp.minimum(depth, east_of(depth))
     north_depth = jnp.minimum(depth, north_of(depth))
@@ -311,7 +309,7 @@
             store(tracer, k, centre + jnp.where(wet, total, 0.0))
         return carry
 
-    lax.fori_loop(0, 16, body, 0)
+    lax.fori_loop(0, 16, body, 0, unroll=unroll)
 
 
 def keep_step(cells_out, fold_out):
@@ -427,7 +425,7 @@
     def store(tracer, k, fresh):
         result[tracer, k] = fresh[:, 0:256]
 
-    run_levels(start, east_ext, north_ext, depth_ext, surface_ext, store, keep=slice(8, 24))
+    run_levels(start, east_ext, north_ext, depth_ext, surface_ext, store, keep=slice(8, 24), unroll=4)
 
 
 def call(kernel, ins, outs, scratch=(), cost=None, earlier=(), ins_any=False, outs_any=False, alias=None, params=PARAMS):
@@ -510,20 +508,16 @@
     from_east = lax.ppermute(to_west, "lon", [((i + 1) % nlon, i) for i in range(nlon)])
     from_west = lax.ppermute(to_east, "lon", [(i, (i + 1) % nlon) for i in range(nlon)])
 
-    def lookups(groups, table, splits=False, last=False, earlier=()):
+    def lookups(groups, ins, splits=False, last=False, earlier=()):
         outs = [((2, 4 * len(groups), 256), F32)]
-        outs += [((512, 512), jnp.bfloat16)] if splits else [((2, 32, 128), F32)] if last else []
-        words = pltpu.VMEM((4, 32, 256), jnp.int32)
+        places = ((4, 32, 256), jnp.int32)
+        outs += [((512, 512), jnp.bfloat16), places, places, (places[0], F32)] if splits else []
+        outs += [((2, 32, 128), F32)] if last else []
         return call(
-            functools.partial(lookup_kernel, groups, splits, last),
-            (info, table, weights, indices, first, second, ghosts) + ((from_east, from_west) if last else ()),
-            outs,
-            [words, words, pltpu.VMEM((4, 32, 256), F32)],
-            lookup_cost(len(groups)),
-            earlier,
+            functools.partial(lookup_kernel, groups, splits, last), (info, *ins), outs, (), lookup_cost(len(groups)), earlier
         )
 
-    surface_a, split_table = lookups((1, 2), table, splits=True)
+    surface_a, *places = lookups((1, 2), (table, weights, indices, first, second, ghosts), splits=True)
 
     wide = (2, 16, 32, 384)
     cells, fold_rows, east_ext, north_ext, depth_ext, partner_ext = call(
@@ -536,13 +530,13 @@
     )
     statics = (east_ext, north_ext, depth_ext)
     received = [fold_permute(fold_rows, 0)]
-    (surface_b,) = lookups((3,), split_table, earlier=(fold_rows,))
+    (surface_b,) = lookups((3,), places, earlier=(fold_rows,))
     received.append(fold_permute(after(fold_rows, surface_b), 1))
-    (surface_c,) = lookups((4,), split_table, earlier=(received[0], surface_b))
+    (surface_c,) = lookups((4,), places, earlier=(received[0], surface_b))
     received.append(fold_permute(after(fold_rows, surface_c), -1))
-    (surface_d,) = lookups((5,), split_table, earlier=(received[1], surface_c))
+    (surface_d,) = lookups((5,), places, earlier=(received[1], surface_c))
     received.append(fold_permute(after(fold_rows, surface_d), 2))
-    surface_e, halo_surface = lookups((6,), split_table, last=True, earlier=(received[2], surface_d))
+    surface_e, halo_surface = lookups((6,), (*places, from_east, from_west), last=True, earlier=(received[2], surface_d))
 
     ghost_rows = pltpu.VMEM((64, 384), F32)
     cells, fold_rows, surface_ext = call(

time: 110 us -> 101 us (0.918)
  Pallas kernels: 49.7 us -> 40.5 us
  waiting for transfers between devices: 11.5 us -> 8.48 us
  starting transfers between devices: 47.3 us -> 49.6 us
    pallas_call x10, Pallas kernels: 49.7 us -> 40.5 us  [call(): pl.pallas_call(body, out_shape=tuple((jax.ShapeDtypeStruct(s, d) for s, d...]
    ppermute x9, waiting for transfers between devices: 5.18 us -> 2.12 us  [fold_permute(): return lax.ppermute(rows, both, pairs)]
    ppermute x9, starting transfers between devices: 27.4 us -> 29.8 us  [fold_permute(): return lax.ppermute(rows, both, pairs)]
  transfers between devices with their start and end apart: 14 -> 14, of which waited for: 3 -> 3; matrix products, arithmetic and copies ran while one was open for 0% -> 0% of each run, Pallas kernels for 21% -> 20%
where the time goes in v3:
time: 101 us; the launch traced here: 99.6 us
  starting transfers between devices  49.6 us (49%)
  Pallas kernels  40.5 us (40%)
  waiting for transfers between devices  8.48 us (8%)
    pallas_call x10, Pallas kernels, call(): pl.pallas_call(body, out_shape=tuple((jax.ShapeDtypeStruct(s, d) for s, d...  40.5 us
    ppermute x9, starting transfers between devices, fold_permute(): return lax.ppermute(rows, both, pairs)  29.8 us
    all_to_all x1, starting transfers between devices, per_device(): table = lax.all_to_all(slots, both, 0, 0, tiled=True)  8.13 us
    ppermute x1, starting transfers between devices, per_device(): lax.ppermute(to_west, 'lon', [((i + 1) % nlon, i) for i in range(nlon)])  6.76 us
    ppermute x1, waiting for transfers between devices, per_device(): second = lax.ppermute(second, both, swaps + facing)  5.24 us
    ppermute x1, starting transfers between devices, per_device(): second = lax.ppermute(second, both, swaps + facing)  4.21 us
    ppermute x9, waiting for transfers between devices, fold_permute(): return lax.ppermute(rows, both, pairs)  2.12 us
  transfers between devices with their start and end apart: 14, of which 3 were waited for; matrix products, arithmetic and copies ran while one was open for 0% of the time, Pallas kernels for 20%

profile of v3, /device:TPU:121, one launch (start us, length us, event | category | flops | bytes accessed | tf_op | source)
XLA Modules:
  0.0 99.6 jit_solution(16757263998726879944)
XLA Ops:
  0.0 0.0 copy-start.2
  0.0 0.0 copy-start.1
  0.0 0.0 copy-start
  0.0 0.0 copy-start.7
  0.1 0.6 stack.35.refs_0_
  0.7 3.6 %shard_map.82 = (f32[73,8,256]{2,1,0:T(8,128)}, f32[73,8,256]{2,1,0:T(8,128)}, f32[10,8,256]{2,1,0:T(8,128)}, f32[128,8,128]{2,1,0:T(8,128)}) custom-call(s32[7]{0:T(128)} %stack.35.refs_0_, f32[2,16,16,256]{3,2,1,0:T(8,128)} %refs_1_.5, f32[16,16,256]{2,1,0:T(8,128)} %refs_2_.7, f32[16,16,256]{2,1,0:T(8,128)} %refs_3_.7, s32[16,256]{1,0:T(8,128)} %refs_4_.5, ...), custom_call_target="tpu_custom_call" | custom-call | tf_op jit(solution)/shard_map/pallas_call | solution.py:446
  4.4 0.7 collective-permute-start
  5.1 4.2 %collective-permute-start.1 = (f32[73,8,256]{2,1,0:T(8,128)}, f32[73,8,256]{2,1,0:T(8,128)S(1)}, u32[]{:S(2)}, u32[]{:S(2)}) collective-permute-start(f32[73,8,256]{2,1,0:T(8,128)} %get-tuple-element.32), channel_id=1, source_target_pairs={{1,2},{3,4},{5,6},{7,8},{9,10},{11,12},{13,14},{2,1},{4,3},{6,5},{... | collective-permute-start | bytes 1794056 | tf_op jit(solution)/shard_map/ppermute | solution.py:497
  9.3 8.1 %all-to-all-start = ((f32[128,8,128]{2,1,0:T(8,128)}), f32[128,8,128]{2,1,0:T(8,128)S(1)}, u32[]{:S(2)}, u32[]{:S(2)}) async-start(f32[128,8,128]{2,1,0:T(8,128)} %get-tuple-element.37), calls=%async_computation | async-start | bytes 1048576 | tf_op jit(solution)/shard_map/all_to_all | solution.py:500
  17.5 1.5 %collective-permute-start.2 = (f32[10,8,256]{2,1,0:T(8,128)}, f32[10,8,256]{2,1,0:T(8,128)S(1)}, u32[]{:S(2)}, u32[]{:S(2)}) collective-permute-start(f32[10,8,256]{2,1,0:T(8,128)} %get-tuple-element.33), channel_id=1, source_target_pairs={{15,15},{31,127},{47,111},{63,95},{79,79},{95,63},{111,47},{127,31}} | collective-permute-start | bytes 245768 | tf_op jit(solution)/shard_map/ppermute | solution.py:476
  19.0 0.0 collective-permute-done.2.refs_10_
  19.0 0.0 collective-permute-done.refs_8_.refs_4_.refs_6_
  19.0 5.2 %collective-permute-done.1.refs_9_.refs_5_.refs_7_ = f32[73,8,256]{2,1,0:T(8,128)S(1)} collective-permute-done((f32[73,8,256]{2,1,0:T(8,128)}, f32[73,8,256]{2,1,0:T(8,128)S(1)}, u32[]{:S(2)}, u32[]{:S(2)}) %collective-permute-start.1) | collective-permute-done | bytes 598048 | tf_op jit(solution)/shard_map/ppermute | solution.py:497
  24.3 0.0 copy-done.2
  24.3 0.0 copy-done.1
  24.3 0.0 copy-done
  24.3 0.0 copy-done.7
  24.3 0.0 copy-done.6
  24.3 1.4 %shard_map.83 = (f32[80,256]{1,0:T(8,128)S(1)}, f32[5,32,128]{2,1,0:T(8,128)S(1)}, f32[5,32,128]{2,1,0:T(8,128)S(1)}) custom-call(s32[7]{0:T(128)S(1)} %copy-done.6, f32[2,16,16,256]{3,2,1,0:T(8,128)S(1)} %copy-done, f32[16,16,256]{2,1,0:T(8,128)S(1)} %copy-done.1, f32[16,16,256]{2,1,0:T(8,128)S(1)} %copy-done.2, s32[16,256]{1,0:T(8,128)S(1)} %copy-done.5, ...), custom_call_target="tpu_custom_call" | custom-call | tf_op jit(solution)/shard_map/pallas_call | solution.py:446
  25.7 6.8 %collective-permute-start.3 = (f32[5,32,128]{2,1,0:T(8,128)S(1)}, f32[5,32,128]{2,1,0:T(8,128)S(1)}, u32[]{:S(2)}, u32[]{:S(2)}) collective-permute-start(f32[5,32,128]{2,1,0:T(8,128)S(1)} %get-tuple-element.35), channel_id=1, source_target_pairs={{16,0},{32,16},{48,32},{64,48},{80,64},{96,80},{112,96},{0,112},{1... | collective-permute-start | bytes 245768 | tf_op jit(solution)/shard_map/ppermute | solution.py:508
  32.4 0.0 collective-permute-start.4
  32.4 1.1 %all-to-all-done.refs_1_ = f32[128,8,128]{2,1,0:T(8,128)S(1)} async-done(((f32[128,8,128]{2,1,0:T(8,128)}), f32[128,8,128]{2,1,0:T(8,128)S(1)}, u32[]{:S(2)}, u32[]{:S(2)}) %all-to-all-start) | async-done | bytes 524320 | tf_op jit(solution)/shard_map/all_to_all | solution.py:500
  33.5 5.6 %shard_map.84 = (f32[2,8,256]{2,1,0:T(8,128)S(1)}, bf16[512,512]{1,0:T(8,128)(2,1)S(1)}, s32[4,32,256]{2,1,0:T(8,128)S(1)}, s32[4,32,256]{2,1,0:T(8,128)S(1)}, f32[4,32,256]{2,1,0:T(8,128)S(1)}) custom-call(s32[7]{0:T(128)S(1)} %copy-done.6, f32[128,8,128]{2,1,0:T(8,128)S(1)} %all-to-all-done.refs_1_, f32[4,16,256]{2,1,0:T(8,128)S(1)} %copy-done.3, ...), custom_call_target="tpu_custom_call" | custom-call | flops 4294967296 | bytes 2097152 | tf_op jit(solution)/shard_map/pallas_call | solution.py:446
  39.2 0.0 collective-permute-done.3.refs_9_.refs_5_
  39.2 0.0 collective-permute-done.4.refs_10_.refs_6_
  39.2 6.1 %shard_map.85 = (f32[2,16,32,384]{3,2,1,0:T(8,128)S(1)}, f32[64,256]{1,0:T(8,128)S(1)}, f32[16,32,384]{2,1,0:T(8,128)S(1)}, f32[16,32,384]{2,1,0:T(8,128)S(1)}, ...) custom-call(s32[7]{0:T(128)S(1)} %copy-done.6, f32[2,16,16,256]{3,2,1,0:T(8,128)S(1)} %copy-done, ...), custom_call_target="tpu_custom_call" | custom-call | flops 10000000 | bytes 16777216 | tf_op jit(solution)/shard_map/pallas_call | solution.py:446
  45.3 7.9 %collective-permute-start.5 = (f32[64,256]{1,0:T(8,128)S(1)}, f32[64,256]{1,0:T(8,128)S(1)}, u32[]{:S(2)}, u32[]{:S(2)}) collective-permute-start(f32[64,256]{1,0:T(8,128)S(1)} %get-tuple-element.51.refs_5_), channel_id=1, source_target_pairs={{15,127},{31,111},{47,95},{63,79},{79,63},{95,47},{111,31},{127,15}} | collective-permute-start | bytes 196616 | tf_op jit(solution)/shard_map/ppermute | solution.py:476
  53.2 3.0 %shard_map.86.refs_6_.refs_11_ = f32[2,4,256]{2,1,0:T(4,128)S(1)} custom-call(s32[7]{0:T(128)S(1)} %copy-done.6, bf16[512,512]{1,0:T(8,128)(2,1)S(1)} %get-tuple-element.45.refs_1_, s32[4,32,256]{2,1,0:T(8,128)S(1)} %get-tuple-element.46.refs_2_, s32[4,32,256]{2,1,0:T(8,128)S(1)} %get-tuple-element.47.refs_3_, f32[4,32,256]{2,1,0:T(8,128)S(1)} %get-tuple-element.48.refs_4_, ...), custom_call_target="tpu_custom_call" | custom-call | flops 2147483648 | bytes 1048576 | tf_op jit(solution)/shard_map/pallas_call | solution.py:446
  56.2 0.7 collective-permute-start.6
  56.9 0.0 collective-permute-done.5.refs_5_.refs_6_
  56.9 3.0 %shard_map.87.refs_6_.refs_12_ = f32[2,4,256]{2,1,0:T(4,128)S(1)} custom-call(s32[7]{0:T(128)S(1)} %copy-done.6, bf16[512,512]{1,0:T(8,128)(2,1)S(1)} %get-tuple-element.45.refs_1_, s32[4,32,256]{2,1,0:T(8,128)S(1)} %get-tuple-element.46.refs_2_, s32[4,32,256]{2,1,0:T(8,128)S(1)} %get-tuple-element.47.refs_3_, f32[4,32,256]{2,1,0:T(8,128)S(1)} %get-tuple-element.48.refs_4_, ...), custom_call_target="tpu_custom_call" | custom-call | flops 2147483648 | bytes 1048576 | tf_op jit(solution)/shard_map/pallas_call | solution.py:446
  59.9 4.2 %collective-permute-start.7 = (f32[64,256]{1,0:T(8,128)S(1)}, f32[64,256]{1,0:T(8,128)S(1)}, u32[]{:S(2)}, u32[]{:S(2)}) collective-permute-start(f32[64,256]{1,0:T(8,128)S(1)} %get-tuple-element.51.refs_5_), channel_id=1, source_target_pairs={{15,111},{31,95},{47,79},{63,63},{79,47},{95,31},{111,15},{127,127}} | collective-permute-start | bytes 196616 | tf_op jit(solution)/shard_map/ppermute | solution.py:476
  64.1 0.0 collective-permute-done.6.refs_5_.refs_7_
  64.1 3.0 %shard_map.88.refs_8_.refs_13_ = f32[2,4,256]{2,1,0:T(4,128)S(1)} custom-call(s32[7]{0:T(128)S(1)} %copy-done.6, bf16[512,512]{1,0:T(8,128)(2,1)S(1)} %get-tuple-element.45.refs_1_, s32[4,32,256]{2,1,0:T(8,128)S(1)} %get-tuple-element.46.refs_2_, s32[4,32,256]{2,1,0:T(8,128)S(1)} %get-tuple-element.47.refs_3_, f32[4,32,256]{2,1,0:T(8,128)S(1)} %get-tuple-element.48.refs_4_, ...), custom_call_target="tpu_custom_call" | custom-call | flops 2147483648 | bytes 1048576 | tf_op jit(solution)/shard_map/pallas_call | solution.py:446
  67.1 1.9 %collective-permute-start.8 = (f32[64,256]{1,0:T(8,128)S(1)}, f32[64,256]{1,0:T(8,128)S(1)}, u32[]{:S(2)}, u32[]{:S(2)}) collective-permute-start(f32[64,256]{1,0:T(8,128)S(1)} %get-tuple-element.51.refs_5_), channel_id=1, source_target_pairs={{15,31},{31,15},{47,127},{63,111},{79,95},{95,79},{111,63},{127,47}} | collective-permute-start | bytes 196616 | tf_op jit(solution)/shard_map/ppermute | solution.py:476
  69.0 0.0 collective-permute-done.7.refs_7_.refs_8_
  69.0 4.0 %shard_map.89 = (f32[2,4,256]{2,1,0:T(4,128)S(1)}, f32[2,32,128]{2,1,0:T(8,128)S(1)}) custom-call(s32[7]{0:T(128)S(1)} %copy-done.6, bf16[512,512]{1,0:T(8,128)(2,1)S(1)} %get-tuple-element.45.refs_1_, s32[4,32,256]{2,1,0:T(8,128)S(1)} %get-tuple-element.46.refs_2_, s32[4,32,256]{2,1,0:T(8,128)S(1)} %get-tuple-element.47.refs_3_, ...), custom_call_target="tpu_custom_call" | custom-call | flops 2147483648 | bytes 1048576 | tf_op jit(solution)/shard_map/pallas_call | solution.py:446
  73.0 0.0 collective-permute-done.8.refs_9_
  73.0 5.5 %shard_map.90 = (f32[2,16,32,384]{3,2,1,0:T(8,128)S(1)}, f32[64,256]{1,0:T(8,128)S(1)}, f32[2,32,384]{2,1,0:T(8,128)S(1)}) custom-call(s32[7]{0:T(128)S(1)} %copy-done.6, f32[2,16,32,384]{3,2,1,0:T(8,128)S(1)} %get-tuple-element.39.refs_1_, f32[16,32,384]{2,1,0:T(8,128)S(1)} %get-tuple-element.40.refs_2_, f32[16,32,384]{2,1,0:T(8,128)S(1)} %get-tuple-element.41.refs_3_, ...), custom_call_target="tpu_custom_call" | custom-call | flops 10000000 | bytes 16777216 | tf_op jit(solution)/shard_map/pallas_call | solution.py:446
  78.5 3.4 %collective-permute-start.12 = (f32[64,256]{1,0:T(8,128)S(1)}, f32[64,256]{1,0:T(8,128)S(1)}, u32[]{:S(2)}, u32[]{:S(2)}) collective-permute-start(f32[64,256]{1,0:T(8,128)S(1)} %get-tuple-element.55), channel_id=1, source_target_pairs={{15,31},{31,15},{47,127},{63,111},{79,95},{95,79},{111,63},{127,47}} | collective-permute-start | bytes 196616 | tf_op jit(solution)/shard_map/ppermute | solution.py:476
  81.9 4.6 %collective-permute-start.11 = (f32[64,256]{1,0:T(8,128)S(1)}, f32[64,256]{1,0:T(8,128)S(1)}, u32[]{:S(2)}, u32[]{:S(2)}) collective-permute-start(f32[64,256]{1,0:T(8,128)S(1)} %get-tuple-element.55), channel_id=1, source_target_pairs={{15,111},{31,95},{47,79},{63,63},{79,47},{95,31},{111,15},{127,127}} | collective-permute-start | bytes 196616 | tf_op jit(solution)/shard_map/ppermute | solution.py:476
  86.5 0.7 collective-permute-start.10
  87.2 5.0 %collective-permute-start.9 = (f32[64,256]{1,0:T(8,128)S(1)}, f32[64,256]{1,0:T(8,128)S(1)}, u32[]{:S(2)}, u32[]{:S(2)}) collective-permute-start(f32[64,256]{1,0:T(8,128)S(1)} %get-tuple-element.55), channel_id=1, source_target_pairs={{15,127},{31,111},{47,95},{63,79},{79,63},{95,47},{111,31},{127,15}} | collective-permute-start | bytes 196616 | tf_op jit(solution)/shard_map/ppermute | solution.py:476
  92.1 0.0 collective-permute-done.12.refs_9_
  92.1 0.0 collective-permute-done.11.refs_8_
  92.2 0.0 collective-permute-done.10.refs_7_
  92.2 2.1 %collective-permute-done.9.refs_6_ = f32[64,256]{1,0:T(8,128)S(1)} collective-permute-done((f32[64,256]{1,0:T(8,128)S(1)}, f32[64,256]{1,0:T(8,128)S(1)}, u32[]{:S(2)}, u32[]{:S(2)}) %collective-permute-start.9) | collective-permute-done | bytes 65568 | tf_op jit(solution)/shard_map/ppermute | solution.py:476
  94.3 5.3 %shard_map.91 = f32[2,16,16,256]{3,2,1,0:T(8,128)} custom-call(s32[7]{0:T(128)S(1)} %copy-done.6, f32[2,16,32,384]{3,2,1,0:T(8,128)S(1)} %get-tuple-element.54.refs_1_, f32[16,32,384]{2,1,0:T(8,128)S(1)} %get-tuple-element.40.refs_2_, f32[16,32,384]{2,1,0:T(8,128)S(1)} %get-tuple-element.41.refs_3_, f32[32,384]{1,0:T(8,128)S(1)} %get-tuple-element.42.refs_4_, ...), custom_call_target="tpu_custom_call" | custom-call | flops 10000000 | bytes 16777216 | tf_op jit(solution)/shard_map/pallas_call | solution.py:446
  (7 shorter events, 0.0 us)
Async XLA Ops:
  0.0 24.3 %copy-start.3 = (f32[4,16,256]{2,1,0:T(8,128)S(1)}, f32[4,16,256]{2,1,0:T(8,128)}, u32[]{:S(2)}) copy-start(f32[4,16,256]{2,1,0:T(8,128)} %refs_2_.6) | copy-start | bytes 196612
  0.0 24.3 %copy-start.4 = (s32[4,16,256]{2,1,0:T(8,128)S(1)}, s32[4,16,256]{2,1,0:T(8,128)}, u32[]{:S(2)}) copy-start(s32[4,16,256]{2,1,0:T(8,128)} %refs_3_.6) | copy-start | bytes 196612
  0.0 24.3 %copy-start.5 = (s32[16,256]{1,0:T(8,128)S(1)}, s32[16,256]{1,0:T(8,128)}, u32[]{:S(2)}) copy-start(s32[16,256]{1,0:T(8,128)} %refs_4_.5) | copy-start | bytes 49156
  0.0 24.3 %copy-start.2 = (f32[16,16,256]{2,1,0:T(8,128)S(1)}, f32[16,16,256]{2,1,0:T(8,128)}, u32[]{:S(2)}) copy-start(f32[16,16,256]{2,1,0:T(8,128)} %refs_3_.7) | copy-start | bytes 786436
  0.0 24.3 %copy-start.1 = (f32[16,16,256]{2,1,0:T(8,128)S(1)}, f32[16,16,256]{2,1,0:T(8,128)}, u32[]{:S(2)}) copy-start(f32[16,16,256]{2,1,0:T(8,128)} %refs_2_.7) | copy-start | bytes 786436
  0.0 24.3 %copy-start = (f32[2,16,16,256]{3,2,1,0:T(8,128)S(1)}, f32[2,16,16,256]{3,2,1,0:T(8,128)}, u32[]{:S(2)}) copy-start(f32[2,16,16,256]{3,2,1,0:T(8,128)} %refs_1_.5) | copy-start | bytes 1572868
  0.0 24.3 %copy-start.7 = (s32[256]{0:T(256)S(1)}, s32[256]{0:T(256)}, u32[]{:S(2)}) copy-start(s32[256]{0:T(256)} %param.12) | copy-start | bytes 3076
  0.7 23.6 %copy-start.6 = (s32[7]{0:T(128)S(1)}, s32[7]{0:T(128)}, u32[]{:S(2)}) copy-start(s32[7]{0:T(128)} %stack.35.refs_0_) | copy-start | bytes 88
  4.4 14.7 %collective-permute-start = (f32[73,8,256]{2,1,0:T(8,128)}, f32[73,8,256]{2,1,0:T(8,128)S(1)}, u32[]{:S(2)}, u32[]{:S(2)}) collective-permute-start(f32[73,8,256]{2,1,0:T(8,128)} %get-tuple-element.31), channel_id=1, source_target_pairs={{0,1},{2,3},{4,5},{6,7},{8,9},{10,11},{12,13},{14,15},{1,0},{3,2},... | collective-permute-start | bytes 1794056 | tf_op jit(solution)/shard_map/ppermute | solution.py:493
  5.1 19.2 %collective-permute-start.1 = (f32[73,8,256]{2,1,0:T(8,128)}, f32[73,8,256]{2,1,0:T(8,128)S(1)}, u32[]{:S(2)}, u32[]{:S(2)}) collective-permute-start(f32[73,8,256]{2,1,0:T(8,128)} %get-tuple-element.32), channel_id=1, source_target_pairs={{1,2},{3,4},{5,6},{7,8},{9,10},{11,12},{13,14},{2,1},{4,3},{6,5},{... | collective-permute-start | bytes 1794056 | tf_op jit(solution)/shard_map/ppermute | solution.py:497
  9.3 24.2 %all-to-all-start = ((f32[128,8,128]{2,1,0:T(8,128)}), f32[128,8,128]{2,1,0:T(8,128)S(1)}, u32[]{:S(2)}, u32[]{:S(2)}) async-start(f32[128,8,128]{2,1,0:T(8,128)} %get-tuple-element.37), calls=%async_computation | async-start | bytes 1048576 | tf_op jit(solution)/shard_map/all_to_all | solution.py:500
  17.5 1.5 %collective-permute-start.2 = (f32[10,8,256]{2,1,0:T(8,128)}, f32[10,8,256]{2,1,0:T(8,128)S(1)}, u32[]{:S(2)}, u32[]{:S(2)}) collective-permute-start(f32[10,8,256]{2,1,0:T(8,128)} %get-tuple-element.33), channel_id=1, source_target_pairs={{15,15},{31,127},{47,111},{63,95},{79,79},{95,63},{111,47},{127,31}} | collective-permute-start | bytes 245768 | tf_op jit(solution)/shard_map/ppermute | solution.py:476
  25.7 13.5 %collective-permute-start.3 = (f32[5,32,128]{2,1,0:T(8,128)S(1)}, f32[5,32,128]{2,1,0:T(8,128)S(1)}, u32[]{:S(2)}, u32[]{:S(2)}) collective-permute-start(f32[5,32,128]{2,1,0:T(8,128)S(1)} %get-tuple-element.35), channel_id=1, source_target_pairs={{16,0},{32,16},{48,32},{64,48},{80,64},{96,80},{112,96},{0,112},{1... | collective-permute-start | bytes 245768 | tf_op jit(solution)/shard_map/ppermute | solution.py:508
  32.4 6.8 %collective-permute-start.4 = (f32[5,32,128]{2,1,0:T(8,128)S(1)}, f32[5,32,128]{2,1,0:T(8,128)S(1)}, u32[]{:S(2)}, u32[]{:S(2)}) collective-permute-start(f32[5,32,128]{2,1,0:T(8,128)S(1)} %get-tuple-element.36), channel_id=1, source_target_pairs={{0,16},{16,32},{32,48},{48,64},{64,80},{80,96},{96,112},{112,0},{1... | collective-permute-start | bytes 245768 | tf_op jit(solution)/shard_map/ppermute | solution.py:509
  45.3 11.6 %collective-permute-start.5 = (f32[64,256]{1,0:T(8,128)S(1)}, f32[64,256]{1,0:T(8,128)S(1)}, u32[]{:S(2)}, u32[]{:S(2)}) collective-permute-start(f32[64,256]{1,0:T(8,128)S(1)} %get-tuple-element.51.refs_5_), channel_id=1, source_target_pairs={{15,127},{31,111},{47,95},{63,79},{79,63},{95,47},{111,31},{127,15}} | collective-permute-start | bytes 196616 | tf_op jit(solution)/shard_map/ppermute | solution.py:476
  56.2 7.9 %collective-permute-start.6 = (f32[64,256]{1,0:T(8,128)S(1)}, f32[64,256]{1,0:T(8,128)S(1)}, u32[]{:S(2)}, u32[]{:S(2)}) collective-permute-start(f32[64,256]{1,0:T(8,128)S(1)} %get-tuple-element.51.refs_5_), channel_id=1, source_target_pairs={{15,15},{31,127},{47,111},{63,95},{79,79},{95,63},{111,47},{127,31}} | collective-permute-start | bytes 196616 | tf_op jit(solution)/shard_map/ppermute | solution.py:476
  59.9 9.1 %collective-permute-start.7 = (f32[64,256]{1,0:T(8,128)S(1)}, f32[64,256]{1,0:T(8,128)S(1)}, u32[]{:S(2)}, u32[]{:S(2)}) collective-permute-start(f32[64,256]{1,0:T(8,128)S(1)} %get-tuple-element.51.refs_5_), channel_id=1, source_target_pairs={{15,111},{31,95},{47,79},{63,63},{79,47},{95,31},{111,15},{127,127}} | collective-permute-start | bytes 196616 | tf_op jit(solution)/shard_map/ppermute | solution.py:476
  67.1 5.9 %collective-permute-start.8 = (f32[64,256]{1,0:T(8,128)S(1)}, f32[64,256]{1,0:T(8,128)S(1)}, u32[]{:S(2)}, u32[]{:S(2)}) collective-permute-start(f32[64,256]{1,0:T(8,128)S(1)} %get-tuple-element.51.refs_5_), channel_id=1, source_target_pairs={{15,31},{31,15},{47,127},{63,111},{79,95},{95,79},{111,63},{127,47}} | collective-permute-start | bytes 196616 | tf_op jit(solution)/shard_map/ppermute | solution.py:476
  78.5 13.6 %collective-permute-start.12 = (f32[64,256]{1,0:T(8,128)S(1)}, f32[64,256]{1,0:T(8,128)S(1)}, u32[]{:S(2)}, u32[]{:S(2)}) collective-permute-start(f32[64,256]{1,0:T(8,128)S(1)} %get-tuple-element.55), channel_id=1, source_target_pairs={{15,31},{31,15},{47,127},{63,111},{79,95},{95,79},{111,63},{127,47}} | collective-permute-start | bytes 196616 | tf_op jit(solution)/shard_map/ppermute | solution.py:476
  81.9 10.3 %collective-permute-start.11 = (f32[64,256]{1,0:T(8,128)S(1)}, f32[64,256]{1,0:T(8,128)S(1)}, u32[]{:S(2)}, u32[]{:S(2)}) collective-permute-start(f32[64,256]{1,0:T(8,128)S(1)} %get-tuple-element.55), channel_id=1, source_target_pairs={{15,111},{31,95},{47,79},{63,63},{79,47},{95,31},{111,15},{127,127}} | collective-permute-start | bytes 196616 | tf_op jit(solution)/shard_map/ppermute | solution.py:476
  86.5 5.7 %collective-permute-start.10 = (f32[64,256]{1,0:T(8,128)S(1)}, f32[64,256]{1,0:T(8,128)S(1)}, u32[]{:S(2)}, u32[]{:S(2)}) collective-permute-start(f32[64,256]{1,0:T(8,128)S(1)} %get-tuple-element.55), channel_id=1, source_target_pairs={{15,15},{31,127},{47,111},{63,95},{79,79},{95,63},{111,47},{127,31}} | collective-permute-start | bytes 196616 | tf_op jit(solution)/shard_map/ppermute | solution.py:476
  87.2 7.1 %collective-permute-start.9 = (f32[64,256]{1,0:T(8,128)S(1)}, f32[64,256]{1,0:T(8,128)S(1)}, u32[]{:S(2)}, u32[]{:S(2)}) collective-permute-start(f32[64,256]{1,0:T(8,128)S(1)} %get-tuple-element.55), channel_id=1, source_target_pairs={{15,127},{31,111},{47,95},{63,79},{79,63},{95,47},{111,31},{127,15}} | collective-permute-start | bytes 196616 | tf_op jit(solution)/shard_map/ppermute | solution.py:476

commit v4 on v3

--- a/solution.py
+++ b/solution.py
@@ -8,8 +8,8 @@
 from jax.sharding import PartitionSpec as P
 
 H = 8
+PLANES = 64
 VMEM = pl.BlockSpec(memory_space=pltpu.VMEM)
-SMEM = pl.BlockSpec(memory_space=pltpu.SMEM)
 PARAMS = pltpu.CompilerParams(vmem_limit_bytes=20 * 2**20)
 F32 = jnp.float32
 LANE_GATHER = lax.GatherDimensionNumbers(
@@ -25,6 +25,13 @@
     return lax.gather(
         values, lanes[..., None], LANE_GATHER, (1, 1), mode=lax.GatherScatterMode.PROMISE_IN_BOUNDS
     )
+
+
+def own_place():
+    nlon, nlat = lax.axis_size("lon"), lax.axis_size("lat")
+    t, lat = lax.axis_index("lon"), lax.axis_index("lat")
+    tiles = [lax.rem(2 * nlon - 1 - t + d, nlon) for d in (0, 1, -1, 2)]
+    return [t, (lat == nlat - 1).astype(jnp.int32), *tiles, lax.rem(lat, 2)]
 
 
 def pick_columns(partner, sources):
@@ -55,26 +62,31 @@
             cut = flux[tracer : tracer + 1, 128 * quarter : 128 * quarter + 128]
             slots[:, 4 * tracer + quarter, :] = jnp.broadcast_to(cut, (128, 128))
 
-    def write(out, rows):
+    def write(out, rows, near, fifth):
         for tracer in range(2):
             out[16 * tracer : 16 * tracer + 16] = tracers[tracer, :, rows, :]
-        out[32:48] = east[:, rows, :]
-        out[48:64] = north[:, rows, :]
-        out[64:68] = weights[:, rows, :]
-        out[68:72] = indices[:, rows, :].astype(F32)
-        out[72] = levels[rows, :].astype(F32)
-
+        for half in range(2):
+            levels_in, rows_out = slice(8 * half, 8 * half + 8), slice(4 * half, 4 * half + 4)
+            out[32:40, rows_out, :] = east[levels_in, near, :]
+            out[40:48, rows_out, :] = north[levels_in, near, :]
+            out[53 + half] = north[levels_in, fifth, :]
+        out[48:52, 0:4, :] = weights[:, near, :]
+        out[48:52, 4:8, :] = indices[:, near, :].astype(F32)
+        out[52] = levels[rows, :].astype(F32)
+        out[55:PLANES] = jnp.zeros((PLANES - 55, H, 256), F32)
+
+    southward, northward = (slice(0, 8), slice(0, 4), 4), (slice(8, 16), slice(12, 16), 11)
     is_odd = info[6] == 1
 
     @pl.when(is_odd)
     def _():
-        write(first, slice(0, 8))
-        write(second, slice(8, 16))
+        write(first, *southward)
+        write(second, *northward)
 
     @pl.when(jnp.logical_not(is_odd))
     def _():
-        write(first, slice(8, 16))
-        write(second, slice(0, 8))
+        write(first, *northward)
+        write(second, *southward)
 
     for r in range(2):
         for tracer in range(2):
@@ -97,15 +109,35 @@
         self.odd, self.top = info[6] == 1, info[1] == 1
         self.first, self.second = first, second
 
-    def south(self, plane, cut=slice(None)):
-        return jnp.where(self.odd, self.first[plane, :, cut], self.second[plane, :, cut])
-
-    def north(self, plane, cut=slice(None)):
-        got = jnp.where(self.odd, self.second[plane, :, cut], self.first[plane, :, cut])
-        return jnp.where(self.top, 0.0, got)
+    def blocks(self, plane, cut):
+        first, second = self.first[plane, :, cut], self.second[plane, :, cut]
+        north = jnp.where(self.top, 0.0, jnp.where(self.odd, second, first))
+        return jnp.where(self.odd, first, second), north
 
     def whole(self, plane, centre, cut=slice(None)):
-        return jnp.concatenate([self.south(plane, cut), centre, self.north(plane, cut)], axis=0)
+        south, north = self.blocks(plane, cut)
+        return jnp.concatenate([south, centre, north], axis=0)
+
+    def near(self, plane, upper, centre, cut=slice(None)):
+        south, north = self.blocks(plane, cut)
+        turned_south, turned_north = pltpu.roll(south, 4, 0), pltpu.roll(north, 4, 0)
+        if isinstance(upper, bool):
+            south, north = (south, turned_north) if upper else (turned_south, north)
+        else:
+            south, north = jnp.where(upper, south, turned_south), jnp.where(upper, turned_north, north)
+        return jnp.concatenate([south, centre, north], axis=0)
+
+    def velocity(self, first_plane, k, centre, cut=slice(None)):
+        if isinstance(k, int):
+            return self.near(first_plane + k % 8, k >= 8, centre, cut)
+        return self.near(first_plane + jnp.bitwise_and(k, 7), k >= 8, centre, cut)
+
+    def north_velocity(self, k, centre, cut=slice(None)):
+        got = self.velocity(40, k, centre, cut)
+        plane, at = (53 + k // 8, k % 8) if isinstance(k, int) else (53 + jnp.right_shift(k, 3), jnp.bitwise_and(k, 7))
+        row = pl.ds(at, 1)
+        fifth = jnp.where(self.odd, self.first[plane, row, cut], self.second[plane, row, cut])
+        return jnp.where(iota(got.shape, 0) == 3, fifth, got)
 
 
 def pack_kernel(info, tracers, east, north, levels, weights, indices, partner, first, second, fold_b, ghosts, to_west, to_east):
@@ -125,7 +157,8 @@
     beyond = jnp.logical_and(row >= 24, is_top)
     west_cut, east_cut = slice(0, 128), slice(128, 256)
 
-    whole = Sides(info, first, second).whole
+    sides = Sides(info, first, second)
+    whole = sides.whole
 
     def value(plane, cut):
         if plane < 32:
@@ -133,15 +166,16 @@
             got = jnp.where(ghost_first, ghosts[plane : plane + 1, cut], got)
             return jnp.where(ghost_second, ghosts[32 + plane : 33 + plane, cut], got)
         if plane < 48:
-            return whole(plane, east[plane - 32, :, cut], cut)
+            return sides.velocity(32, plane - 32, east[plane - 32, :, cut], cut)
         if plane < 64:
-            return jnp.where(last_north, 0.0, whole(plane, north[plane - 48, :, cut], cut))
+            return jnp.where(last_north, 0.0, sides.north_velocity(plane - 48, north[plane - 48, :, cut], cut))
         if plane < 72:
             centre = weights[plane - 64, :, cut] if plane < 68 else indices[plane - 68, :, cut].astype(F32)
-            got = jnp.where(ghost_first, ghosts[plane : plane + 1, cut], whole(plane, centre, cut))
+            got = sides.near(48 + plane % 4, plane >= 68, centre, cut)
+            got = jnp.where(ghost_first, ghosts[plane : plane + 1, cut], got)
             return jnp.where(ghost_second, ghosts[plane + 8 : plane + 9, cut], got)
         if plane == 72:
-            return jnp.where(beyond, 16.0, whole(plane, levels[:, cut].astype(F32), cut))
+            return jnp.where(beyond, 16.0, whole(52, levels[:, cut].astype(F32), cut))
         return jnp.broadcast_to(partner[:, cut].astype(F32), (32, 128))
 
     for group in range(5):
@@ -197,11 +231,11 @@
         weights, indices, first, second, ghosts, surface, split_table, high, low, weight = rest
         split_kernel_table(table, split_table)
         is_top = info[1] == 1
-        whole = Sides(info, first, second).whole
+        near = Sides(info, first, second).near
         row = iota((32, 256), 0)
         for j in range(4):
-            index = whole(68 + j, indices[j].astype(F32))
-            scale = whole(64 + j, weights[j])
+            index = near(48 + j, True, indices[j].astype(F32))
+            scale = near(48 + j, False, weights[j])
             for r in range(2):
                 ghost = jnp.logical_and(row == 24 + r, is_top)
                 scale = jnp.where(ghost, ghosts[64 + 8 * r + j : 65 + 8 * r + j, :], scale)
@@ -341,15 +375,16 @@
     last_north = jnp.logical_and(row == 23, is_top)
     halo = functools.partial(halo_tile, from_east, from_west, lane)
 
-    whole = Sides(info, first, second).whole
+    sides = Sides(info, first, second)
+    whole = sides.whole
 
     def fill(k, carry):
         for tracer in range(2):
             start[tracer, k, :, 0:256] = whole(tracer * 16 + k, tracers[tracer, k])
             start[tracer, k, :, 256:384] = halo(tracer, k)
-        east_ext[k, :, 0:256] = 0.5 * whole(32 + k, east[k])
+        east_ext[k, :, 0:256] = 0.5 * sides.velocity(32, k, east[k])
         east_ext[k, :, 256:384] = 0.5 * halo(2, k)
-        north_ext[k, :, 0:256] = jnp.where(last_north, 0.0, 0.5 * whole(48 + k, north[k]))
+        north_ext[k, :, 0:256] = jnp.where(last_north, 0.0, 0.5 * sides.north_velocity(k, north[k]))
         north_ext[k, :, 256:384] = 0.5 * halo(3, k)
         return carry
 
@@ -360,7 +395,7 @@
         place_ghosts(start, ghosts, 256)
 
     depth_ext[:, 0:256] = jnp.where(
-        jnp.logical_and(row >= 24, is_top), 16.0, whole(72, levels[...].astype(F32))
+        jnp.logical_and(row >= 24, is_top), 16.0, whole(52, levels[...].astype(F32))
     )
     depth_ext[:, 256:384] = halo(4, 8)
     partner_ext[:, 0:256] = jnp.broadcast_to(partner[...], (8, 256))
@@ -432,14 +467,12 @@
     used = len(ins)
 
     def body(*refs):
-        kernel(*refs[:used], *refs[used + len(earlier) :])
+        kernel(own_place(), *refs[:used], *refs[used + len(earlier) :])
 
     anywhere = pl.BlockSpec(memory_space=pl.ANY)
     hbm = pl.BlockSpec(memory_space=pltpu.HBM)
 
     def place(i, v):
-        if v.ndim == 1:
-            return SMEM
         return hbm if ins_any or i == alias else anywhere if i >= used else VMEM
 
     arrays = tuple(ins) + tuple(earlier)
@@ -465,22 +498,18 @@
 def per_device(tracers, east, north, levels, partner, atm_flux, indices, weights):
     nlon, nlat = lax.axis_size("lon"), lax.axis_size("lat")
     both = ("lon", "lat")
-    t, lat = lax.axis_index("lon"), lax.axis_index("lat")
-    is_top = (lat == nlat - 1).astype(jnp.int32)
-    tiles = [jnp.remainder(nlon - 1 - t + d, nlon) for d in (0, 1, -1, 2)]
-    info = jnp.stack([t, is_top] + tiles + [lat % 2]).astype(jnp.int32)
     top = nlat - 1
 
     def fold_permute(rows, d):
         pairs = [(i * nlat + top, ((nlon - 1 + d - i) % nlon) * nlat + top) for i in range(nlon)]
         return lax.ppermute(rows, both, pairs)
 
-    message = ((73, H, 256), F32)
+    message = ((PLANES, H, 256), F32)
     whole_inputs = (tracers, east, north, levels, weights, indices)
     build_inputs = (*whole_inputs, atm_flux)
     first, second, fold_rows, slots = call(
         build_kernel,
-        (info, *build_inputs),
+        build_inputs,
         [message, message, ((10, 8, 256), F32), ((nlon * nlat, 8, 128), F32)],
         [pltpu.VMEM(a.shape, a.dtype) for a in build_inputs] + [pltpu.SemaphoreType.DMA((7,))],
         ins_any=True,
@@ -502,7 +531,7 @@
     partner_row = partner.reshape(1, -1)
     ghosts, to_west, to_east = call(
         pack_kernel,
-        (info, *whole_inputs, partner_row, first, second, fold_b),
+        (*whole_inputs, partner_row, first, second, fold_b),
         [((80, 256), F32), ((5, 32, 128), F32), ((5, 32, 128), F32)],
     )
     from_east = lax.ppermute(to_west, "lon", [((i + 1) % nlon, i) for i in range(nlon)])
@@ -514,7 +543,7 @@
         outs += [((512, 512), jnp.bfloat16), places, places, (places[0], F32)] if splits else []
         outs += [((2, 32, 128), F32)] if last else []
         return call(
-            functools.partial(lookup_kernel, groups, splits, last), (info, *ins), outs, (), lookup_cost(len(groups)), earlier
+            functools.partial(lookup_kernel, groups, splits, last), ins, outs, (), lookup_cost(len(groups)), earlier
         )
 
     surface_a, *places = lookups((1, 2), (table, weights, indices, first, second, ghosts), splits=True)
@@ -522,7 +551,7 @@
     wide = (2, 16, 32, 384)
     cells, fold_rows, east_ext, north_ext, depth_ext, partner_ext = call(
         first_kernel,
-        (info, tracers, east, north, levels, partner_row, first, second, ghosts, from_east, from_west),
+        (tracers, east, north, levels, partner_row, first, second, ghosts, from_east, from_west),
         [(wide, F32), ((64, 256), F32), (wide[1:], F32), (wide[1:], F32), ((32, 384), F32), ((8, 384), jnp.int32)],
         [pltpu.VMEM(wide, F32)],
         STEP_COST,
@@ -541,7 +570,7 @@
     ghost_rows = pltpu.VMEM((64, 384), F32)
     cells, fold_rows, surface_ext = call(
         second_kernel,
-        (info, cells, *statics, partner_ext, *received, surface_a, surface_b, surface_c, surface_d, surface_e,
+        (cells, *statics, partner_ext, *received, surface_a, surface_b, surface_c, surface_d, surface_e,
          halo_surface),
         [(wide, F32), ((64, 256), F32), ((2, 32, 384), F32)],
         [ghost_rows, pltpu.VMEM(wide, F32)],
@@ -550,7 +579,7 @@
     received = [fold_permute(fold_rows, d) for d in (0, 1, -1, 2)]
     (result,) = call(
         last_kernel,
-        (info, cells, *statics, partner_ext, *received, surface_ext),
+        (cells, *statics, partner_ext, *received, surface_ext),
         [(tracers.shape, F32)],
         [ghost_rows, pltpu.VMEM(wide, F32)],
         STEP_COST,

time: 101 us -> 92 us (0.911)
  Pallas kernels: 40.5 us -> 34.3 us
  waiting for transfers between devices: 8.48 us -> 4.1 us
  starting transfers between devices: 49.6 us -> 52.2 us
    pallas_call x10, Pallas kernels: 40.5 us -> 34.3 us  [call(): pl.pallas_call(body, out_shape=tuple((jax.ShapeDtypeStruct(s, d) for s, d...]
    ppermute x1, waiting for transfers between devices: 5.24 us -> 1.73 us  [per_device(): second = lax.ppermute(second, both, swaps + facing)]
    ppermute x1, starting transfers between devices: 6.76 us -> 9.62 us  [per_device(): lax.ppermute(to_west, 'lon', [((i + 1) % nlon, i) for i in range(nlon)])]
    all_to_all x1, waiting for transfers between devices: 1.1 us -> 0.06 us  [per_device(): table = lax.all_to_all(slots, both, 0, 0, tiled=True)]
  transfers between devices with their start and end apart: 14 -> 14, of which waited for: 3 -> 4; matrix products, arithmetic and copies ran while one was open for 0% -> 0% of each run, Pallas kernels for 20% -> 18%
where the time goes in v4:
time: 92 us; the launch traced here: 90.9 us
  starting transfers between devices  52.2 us (57%)
  Pallas kernels  34.3 us (37%)
  waiting for transfers between devices  4.1 us (4%)
    pallas_call x10, Pallas kernels, call(): pl.pallas_call(body, out_shape=tuple((jax.ShapeDtypeStruct(s, d) for s, d...  34.3 us
    ppermute x9, starting transfers between devices, fold_permute(): return lax.ppermute(rows, both, pairs)  29.5 us
    ppermute x1, starting transfers between devices, per_device(): lax.ppermute(to_west, 'lon', [((i + 1) % nlon, i) for i in range(nlon)])  9.62 us
    all_to_all x1, starting transfers between devices, per_device(): table = lax.all_to_all(slots, both, 0, 0, tiled=True)  8.13 us
    ppermute x1, starting transfers between devices, per_device(): second = lax.ppermute(second, both, swaps + facing)  4.21 us
    ppermute x9, waiting for transfers between devices, fold_permute(): return lax.ppermute(rows, both, pairs)  2.12 us
  transfers between devices with their start and end apart: 14, of which 4 were waited for; matrix products, arithmetic and copies ran while one was open for 0% of the time, Pallas kernels for 18%

profile of v4, /device:TPU:121, one launch (start us, length us, event | category | flops | bytes accessed | tf_op | source)
XLA Modules:
  0.0 90.9 jit_solution(12390679454460929465)
XLA Ops:
  0.0 0.0 copy-start.2
  0.0 0.0 copy-start.1
  0.0 0.0 copy-start
  0.0 0.0 copy-start.6
  0.0 3.0 %shard_map.82 = (f32[64,8,256]{2,1,0:T(8,128)}, f32[64,8,256]{2,1,0:T(8,128)}, f32[10,8,256]{2,1,0:T(8,128)}, f32[128,8,128]{2,1,0:T(8,128)}) custom-call(f32[2,16,16,256]{3,2,1,0:T(8,128)} %refs_0_.5, f32[16,16,256]{2,1,0:T(8,128)} %refs_1_.7, f32[16,16,256]{2,1,0:T(8,128)} %refs_2_.7, s32[16,256]{1,0:T(8,128)} %refs_3_.5, f32[4,16,256]{2,1,0:T(8,128)} %refs_1_.6, ...), custom_call_target="tpu_custom_call" | custom-call | tf_op jit(solution)/shard_map/pallas_call | solution.py:479
  3.0 0.7 collective-permute-start
  3.8 4.2 %collective-permute-start.1 = (f32[64,8,256]{2,1,0:T(8,128)}, f32[64,8,256]{2,1,0:T(8,128)S(1)}, u32[]{:S(2)}, u32[]{:S(2)}) collective-permute-start(f32[64,8,256]{2,1,0:T(8,128)} %get-tuple-element.32), channel_id=1, source_target_pairs={{1,2},{3,4},{5,6},{7,8},{9,10},{11,12},{13,14},{2,1},{4,3},{6,5},{... | collective-permute-start | bytes 1572872 | tf_op jit(solution)/shard_map/ppermute | solution.py:526
  8.0 8.1 %all-to-all-start = ((f32[128,8,128]{2,1,0:T(8,128)}), f32[128,8,128]{2,1,0:T(8,128)S(1)}, u32[]{:S(2)}, u32[]{:S(2)}) async-start(f32[128,8,128]{2,1,0:T(8,128)} %get-tuple-element.37), calls=%async_computation | async-start | bytes 1048576 | tf_op jit(solution)/shard_map/all_to_all | solution.py:529
  16.1 1.5 %collective-permute-start.2 = (f32[10,8,256]{2,1,0:T(8,128)}, f32[10,8,256]{2,1,0:T(8,128)S(1)}, u32[]{:S(2)}, u32[]{:S(2)}) collective-permute-start(f32[10,8,256]{2,1,0:T(8,128)} %get-tuple-element.33), channel_id=1, source_target_pairs={{15,15},{31,127},{47,111},{63,95},{79,79},{95,63},{111,47},{127,31}} | collective-permute-start | bytes 245768 | tf_op jit(solution)/shard_map/ppermute | solution.py:505
  17.7 0.0 collective-permute-done.2.refs_9_
  17.7 0.0 collective-permute-done.refs_7_.refs_3_.refs_5_
  17.7 1.7 %collective-permute-done.1.refs_8_.refs_4_.refs_6_ = f32[64,8,256]{2,1,0:T(8,128)S(1)} collective-permute-done((f32[64,8,256]{2,1,0:T(8,128)}, f32[64,8,256]{2,1,0:T(8,128)S(1)}, u32[]{:S(2)}, u32[]{:S(2)}) %collective-permute-start.1) | collective-permute-done | bytes 524320 | tf_op jit(solution)/shard_map/ppermute | solution.py:526
  19.4 0.0 copy-done.3
  19.4 0.0 copy-done.4
  19.4 0.0 copy-done.5
  19.4 0.0 copy-done.2
  19.4 0.0 copy-done.1
  19.4 0.0 copy-done
  19.5 0.8 shard_map.83
  20.3 9.6 %collective-permute-start.3 = (f32[5,32,128]{2,1,0:T(8,128)S(1)}, f32[5,32,128]{2,1,0:T(8,128)S(1)}, u32[]{:S(2)}, u32[]{:S(2)}) collective-permute-start(f32[5,32,128]{2,1,0:T(8,128)S(1)} %get-tuple-element.35), channel_id=1, source_target_pairs={{16,0},{32,16},{48,32},{64,48},{80,64},{96,80},{112,96},{0,112},{1... | collective-permute-start | bytes 245768 | tf_op jit(solution)/shard_map/ppermute | solution.py:537
  29.9 0.0 collective-permute-start.4
  29.9 0.1 all-to-all-done.refs_0_
  30.0 5.1 %shard_map.84 = (f32[2,8,256]{2,1,0:T(8,128)S(1)}, bf16[512,512]{1,0:T(8,128)(2,1)S(1)}, s32[4,32,256]{2,1,0:T(8,128)S(1)}, s32[4,32,256]{2,1,0:T(8,128)S(1)}, f32[4,32,256]{2,1,0:T(8,128)S(1)}) custom-call(f32[128,8,128]{2,1,0:T(8,128)S(1)} %all-to-all-done.refs_0_, f32[4,16,256]{2,1,0:T(8,128)S(1)} %copy-done.3, s32[4,16,256]{2,1,0:T(8,128)S(1)} %copy-done.4, ...), custom_call_target="tpu_custom_call" | custom-call | flops 4294967296 | bytes 2097152 | tf_op jit(solution)/shard_map/pallas_call | solution.py:479
  35.1 0.0 collective-permute-done.3.refs_8_.refs_4_
  35.1 0.2 collective-permute-done.4.refs_9_.refs_5_
  35.3 5.2 %shard_map.85 = (f32[2,16,32,384]{3,2,1,0:T(8,128)S(1)}, f32[64,256]{1,0:T(8,128)S(1)}, f32[16,32,384]{2,1,0:T(8,128)S(1)}, f32[16,32,384]{2,1,0:T(8,128)S(1)}, ...) custom-call(f32[2,16,16,256]{3,2,1,0:T(8,128)S(1)} %copy-done, f32[16,16,256]{2,1,0:T(8,128)S(1)} %copy-done.1, ...), custom_call_target="tpu_custom_call" | custom-call | flops 10000000 | bytes 16777216 | tf_op jit(solution)/shard_map/pallas_call | solution.py:479
  40.5 7.6 %collective-permute-start.5 = (f32[64,256]{1,0:T(8,128)S(1)}, f32[64,256]{1,0:T(8,128)S(1)}, u32[]{:S(2)}, u32[]{:S(2)}) collective-permute-start(f32[64,256]{1,0:T(8,128)S(1)} %get-tuple-element.51.refs_4_), channel_id=1, source_target_pairs={{15,127},{31,111},{47,95},{63,79},{79,63},{95,47},{111,31},{127,15}} | collective-permute-start | bytes 196616 | tf_op jit(solution)/shard_map/ppermute | solution.py:505
  48.1 2.5 %shard_map.86.refs_5_.refs_10_ = f32[2,4,256]{2,1,0:T(4,128)S(1)} custom-call(bf16[512,512]{1,0:T(8,128)(2,1)S(1)} %get-tuple-element.45.refs_0_, s32[4,32,256]{2,1,0:T(8,128)S(1)} %get-tuple-element.46.refs_1_, s32[4,32,256]{2,1,0:T(8,128)S(1)} %get-tuple-element.47.refs_2_, f32[4,32,256]{2,1,0:T(8,128)S(1)} %get-tuple-element.48.refs_3_, ...), custom_call_target="tpu_custom_call" | custom-call | flops 2147483648 | bytes 1048576 | tf_op jit(solution)/shard_map/pallas_call | solution.py:479
  50.6 0.7 collective-permute-start.6
  51.3 0.0 collective-permute-done.5.refs_4_.refs_5_
  51.3 2.5 %shard_map.87.refs_5_.refs_11_ = f32[2,4,256]{2,1,0:T(4,128)S(1)} custom-call(bf16[512,512]{1,0:T(8,128)(2,1)S(1)} %get-tuple-element.45.refs_0_, s32[4,32,256]{2,1,0:T(8,128)S(1)} %get-tuple-element.46.refs_1_, s32[4,32,256]{2,1,0:T(8,128)S(1)} %get-tuple-element.47.refs_2_, f32[4,32,256]{2,1,0:T(8,128)S(1)} %get-tuple-element.48.refs_3_, ...), custom_call_target="tpu_custom_call" | custom-call | flops 2147483648 | bytes 1048576 | tf_op jit(solution)/shard_map/pallas_call | solution.py:479
  53.8 4.2 %collective-permute-start.7 = (f32[64,256]{1,0:T(8,128)S(1)}, f32[64,256]{1,0:T(8,128)S(1)}, u32[]{:S(2)}, u32[]{:S(2)}) collective-permute-start(f32[64,256]{1,0:T(8,128)S(1)} %get-tuple-element.51.refs_4_), channel_id=1, source_target_pairs={{15,111},{31,95},{47,79},{63,63},{79,47},{95,31},{111,15},{127,127}} | collective-permute-start | bytes 196616 | tf_op jit(solution)/shard_map/ppermute | solution.py:505
  57.9 0.0 collective-permute-done.6.refs_4_.refs_6_
  57.9 2.5 %shard_map.88.refs_7_.refs_12_ = f32[2,4,256]{2,1,0:T(4,128)S(1)} custom-call(bf16[512,512]{1,0:T(8,128)(2,1)S(1)} %get-tuple-element.45.refs_0_, s32[4,32,256]{2,1,0:T(8,128)S(1)} %get-tuple-element.46.refs_1_, s32[4,32,256]{2,1,0:T(8,128)S(1)} %get-tuple-element.47.refs_2_, f32[4,32,256]{2,1,0:T(8,128)S(1)} %get-tuple-element.48.refs_3_, ...), custom_call_target="tpu_custom_call" | custom-call | flops 2147483648 | bytes 1048576 | tf_op jit(solution)/shard_map/pallas_call | solution.py:479
  60.4 1.9 %collective-permute-start.8 = (f32[64,256]{1,0:T(8,128)S(1)}, f32[64,256]{1,0:T(8,128)S(1)}, u32[]{:S(2)}, u32[]{:S(2)}) collective-permute-start(f32[64,256]{1,0:T(8,128)S(1)} %get-tuple-element.51.refs_4_), channel_id=1, source_target_pairs={{15,31},{31,15},{47,127},{63,111},{79,95},{95,79},{111,63},{127,47}} | collective-permute-start | bytes 196616 | tf_op jit(solution)/shard_map/ppermute | solution.py:505
  62.3 0.0 collective-permute-done.7.refs_6_.refs_7_
  62.3 3.4 %shard_map.89 = (f32[2,4,256]{2,1,0:T(4,128)S(1)}, f32[2,32,128]{2,1,0:T(8,128)S(1)}) custom-call(bf16[512,512]{1,0:T(8,128)(2,1)S(1)} %get-tuple-element.45.refs_0_, s32[4,32,256]{2,1,0:T(8,128)S(1)} %get-tuple-element.46.refs_1_, s32[4,32,256]{2,1,0:T(8,128)S(1)} %get-tuple-element.47.refs_2_, f32[4,32,256]{2,1,0:T(8,128)S(1)} %get-tuple-element.48.refs_3_, ...), custom_call_target="tpu_custom_call" | custom-call | flops 2147483648 | bytes 1048576 | tf_op jit(solution)/shard_map/pallas_call | solution.py:479
  65.7 0.0 collective-permute-done.8.refs_8_
  65.7 4.7 %shard_map.90 = (f32[2,16,32,384]{3,2,1,0:T(8,128)S(1)}, f32[64,256]{1,0:T(8,128)S(1)}, f32[2,32,384]{2,1,0:T(8,128)S(1)}) custom-call(f32[2,16,32,384]{3,2,1,0:T(8,128)S(1)} %get-tuple-element.39.refs_0_, f32[16,32,384]{2,1,0:T(8,128)S(1)} %get-tuple-element.40.refs_1_, f32[16,32,384]{2,1,0:T(8,128)S(1)} %get-tuple-element.41.refs_2_, ...), custom_call_target="tpu_custom_call" | custom-call | flops 10000000 | bytes 16777216 | tf_op jit(solution)/shard_map/pallas_call | solution.py:479
  70.4 3.4 %collective-permute-start.12 = (f32[64,256]{1,0:T(8,128)S(1)}, f32[64,256]{1,0:T(8,128)S(1)}, u32[]{:S(2)}, u32[]{:S(2)}) collective-permute-start(f32[64,256]{1,0:T(8,128)S(1)} %get-tuple-element.55), channel_id=1, source_target_pairs={{15,31},{31,15},{47,127},{63,111},{79,95},{95,79},{111,63},{127,47}} | collective-permute-start | bytes 196616 | tf_op jit(solution)/shard_map/ppermute | solution.py:505
  73.8 4.6 %collective-permute-start.11 = (f32[64,256]{1,0:T(8,128)S(1)}, f32[64,256]{1,0:T(8,128)S(1)}, u32[]{:S(2)}, u32[]{:S(2)}) collective-permute-start(f32[64,256]{1,0:T(8,128)S(1)} %get-tuple-element.55), channel_id=1, source_target_pairs={{15,111},{31,95},{47,79},{63,63},{79,47},{95,31},{111,15},{127,127}} | collective-permute-start | bytes 196616 | tf_op jit(solution)/shard_map/ppermute | solution.py:505
  78.4 0.7 collective-permute-start.10
  79.1 5.0 %collective-permute-start.9 = (f32[64,256]{1,0:T(8,128)S(1)}, f32[64,256]{1,0:T(8,128)S(1)}, u32[]{:S(2)}, u32[]{:S(2)}) collective-permute-start(f32[64,256]{1,0:T(8,128)S(1)} %get-tuple-element.55), channel_id=1, source_target_pairs={{15,127},{31,111},{47,95},{63,79},{79,63},{95,47},{111,31},{127,15}} | collective-permute-start | bytes 196616 | tf_op jit(solution)/shard_map/ppermute | solution.py:505
  84.1 0.0 collective-permute-done.12.refs_8_
  84.1 0.0 collective-permute-done.11.refs_7_
  84.1 0.0 collective-permute-done.10.refs_6_
  84.1 2.1 %collective-permute-done.9.refs_5_ = f32[64,256]{1,0:T(8,128)S(1)} collective-permute-done((f32[64,256]{1,0:T(8,128)S(1)}, f32[64,256]{1,0:T(8,128)S(1)}, u32[]{:S(2)}, u32[]{:S(2)}) %collective-permute-start.9) | collective-permute-done | bytes 65568 | tf_op jit(solution)/shard_map/ppermute | solution.py:505
  86.2 4.6 %shard_map.91 = f32[2,16,16,256]{3,2,1,0:T(8,128)} custom-call(f32[2,16,32,384]{3,2,1,0:T(8,128)S(1)} %get-tuple-element.54.refs_0_, f32[16,32,384]{2,1,0:T(8,128)S(1)} %get-tuple-element.40.refs_1_, f32[16,32,384]{2,1,0:T(8,128)S(1)} %get-tuple-element.41.refs_2_, f32[32,384]{1,0:T(8,128)S(1)} %get-tuple-element.42.refs_3_, ...), custom_call_target="tpu_custom_call" | custom-call | flops 10000000 | bytes 16777216 | tf_op jit(solution)/shard_map/pallas_call | solution.py:479
  (4 shorter events, 0.0 us)
Async XLA Ops:
  0.0 19.4 %copy-start.3 = (f32[4,16,256]{2,1,0:T(8,128)S(1)}, f32[4,16,256]{2,1,0:T(8,128)}, u32[]{:S(2)}) copy-start(f32[4,16,256]{2,1,0:T(8,128)} %refs_1_.6) | copy-start | bytes 196612
  0.0 19.4 %copy-start.4 = (s32[4,16,256]{2,1,0:T(8,128)S(1)}, s32[4,16,256]{2,1,0:T(8,128)}, u32[]{:S(2)}) copy-start(s32[4,16,256]{2,1,0:T(8,128)} %refs_2_.6) | copy-start | bytes 196612
  0.0 19.4 %copy-start.5 = (s32[16,256]{1,0:T(8,128)S(1)}, s32[16,256]{1,0:T(8,128)}, u32[]{:S(2)}) copy-start(s32[16,256]{1,0:T(8,128)} %refs_3_.5) | copy-start | bytes 49156
  0.0 19.4 %copy-start.2 = (f32[16,16,256]{2,1,0:T(8,128)S(1)}, f32[16,16,256]{2,1,0:T(8,128)}, u32[]{:S(2)}) copy-start(f32[16,16,256]{2,1,0:T(8,128)} %refs_2_.7) | copy-start | bytes 786436
  0.0 19.4 %copy-start.1 = (f32[16,16,256]{2,1,0:T(8,128)S(1)}, f32[16,16,256]{2,1,0:T(8,128)}, u32[]{:S(2)}) copy-start(f32[16,16,256]{2,1,0:T(8,128)} %refs_1_.7) | copy-start | bytes 786436
  0.0 19.4 %copy-start = (f32[2,16,16,256]{3,2,1,0:T(8,128)S(1)}, f32[2,16,16,256]{3,2,1,0:T(8,128)}, u32[]{:S(2)}) copy-start(f32[2,16,16,256]{3,2,1,0:T(8,128)} %refs_0_.5) | copy-start | bytes 1572868
  0.0 19.4 %copy-start.6 = (s32[256]{0:T(256)S(1)}, s32[256]{0:T(256)}, u32[]{:S(2)}) copy-start(s32[256]{0:T(256)} %param.12) | copy-start | bytes 3076
  3.0 14.7 %collective-permute-start = (f32[64,8,256]{2,1,0:T(8,128)}, f32[64,8,256]{2,1,0:T(8,128)S(1)}, u32[]{:S(2)}, u32[]{:S(2)}) collective-permute-start(f32[64,8,256]{2,1,0:T(8,128)} %get-tuple-element.31), channel_id=1, source_target_pairs={{0,1},{2,3},{4,5},{6,7},{8,9},{10,11},{12,13},{14,15},{1,0},{3,2},... | collective-permute-start | bytes 1572872 | tf_op jit(solution)/shard_map/ppermute | solution.py:522
  3.8 15.6 %collective-permute-start.1 = (f32[64,8,256]{2,1,0:T(8,128)}, f32[64,8,256]{2,1,0:T(8,128)S(1)}, u32[]{:S(2)}, u32[]{:S(2)}) collective-permute-start(f32[64,8,256]{2,1,0:T(8,128)} %get-tuple-element.32), channel_id=1, source_target_pairs={{1,2},{3,4},{5,6},{7,8},{9,10},{11,12},{13,14},{2,1},{4,3},{6,5},{... | collective-permute-start | bytes 1572872 | tf_op jit(solution)/shard_map/ppermute | solution.py:526
  8.0 22.0 %all-to-all-start = ((f32[128,8,128]{2,1,0:T(8,128)}), f32[128,8,128]{2,1,0:T(8,128)S(1)}, u32[]{:S(2)}, u32[]{:S(2)}) async-start(f32[128,8,128]{2,1,0:T(8,128)} %get-tuple-element.37), calls=%async_computation | async-start | bytes 1048576 | tf_op jit(solution)/shard_map/all_to_all | solution.py:529
  16.1 1.5 %collective-permute-start.2 = (f32[10,8,256]{2,1,0:T(8,128)}, f32[10,8,256]{2,1,0:T(8,128)S(1)}, u32[]{:S(2)}, u32[]{:S(2)}) collective-permute-start(f32[10,8,256]{2,1,0:T(8,128)} %get-tuple-element.33), channel_id=1, source_target_pairs={{15,15},{31,127},{47,111},{63,95},{79,79},{95,63},{111,47},{127,31}} | collective-permute-start | bytes 245768 | tf_op jit(solution)/shard_map/ppermute | solution.py:505
  20.3 14.8 %collective-permute-start.3 = (f32[5,32,128]{2,1,0:T(8,128)S(1)}, f32[5,32,128]{2,1,0:T(8,128)S(1)}, u32[]{:S(2)}, u32[]{:S(2)}) collective-permute-start(f32[5,32,128]{2,1,0:T(8,128)S(1)} %get-tuple-element.35), channel_id=1, source_target_pairs={{16,0},{32,16},{48,32},{64,48},{80,64},{96,80},{112,96},{0,112},{1... | collective-permute-start | bytes 245768 | tf_op jit(solution)/shard_map/ppermute | solution.py:537
  29.9 5.4 %collective-permute-start.4 = (f32[5,32,128]{2,1,0:T(8,128)S(1)}, f32[5,32,128]{2,1,0:T(8,128)S(1)}, u32[]{:S(2)}, u32[]{:S(2)}) collective-permute-start(f32[5,32,128]{2,1,0:T(8,128)S(1)} %get-tuple-element.36), channel_id=1, source_target_pairs={{0,16},{16,32},{32,48},{48,64},{64,80},{80,96},{96,112},{112,0},{1... | collective-permute-start | bytes 245768 | tf_op jit(solution)/shard_map/ppermute | solution.py:538
  40.5 10.7 %collective-permute-start.5 = (f32[64,256]{1,0:T(8,128)S(1)}, f32[64,256]{1,0:T(8,128)S(1)}, u32[]{:S(2)}, u32[]{:S(2)}) collective-permute-start(f32[64,256]{1,0:T(8,128)S(1)} %get-tuple-element.51.refs_4_), channel_id=1, source_target_pairs={{15,127},{31,111},{47,95},{63,79},{79,63},{95,47},{111,31},{127,15}} | collective-permute-start | bytes 196616 | tf_op jit(solution)/shard_map/ppermute | solution.py:505
  50.6 7.3 %collective-permute-start.6 = (f32[64,256]{1,0:T(8,128)S(1)}, f32[64,256]{1,0:T(8,128)S(1)}, u32[]{:S(2)}, u32[]{:S(2)}) collective-permute-start(f32[64,256]{1,0:T(8,128)S(1)} %get-tuple-element.51.refs_4_), channel_id=1, source_target_pairs={{15,15},{31,127},{47,111},{63,95},{79,79},{95,63},{111,47},{127,31}} | collective-permute-start | bytes 196616 | tf_op jit(solution)/shard_map/ppermute | solution.py:505
  53.8 8.6 %collective-permute-start.7 = (f32[64,256]{1,0:T(8,128)S(1)}, f32[64,256]{1,0:T(8,128)S(1)}, u32[]{:S(2)}, u32[]{:S(2)}) collective-permute-start(f32[64,256]{1,0:T(8,128)S(1)} %get-tuple-element.51.refs_4_), channel_id=1, source_target_pairs={{15,111},{31,95},{47,79},{63,63},{79,47},{95,31},{111,15},{127,127}} | collective-permute-start | bytes 196616 | tf_op jit(solution)/shard_map/ppermute | solution.py:505
  60.4 5.3 %collective-permute-start.8 = (f32[64,256]{1,0:T(8,128)S(1)}, f32[64,256]{1,0:T(8,128)S(1)}, u32[]{:S(2)}, u32[]{:S(2)}) collective-permute-start(f32[64,256]{1,0:T(8,128)S(1)} %get-tuple-element.51.refs_4_), channel_id=1, source_target_pairs={{15,31},{31,15},{47,127},{63,111},{79,95},{95,79},{111,63},{127,47}} | collective-permute-start | bytes 196616 | tf_op jit(solution)/shard_map/ppermute | solution.py:505
  70.4 13.6 %collective-permute-start.12 = (f32[64,256]{1,0:T(8,128)S(1)}, f32[64,256]{1,0:T(8,128)S(1)}, u32[]{:S(2)}, u32[]{:S(2)}) collective-permute-start(f32[64,256]{1,0:T(8,128)S(1)} %get-tuple-element.55), channel_id=1, source_target_pairs={{15,31},{31,15},{47,127},{63,111},{79,95},{95,79},{111,63},{127,47}} | collective-permute-start | bytes 196616 | tf_op jit(solution)/shard_map/ppermute | solution.py:505
  73.8 10.3 %collective-permute-start.11 = (f32[64,256]{1,0:T(8,128)S(1)}, f32[64,256]{1,0:T(8,128)S(1)}, u32[]{:S(2)}, u32[]{:S(2)}) collective-permute-start(f32[64,256]{1,0:T(8,128)S(1)} %get-tuple-element.55), channel_id=1, source_target_pairs={{15,111},{31,95},{47,79},{63,63},{79,47},{95,31},{111,15},{127,127}} | collective-permute-start | bytes 196616 | tf_op jit(solution)/shard_map/ppermute | solution.py:505
  78.4 5.7 %collective-permute-start.10 = (f32[64,256]{1,0:T(8,128)S(1)}, f32[64,256]{1,0:T(8,128)S(1)}, u32[]{:S(2)}, u32[]{:S(2)}) collective-permute-start(f32[64,256]{1,0:T(8,128)S(1)} %get-tuple-element.55), channel_id=1, source_target_pairs={{15,15},{31,127},{47,111},{63,95},{79,79},{95,63},{111,47},{127,31}} | collective-permute-start | bytes 196616 | tf_op jit(solution)/shard_map/ppermute | solution.py:505
  79.1 7.1 %collective-permute-start.9 = (f32[64,256]{1,0:T(8,128)S(1)}, f32[64,256]{1,0:T(8,128)S(1)}, u32[]{:S(2)}, u32[]{:S(2)}) collective-permute-start(f32[64,256]{1,0:T(8,128)S(1)} %get-tuple-element.55), channel_id=1, source_target_pairs={{15,127},{31,111},{47,95},{63,79},{79,63},{95,47},{111,31},{127,15}} | collective-permute-start | bytes 196616 | tf_op jit(solution)/shard_map/ppermute | solution.py:505

commit v5 on v4

--- a/solution.py
+++ b/solution.py
@@ -248,18 +248,26 @@
             high, low, weight, from_east, from_west, surface, halo_surface = rest
         else:
             high, low, weight, surface = rest
-    for i, group in enumerate(groups):
-        totals = [[jnp.zeros((1, 256), F32) for _ in range(4)] for _ in range(2)]
+    def look_up(i, group, count):
+        totals = [[jnp.zeros((1, 256), F32) for _ in range(count)] for _ in range(2)]
+        rows = [slice(4 * group + q, 4 * group + q + 1) for q in range(count)]
         for j in range(4):
-            rows = [slice(4 * group + q, 4 * group + q + 1) for q in range(4)]
             join = lambda ref: jnp.concatenate([ref[j, r, :] for r in rows], axis=1)
-            pair = one_hot_lookup(split_table, join(high), join(low), 1024)
+            pair = one_hot_lookup(split_table, join(high), join(low), 256 * count)
             for q, r in enumerate(rows):
                 for tracer in range(2):
                     totals[tracer][q] += weight[j, r, :] * pair[tracer][:, 256 * q : 256 * q + 256]
         for tracer in range(2):
-            for q in range(4):
+            for q in range(count):
                 surface[tracer, 4 * i + q : 4 * i + q + 1, :] = totals[tracer][q]
+
+    if last:
+        surface[...] = jnp.zeros(surface.shape, F32)
+        pl.when(info[1] == 1)(lambda: look_up(0, groups[0], 2))
+        pl.when(info[1] != 1)(lambda: look_up(0, groups[0], 4))
+    else:
+        for i, group in enumerate(groups):
+            look_up(i, group, 4)
     if last:
         lane = iota((32, 128), 1)
         small_lane, small_row = iota((16, 128), 1), iota((16, 128), 0)

time: 92 us -> 91.6 us (level)
  transfers between devices with their start and end apart: 14 -> 14, of which waited for: 4 -> 5; matrix products, arithmetic and copies ran while one was open for 0% -> 0% of each run, Pallas kernels for 18% -> 18%
where the time goes in v5:
time: 91.6 us; the launch traced here: 90.4 us
  starting transfers between devices  52.1 us (57%)
  Pallas kernels  33.8 us (37%)
  waiting for transfers between devices  4.22 us (5%)
    pallas_call x10, Pallas kernels, call(): pl.pallas_call(body, out_shape=tuple((jax.ShapeDtypeStruct(s, d) for s, d...  33.8 us
    ppermute x9, starting transfers between devices, fold_permute(): return lax.ppermute(rows, both, pairs)  29.4 us
    ppermute x1, starting transfers between devices, per_device(): lax.ppermute(to_west, 'lon', [((i + 1) % nlon, i) for i in range(nlon)])  9.62 us
    all_to_all x1, starting transfers between devices, per_device(): table = lax.all_to_all(slots, both, 0, 0, tiled=True)  8.13 us
    ppermute x1, starting transfers between devices, per_device(): second = lax.ppermute(second, both, swaps + facing)  4.21 us
    ppermute x9, waiting for transfers between devices, fold_permute(): return lax.ppermute(rows, both, pairs)  2.24 us
  transfers between devices with their start and end apart: 14, of which 5 were waited for; matrix products, arithmetic and copies ran while one was open for 0% of the time, Pallas kernels for 18%

profile of v5, /device:TPU:121, one launch (start us, length us, event | category | flops | bytes accessed | tf_op | source)
XLA Modules:
  0.0 90.4 jit_solution(5279107809026073709)
XLA Ops:
  0.0 0.0 copy-start.2
  0.0 0.0 copy-start.1
  0.0 0.0 copy-start
  0.0 0.0 copy-start.6
  0.0 3.0 %shard_map.82 = (f32[64,8,256]{2,1,0:T(8,128)}, f32[64,8,256]{2,1,0:T(8,128)}, f32[10,8,256]{2,1,0:T(8,128)}, f32[128,8,128]{2,1,0:T(8,128)}) custom-call(f32[2,16,16,256]{3,2,1,0:T(8,128)} %refs_0_.5, f32[16,16,256]{2,1,0:T(8,128)} %refs_1_.7, f32[16,16,256]{2,1,0:T(8,128)} %refs_2_.7, s32[16,256]{1,0:T(8,128)} %refs_3_.5, f32[4,16,256]{2,1,0:T(8,128)} %refs_1_.6, ...), custom_call_target="tpu_custom_call" | custom-call | tf_op jit(solution)/shard_map/pallas_call | solution.py:487
  3.0 0.7 collective-permute-start
  3.8 4.2 %collective-permute-start.1 = (f32[64,8,256]{2,1,0:T(8,128)}, f32[64,8,256]{2,1,0:T(8,128)S(1)}, u32[]{:S(2)}, u32[]{:S(2)}) collective-permute-start(f32[64,8,256]{2,1,0:T(8,128)} %get-tuple-element.32), channel_id=1, source_target_pairs={{1,2},{3,4},{5,6},{7,8},{9,10},{11,12},{13,14},{2,1},{4,3},{6,5},{... | collective-permute-start | bytes 1572872 | tf_op jit(solution)/shard_map/ppermute | solution.py:534
  8.0 8.1 %all-to-all-start = ((f32[128,8,128]{2,1,0:T(8,128)}), f32[128,8,128]{2,1,0:T(8,128)S(1)}, u32[]{:S(2)}, u32[]{:S(2)}) async-start(f32[128,8,128]{2,1,0:T(8,128)} %get-tuple-element.37), calls=%async_computation | async-start | bytes 1048576 | tf_op jit(solution)/shard_map/all_to_all | solution.py:537
  16.1 1.5 %collective-permute-start.2 = (f32[10,8,256]{2,1,0:T(8,128)}, f32[10,8,256]{2,1,0:T(8,128)S(1)}, u32[]{:S(2)}, u32[]{:S(2)}) collective-permute-start(f32[10,8,256]{2,1,0:T(8,128)} %get-tuple-element.33), channel_id=1, source_target_pairs={{15,15},{31,127},{47,111},{63,95},{79,79},{95,63},{111,47},{127,31}} | collective-permute-start | bytes 245768 | tf_op jit(solution)/shard_map/ppermute | solution.py:513
  17.7 0.0 collective-permute-done.2.refs_9_
  17.7 0.0 collective-permute-done.refs_7_.refs_3_.refs_5_
  17.7 1.7 %collective-permute-done.1.refs_8_.refs_4_.refs_6_ = f32[64,8,256]{2,1,0:T(8,128)S(1)} collective-permute-done((f32[64,8,256]{2,1,0:T(8,128)}, f32[64,8,256]{2,1,0:T(8,128)S(1)}, u32[]{:S(2)}, u32[]{:S(2)}) %collective-permute-start.1) | collective-permute-done | bytes 524320 | tf_op jit(solution)/shard_map/ppermute | solution.py:534
  19.4 0.0 copy-done.3
  19.4 0.0 copy-done.4
  19.4 0.0 copy-done.5
  19.4 0.0 copy-done.2
  19.4 0.0 copy-done.1
  19.4 0.0 copy-done
  19.5 0.8 shard_map.83
  20.3 9.6 %collective-permute-start.3 = (f32[5,32,128]{2,1,0:T(8,128)S(1)}, f32[5,32,128]{2,1,0:T(8,128)S(1)}, u32[]{:S(2)}, u32[]{:S(2)}) collective-permute-start(f32[5,32,128]{2,1,0:T(8,128)S(1)} %get-tuple-element.35), channel_id=1, source_target_pairs={{16,0},{32,16},{48,32},{64,48},{80,64},{96,80},{112,96},{0,112},{1... | collective-permute-start | bytes 245768 | tf_op jit(solution)/shard_map/ppermute | solution.py:545
  29.9 0.0 collective-permute-start.4
  29.9 0.1 all-to-all-done.refs_0_
  30.0 5.1 %shard_map.84 = (f32[2,8,256]{2,1,0:T(8,128)S(1)}, bf16[512,512]{1,0:T(8,128)(2,1)S(1)}, s32[4,32,256]{2,1,0:T(8,128)S(1)}, s32[4,32,256]{2,1,0:T(8,128)S(1)}, f32[4,32,256]{2,1,0:T(8,128)S(1)}) custom-call(f32[128,8,128]{2,1,0:T(8,128)S(1)} %all-to-all-done.refs_0_, f32[4,16,256]{2,1,0:T(8,128)S(1)} %copy-done.3, s32[4,16,256]{2,1,0:T(8,128)S(1)} %copy-done.4, ...), custom_call_target="tpu_custom_call" | custom-call | flops 4294967296 | bytes 2097152 | tf_op jit(solution)/shard_map/pallas_call | solution.py:487
  35.1 0.0 collective-permute-done.3.refs_8_.refs_4_
  35.1 0.2 collective-permute-done.4.refs_9_.refs_5_
  35.3 5.2 %shard_map.85 = (f32[2,16,32,384]{3,2,1,0:T(8,128)S(1)}, f32[64,256]{1,0:T(8,128)S(1)}, f32[16,32,384]{2,1,0:T(8,128)S(1)}, f32[16,32,384]{2,1,0:T(8,128)S(1)}, ...) custom-call(f32[2,16,16,256]{3,2,1,0:T(8,128)S(1)} %copy-done, f32[16,16,256]{2,1,0:T(8,128)S(1)} %copy-done.1, ...), custom_call_target="tpu_custom_call" | custom-call | flops 10000000 | bytes 16777216 | tf_op jit(solution)/shard_map/pallas_call | solution.py:487
  40.5 7.6 %collective-permute-start.5 = (f32[64,256]{1,0:T(8,128)S(1)}, f32[64,256]{1,0:T(8,128)S(1)}, u32[]{:S(2)}, u32[]{:S(2)}) collective-permute-start(f32[64,256]{1,0:T(8,128)S(1)} %get-tuple-element.51.refs_4_), channel_id=1, source_target_pairs={{15,127},{31,111},{47,95},{63,79},{79,63},{95,47},{111,31},{127,15}} | collective-permute-start | bytes 196616 | tf_op jit(solution)/shard_map/ppermute | solution.py:513
  48.1 2.5 %shard_map.86.refs_5_.refs_10_ = f32[2,4,256]{2,1,0:T(4,128)S(1)} custom-call(bf16[512,512]{1,0:T(8,128)(2,1)S(1)} %get-tuple-element.45.refs_0_, s32[4,32,256]{2,1,0:T(8,128)S(1)} %get-tuple-element.46.refs_1_, s32[4,32,256]{2,1,0:T(8,128)S(1)} %get-tuple-element.47.refs_2_, f32[4,32,256]{2,1,0:T(8,128)S(1)} %get-tuple-element.48.refs_3_, ...), custom_call_target="tpu_custom_call" | custom-call | flops 2147483648 | bytes 1048576 | tf_op jit(solution)/shard_map/pallas_call | solution.py:487
  50.6 0.7 collective-permute-start.6
  51.3 0.0 collective-permute-done.5.refs_4_.refs_5_
  51.3 2.5 %shard_map.87.refs_5_.refs_11_ = f32[2,4,256]{2,1,0:T(4,128)S(1)} custom-call(bf16[512,512]{1,0:T(8,128)(2,1)S(1)} %get-tuple-element.45.refs_0_, s32[4,32,256]{2,1,0:T(8,128)S(1)} %get-tuple-element.46.refs_1_, s32[4,32,256]{2,1,0:T(8,128)S(1)} %get-tuple-element.47.refs_2_, f32[4,32,256]{2,1,0:T(8,128)S(1)} %get-tuple-element.48.refs_3_, ...), custom_call_target="tpu_custom_call" | custom-call | flops 2147483648 | bytes 1048576 | tf_op jit(solution)/shard_map/pallas_call | solution.py:487
  53.8 4.2 %collective-permute-start.7 = (f32[64,256]{1,0:T(8,128)S(1)}, f32[64,256]{1,0:T(8,128)S(1)}, u32[]{:S(2)}, u32[]{:S(2)}) collective-permute-start(f32[64,256]{1,0:T(8,128)S(1)} %get-tuple-element.51.refs_4_), channel_id=1, source_target_pairs={{15,111},{31,95},{47,79},{63,63},{79,47},{95,31},{111,15},{127,127}} | collective-permute-start | bytes 196616 | tf_op jit(solution)/shard_map/ppermute | solution.py:513
  57.9 0.0 collective-permute-done.6.refs_4_.refs_6_
  57.9 2.5 %shard_map.88.refs_7_.refs_12_ = f32[2,4,256]{2,1,0:T(4,128)S(1)} custom-call(bf16[512,512]{1,0:T(8,128)(2,1)S(1)} %get-tuple-element.45.refs_0_, s32[4,32,256]{2,1,0:T(8,128)S(1)} %get-tuple-element.46.refs_1_, s32[4,32,256]{2,1,0:T(8,128)S(1)} %get-tuple-element.47.refs_2_, f32[4,32,256]{2,1,0:T(8,128)S(1)} %get-tuple-element.48.refs_3_, ...), custom_call_target="tpu_custom_call" | custom-call | flops 2147483648 | bytes 1048576 | tf_op jit(solution)/shard_map/pallas_call | solution.py:487
  60.4 1.9 %collective-permute-start.8 = (f32[64,256]{1,0:T(8,128)S(1)}, f32[64,256]{1,0:T(8,128)S(1)}, u32[]{:S(2)}, u32[]{:S(2)}) collective-permute-start(f32[64,256]{1,0:T(8,128)S(1)} %get-tuple-element.51.refs_4_), channel_id=1, source_target_pairs={{15,31},{31,15},{47,127},{63,111},{79,95},{95,79},{111,63},{127,47}} | collective-permute-start | bytes 196616 | tf_op jit(solution)/shard_map/ppermute | solution.py:513
  62.3 0.0 collective-permute-done.7.refs_6_.refs_7_
  62.3 3.0 %shard_map.89 = (f32[2,4,256]{2,1,0:T(4,128)S(1)}, f32[2,32,128]{2,1,0:T(8,128)S(1)}) custom-call(bf16[512,512]{1,0:T(8,128)(2,1)S(1)} %get-tuple-element.45.refs_0_, s32[4,32,256]{2,1,0:T(8,128)S(1)} %get-tuple-element.46.refs_1_, s32[4,32,256]{2,1,0:T(8,128)S(1)} %get-tuple-element.47.refs_2_, f32[4,32,256]{2,1,0:T(8,128)S(1)} %get-tuple-element.48.refs_3_, ...), custom_call_target="tpu_custom_call" | custom-call | flops 2147483648 | bytes 1048576 | tf_op jit(solution)/shard_map/pallas_call | solution.py:487
  65.3 0.1 collective-permute-done.8.refs_8_
  65.4 4.7 %shard_map.90 = (f32[2,16,32,384]{3,2,1,0:T(8,128)S(1)}, f32[64,256]{1,0:T(8,128)S(1)}, f32[2,32,384]{2,1,0:T(8,128)S(1)}) custom-call(f32[2,16,32,384]{3,2,1,0:T(8,128)S(1)} %get-tuple-element.39.refs_0_, f32[16,32,384]{2,1,0:T(8,128)S(1)} %get-tuple-element.40.refs_1_, f32[16,32,384]{2,1,0:T(8,128)S(1)} %get-tuple-element.41.refs_2_, ...), custom_call_target="tpu_custom_call" | custom-call | flops 10000000 | bytes 16777216 | tf_op jit(solution)/shard_map/pallas_call | solution.py:487
  70.1 3.3 %collective-permute-start.12 = (f32[64,256]{1,0:T(8,128)S(1)}, f32[64,256]{1,0:T(8,128)S(1)}, u32[]{:S(2)}, u32[]{:S(2)}) collective-permute-start(f32[64,256]{1,0:T(8,128)S(1)} %get-tuple-element.55), channel_id=1, source_target_pairs={{15,31},{31,15},{47,127},{63,111},{79,95},{95,79},{111,63},{127,47}} | collective-permute-start | bytes 196616 | tf_op jit(solution)/shard_map/ppermute | solution.py:513
  73.4 4.6 %collective-permute-start.11 = (f32[64,256]{1,0:T(8,128)S(1)}, f32[64,256]{1,0:T(8,128)S(1)}, u32[]{:S(2)}, u32[]{:S(2)}) collective-permute-start(f32[64,256]{1,0:T(8,128)S(1)} %get-tuple-element.55), channel_id=1, source_target_pairs={{15,111},{31,95},{47,79},{63,63},{79,47},{95,31},{111,15},{127,127}} | collective-permute-start | bytes 196616 | tf_op jit(solution)/shard_map/ppermute | solution.py:513
  78.0 0.7 collective-permute-start.10
  78.7 5.0 %collective-permute-start.9 = (f32[64,256]{1,0:T(8,128)S(1)}, f32[64,256]{1,0:T(8,128)S(1)}, u32[]{:S(2)}, u32[]{:S(2)}) collective-permute-start(f32[64,256]{1,0:T(8,128)S(1)} %get-tuple-element.55), channel_id=1, source_target_pairs={{15,127},{31,111},{47,95},{63,79},{79,63},{95,47},{111,31},{127,15}} | collective-permute-start | bytes 196616 | tf_op jit(solution)/shard_map/ppermute | solution.py:513
  83.6 0.0 collective-permute-done.12.refs_8_
  83.6 0.0 collective-permute-done.11.refs_7_
  83.7 0.0 collective-permute-done.10.refs_6_
  83.7 2.1 %collective-permute-done.9.refs_5_ = f32[64,256]{1,0:T(8,128)S(1)} collective-permute-done((f32[64,256]{1,0:T(8,128)S(1)}, f32[64,256]{1,0:T(8,128)S(1)}, u32[]{:S(2)}, u32[]{:S(2)}) %collective-permute-start.9) | collective-permute-done | bytes 65568 | tf_op jit(solution)/shard_map/ppermute | solution.py:513
  85.8 4.6 %shard_map.91 = f32[2,16,16,256]{3,2,1,0:T(8,128)} custom-call(f32[2,16,32,384]{3,2,1,0:T(8,128)S(1)} %get-tuple-element.54.refs_0_, f32[16,32,384]{2,1,0:T(8,128)S(1)} %get-tuple-element.40.refs_1_, f32[16,32,384]{2,1,0:T(8,128)S(1)} %get-tuple-element.41.refs_2_, f32[32,384]{1,0:T(8,128)S(1)} %get-tuple-element.42.refs_3_, ...), custom_call_target="tpu_custom_call" | custom-call | flops 10000000 | bytes 16777216 | tf_op jit(solution)/shard_map/pallas_call | solution.py:487
  (4 shorter events, 0.0 us)
Async XLA Ops:
  0.0 19.4 %copy-start.3 = (f32[4,16,256]{2,1,0:T(8,128)S(1)}, f32[4,16,256]{2,1,0:T(8,128)}, u32[]{:S(2)}) copy-start(f32[4,16,256]{2,1,0:T(8,128)} %refs_1_.6) | copy-start | bytes 196612
  0.0 19.4 %copy-start.4 = (s32[4,16,256]{2,1,0:T(8,128)S(1)}, s32[4,16,256]{2,1,0:T(8,128)}, u32[]{:S(2)}) copy-start(s32[4,16,256]{2,1,0:T(8,128)} %refs_2_.6) | copy-start | bytes 196612
  0.0 19.4 %copy-start.5 = (s32[16,256]{1,0:T(8,128)S(1)}, s32[16,256]{1,0:T(8,128)}, u32[]{:S(2)}) copy-start(s32[16,256]{1,0:T(8,128)} %refs_3_.5) | copy-start | bytes 49156
  0.0 19.4 %copy-start.2 = (f32[16,16,256]{2,1,0:T(8,128)S(1)}, f32[16,16,256]{2,1,0:T(8,128)}, u32[]{:S(2)}) copy-start(f32[16,16,256]{2,1,0:T(8,128)} %refs_2_.7) | copy-start | bytes 786436
  0.0 19.4 %copy-start.1 = (f32[16,16,256]{2,1,0:T(8,128)S(1)}, f32[16,16,256]{2,1,0:T(8,128)}, u32[]{:S(2)}) copy-start(f32[16,16,256]{2,1,0:T(8,128)} %refs_1_.7) | copy-start | bytes 786436
  0.0 19.4 %copy-start = (f32[2,16,16,256]{3,2,1,0:T(8,128)S(1)}, f32[2,16,16,256]{3,2,1,0:T(8,128)}, u32[]{:S(2)}) copy-start(f32[2,16,16,256]{3,2,1,0:T(8,128)} %refs_0_.5) | copy-start | bytes 1572868
  0.0 19.4 %copy-start.6 = (s32[256]{0:T(256)S(1)}, s32[256]{0:T(256)}, u32[]{:S(2)}) copy-start(s32[256]{0:T(256)} %param.12) | copy-start | bytes 3076
  3.0 14.7 %collective-permute-start = (f32[64,8,256]{2,1,0:T(8,128)}, f32[64,8,256]{2,1,0:T(8,128)S(1)}, u32[]{:S(2)}, u32[]{:S(2)}) collective-permute-start(f32[64,8,256]{2,1,0:T(8,128)} %get-tuple-element.31), channel_id=1, source_target_pairs={{0,1},{2,3},{4,5},{6,7},{8,9},{10,11},{12,13},{14,15},{1,0},{3,2},... | collective-permute-start | bytes 1572872 | tf_op jit(solution)/shard_map/ppermute | solution.py:530
  3.8 15.6 %collective-permute-start.1 = (f32[64,8,256]{2,1,0:T(8,128)}, f32[64,8,256]{2,1,0:T(8,128)S(1)}, u32[]{:S(2)}, u32[]{:S(2)}) collective-permute-start(f32[64,8,256]{2,1,0:T(8,128)} %get-tuple-element.32), channel_id=1, source_target_pairs={{1,2},{3,4},{5,6},{7,8},{9,10},{11,12},{13,14},{2,1},{4,3},{6,5},{... | collective-permute-start | bytes 1572872 | tf_op jit(solution)/shard_map/ppermute | solution.py:534
  8.0 22.0 %all-to-all-start = ((f32[128,8,128]{2,1,0:T(8,128)}), f32[128,8,128]{2,1,0:T(8,128)S(1)}, u32[]{:S(2)}, u32[]{:S(2)}) async-start(f32[128,8,128]{2,1,0:T(8,128)} %get-tuple-element.37), calls=%async_computation | async-start | bytes 1048576 | tf_op jit(solution)/shard_map/all_to_all | solution.py:537
  16.1 1.5 %collective-permute-start.2 = (f32[10,8,256]{2,1,0:T(8,128)}, f32[10,8,256]{2,1,0:T(8,128)S(1)}, u32[]{:S(2)}, u32[]{:S(2)}) collective-permute-start(f32[10,8,256]{2,1,0:T(8,128)} %get-tuple-element.33), channel_id=1, source_target_pairs={{15,15},{31,127},{47,111},{63,95},{79,79},{95,63},{111,47},{127,31}} | collective-permute-start | bytes 245768 | tf_op jit(solution)/shard_map/ppermute | solution.py:513
  20.3 14.8 %collective-permute-start.3 = (f32[5,32,128]{2,1,0:T(8,128)S(1)}, f32[5,32,128]{2,1,0:T(8,128)S(1)}, u32[]{:S(2)}, u32[]{:S(2)}) collective-permute-start(f32[5,32,128]{2,1,0:T(8,128)S(1)} %get-tuple-element.35), channel_id=1, source_target_pairs={{16,0},{32,16},{48,32},{64,48},{80,64},{96,80},{112,96},{0,112},{1... | collective-permute-start | bytes 245768 | tf_op jit(solution)/shard_map/ppermute | solution.py:545
  29.9 5.4 %collective-permute-start.4 = (f32[5,32,128]{2,1,0:T(8,128)S(1)}, f32[5,32,128]{2,1,0:T(8,128)S(1)}, u32[]{:S(2)}, u32[]{:S(2)}) collective-permute-start(f32[5,32,128]{2,1,0:T(8,128)S(1)} %get-tuple-element.36), channel_id=1, source_target_pairs={{0,16},{16,32},{32,48},{48,64},{64,80},{80,96},{96,112},{112,0},{1... | collective-permute-start | bytes 245768 | tf_op jit(solution)/shard_map/ppermute | solution.py:546
  40.5 10.7 %collective-permute-start.5 = (f32[64,256]{1,0:T(8,128)S(1)}, f32[64,256]{1,0:T(8,128)S(1)}, u32[]{:S(2)}, u32[]{:S(2)}) collective-permute-start(f32[64,256]{1,0:T(8,128)S(1)} %get-tuple-element.51.refs_4_), channel_id=1, source_target_pairs={{15,127},{31,111},{47,95},{63,79},{79,63},{95,47},{111,31},{127,15}} | collective-permute-start | bytes 196616 | tf_op jit(solution)/shard_map/ppermute | solution.py:513
  50.6 7.3 %collective-permute-start.6 = (f32[64,256]{1,0:T(8,128)S(1)}, f32[64,256]{1,0:T(8,128)S(1)}, u32[]{:S(2)}, u32[]{:S(2)}) collective-permute-start(f32[64,256]{1,0:T(8,128)S(1)} %get-tuple-element.51.refs_4_), channel_id=1, source_target_pairs={{15,15},{31,127},{47,111},{63,95},{79,79},{95,63},{111,47},{127,31}} | collective-permute-start | bytes 196616 | tf_op jit(solution)/shard_map/ppermute | solution.py:513
  53.8 8.6 %collective-permute-start.7 = (f32[64,256]{1,0:T(8,128)S(1)}, f32[64,256]{1,0:T(8,128)S(1)}, u32[]{:S(2)}, u32[]{:S(2)}) collective-permute-start(f32[64,256]{1,0:T(8,128)S(1)} %get-tuple-element.51.refs_4_), channel_id=1, source_target_pairs={{15,111},{31,95},{47,79},{63,63},{79,47},{95,31},{111,15},{127,127}} | collective-permute-start | bytes 196616 | tf_op jit(solution)/shard_map/ppermute | solution.py:513
  60.4 5.0 %collective-permute-start.8 = (f32[64,256]{1,0:T(8,128)S(1)}, f32[64,256]{1,0:T(8,128)S(1)}, u32[]{:S(2)}, u32[]{:S(2)}) collective-permute-start(f32[64,256]{1,0:T(8,128)S(1)} %get-tuple-element.51.refs_4_), channel_id=1, source_target_pairs={{15,31},{31,15},{47,127},{63,111},{79,95},{95,79},{111,63},{127,47}} | collective-permute-start | bytes 196616 | tf_op jit(solution)/shard_map/ppermute | solution.py:513
  70.1 13.5 %collective-permute-start.12 = (f32[64,256]{1,0:T(8,128)S(1)}, f32[64,256]{1,0:T(8,128)S(1)}, u32[]{:S(2)}, u32[]{:S(2)}) collective-permute-start(f32[64,256]{1,0:T(8,128)S(1)} %get-tuple-element.55), channel_id=1, source_target_pairs={{15,31},{31,15},{47,127},{63,111},{79,95},{95,79},{111,63},{127,47}} | collective-permute-start | bytes 196616 | tf_op jit(solution)/shard_map/ppermute | solution.py:513
  73.4 10.3 %collective-permute-start.11 = (f32[64,256]{1,0:T(8,128)S(1)}, f32[64,256]{1,0:T(8,128)S(1)}, u32[]{:S(2)}, u32[]{:S(2)}) collective-permute-start(f32[64,256]{1,0:T(8,128)S(1)} %get-tuple-element.55), channel_id=1, source_target_pairs={{15,111},{31,95},{47,79},{63,63},{79,47},{95,31},{111,15},{127,127}} | collective-permute-start | bytes 196616 | tf_op jit(solution)/shard_map/ppermute | solution.py:513
  78.0 5.7 %collective-permute-start.10 = (f32[64,256]{1,0:T(8,128)S(1)}, f32[64,256]{1,0:T(8,128)S(1)}, u32[]{:S(2)}, u32[]{:S(2)}) collective-permute-start(f32[64,256]{1,0:T(8,128)S(1)} %get-tuple-element.55), channel_id=1, source_target_pairs={{15,15},{31,127},{47,111},{63,95},{79,79},{95,63},{111,47},{127,31}} | collective-permute-start | bytes 196616 | tf_op jit(solution)/shard_map/ppermute | solution.py:513
  78.7 7.1 %collective-permute-start.9 = (f32[64,256]{1,0:T(8,128)S(1)}, f32[64,256]{1,0:T(8,128)S(1)}, u32[]{:S(2)}, u32[]{:S(2)}) collective-permute-start(f32[64,256]{1,0:T(8,128)S(1)} %get-tuple-element.55), channel_id=1, source_target_pairs={{15,127},{31,111},{47,95},{63,79},{79,63},{95,47},{111,31},{127,15}} | collective-permute-start | bytes 196616 | tf_op jit(solution)/shard_map/ppermute | solution.py:513

commit v6 on v5

--- a/solution.py
+++ b/solution.py
@@ -370,7 +370,7 @@
                 cells[tracer, k, row + r : row + r + 1, 0:columns] = ghosts[pl.ds(32 * r + 16 * tracer + k, 1), :]
         return carry
 
-    lax.fori_loop(0, 16, place, 0)
+    lax.fori_loop(0, 16, place, 0, unroll=4)
 
 
 def first_kernel(
@@ -396,7 +396,7 @@
         north_ext[k, :, 256:384] = 0.5 * halo(3, k)
         return carry
 
-    lax.fori_loop(0, 16, fill, 0)
+    lax.fori_loop(0, 16, fill, 0, unroll=4)
 
     @pl.when(is_top)
     def _():
@@ -420,7 +420,7 @@
             ghosts[rows, cut] = pick_columns(partner_ext[:, cut], sources)
         return carry
 
-    lax.fori_loop(0, 8, block_body, 0)
+    lax.fori_loop(0, 8, block_body, 0, unroll=4)
 
 
 def second_kernel(
@@ -432,7 +432,7 @@
             start[tracer, k] = cells[tracer, k]
         return carry
 
-    lax.fori_loop(0, 16, fill, 0)
+    lax.fori_loop(0, 16, fill, 0, unroll=4)
 
     @pl.when(info[1] == 1)
     def _():
@@ -458,7 +458,7 @@
             start[tracer, k] = cells[tracer, k]
         return carry
 
-    lax.fori_loop(0, 16, fill, 0)
+    lax.fori_loop(0, 16, fill, 0, unroll=4)
 
     @pl.when(info[1] == 1)
     def _():

time: 91.6 us -> 89.7 us (0.979)
  Pallas kernels: 33.8 us -> 32 us
    pallas_call x10, Pallas kernels: 33.8 us -> 32 us  [call(): pl.pallas_call(body, out_shape=tuple((jax.ShapeDtypeStruct(s, d) for s, d...]
where the time goes in v6:
time: 89.7 us; the launch traced here: 88.6 us
  starting transfers between devices  52.1 us (58%)
  Pallas kernels  32 us (36%)
  waiting for transfers between devices  4.23 us (5%)
    pallas_call x10, Pallas kernels, call(): pl.pallas_call(body, out_shape=tuple((jax.ShapeDtypeStruct(s, d) for s, d...  32 us
    ppermute x9, starting transfers between devices, fold_permute(): return lax.ppermute(rows, both, pairs)  29.4 us
    ppermute x1, starting transfers between devices, per_device(): lax.ppermute(to_west, 'lon', [((i + 1) % nlon, i) for i in range(nlon)])  9.62 us
    all_to_all x1, starting transfers between devices, per_device(): table = lax.all_to_all(slots, both, 0, 0, tiled=True)  8.13 us
    ppermute x1, starting transfers between devices, per_device(): second = lax.ppermute(second, both, swaps + facing)  4.21 us
    ppermute x9, waiting for transfers between devices, fold_permute(): return lax.ppermute(rows, both, pairs)  2.25 us
  transfers between devices with their start and end apart: 14, of which 5 were waited for; matrix products, arithmetic and copies ran while one was open for 0% of the time, Pallas kernels for 18%

profile of v6, /device:TPU:121, one launch (start us, length us, event | category | flops | bytes accessed | tf_op | source)
XLA Modules:
  0.0 88.6 jit_solution(1130254141279085764)
XLA Ops:
  0.0 0.0 copy-start.2
  0.0 0.0 copy-start.1
  0.0 0.0 copy-start
  0.0 0.0 copy-start.6
  0.0 3.0 %shard_map.82 = (f32[64,8,256]{2,1,0:T(8,128)}, f32[64,8,256]{2,1,0:T(8,128)}, f32[10,8,256]{2,1,0:T(8,128)}, f32[128,8,128]{2,1,0:T(8,128)}) custom-call(f32[2,16,16,256]{3,2,1,0:T(8,128)} %refs_0_.5, f32[16,16,256]{2,1,0:T(8,128)} %refs_1_.7, f32[16,16,256]{2,1,0:T(8,128)} %refs_2_.7, s32[16,256]{1,0:T(8,128)} %refs_3_.5, f32[4,16,256]{2,1,0:T(8,128)} %refs_1_.6, ...), custom_call_target="tpu_custom_call" | custom-call | tf_op jit(solution)/shard_map/pallas_call | solution.py:487
  3.0 0.7 collective-permute-start
  3.8 4.2 %collective-permute-start.1 = (f32[64,8,256]{2,1,0:T(8,128)}, f32[64,8,256]{2,1,0:T(8,128)S(1)}, u32[]{:S(2)}, u32[]{:S(2)}) collective-permute-start(f32[64,8,256]{2,1,0:T(8,128)} %get-tuple-element.32), channel_id=1, source_target_pairs={{1,2},{3,4},{5,6},{7,8},{9,10},{11,12},{13,14},{2,1},{4,3},{6,5},{... | collective-permute-start | bytes 1572872 | tf_op jit(solution)/shard_map/ppermute | solution.py:534
  8.0 8.1 %all-to-all-start = ((f32[128,8,128]{2,1,0:T(8,128)}), f32[128,8,128]{2,1,0:T(8,128)S(1)}, u32[]{:S(2)}, u32[]{:S(2)}) async-start(f32[128,8,128]{2,1,0:T(8,128)} %get-tuple-element.37), calls=%async_computation | async-start | bytes 1048576 | tf_op jit(solution)/shard_map/all_to_all | solution.py:537
  16.1 1.5 %collective-permute-start.2 = (f32[10,8,256]{2,1,0:T(8,128)}, f32[10,8,256]{2,1,0:T(8,128)S(1)}, u32[]{:S(2)}, u32[]{:S(2)}) collective-permute-start(f32[10,8,256]{2,1,0:T(8,128)} %get-tuple-element.33), channel_id=1, source_target_pairs={{15,15},{31,127},{47,111},{63,95},{79,79},{95,63},{111,47},{127,31}} | collective-permute-start | bytes 245768 | tf_op jit(solution)/shard_map/ppermute | solution.py:513
  17.7 0.0 collective-permute-done.2.refs_9_
  17.7 0.0 collective-permute-done.refs_7_.refs_3_.refs_5_
  17.7 1.7 %collective-permute-done.1.refs_8_.refs_4_.refs_6_ = f32[64,8,256]{2,1,0:T(8,128)S(1)} collective-permute-done((f32[64,8,256]{2,1,0:T(8,128)}, f32[64,8,256]{2,1,0:T(8,128)S(1)}, u32[]{:S(2)}, u32[]{:S(2)}) %collective-permute-start.1) | collective-permute-done | bytes 524320 | tf_op jit(solution)/shard_map/ppermute | solution.py:534
  19.4 0.0 copy-done.3
  19.4 0.0 copy-done.4
  19.4 0.0 copy-done.5
  19.4 0.0 copy-done.2
  19.4 0.0 copy-done.1
  19.4 0.0 copy-done
  19.5 0.8 shard_map.83
  20.3 9.6 %collective-permute-start.3 = (f32[5,32,128]{2,1,0:T(8,128)S(1)}, f32[5,32,128]{2,1,0:T(8,128)S(1)}, u32[]{:S(2)}, u32[]{:S(2)}) collective-permute-start(f32[5,32,128]{2,1,0:T(8,128)S(1)} %get-tuple-element.35), channel_id=1, source_target_pairs={{16,0},{32,16},{48,32},{64,48},{80,64},{96,80},{112,96},{0,112},{1... | collective-permute-start | bytes 245768 | tf_op jit(solution)/shard_map/ppermute | solution.py:545
  29.9 0.0 collective-permute-start.4
  29.9 0.1 all-to-all-done.refs_0_
  30.0 5.1 %shard_map.84 = (f32[2,8,256]{2,1,0:T(8,128)S(1)}, bf16[512,512]{1,0:T(8,128)(2,1)S(1)}, s32[4,32,256]{2,1,0:T(8,128)S(1)}, s32[4,32,256]{2,1,0:T(8,128)S(1)}, f32[4,32,256]{2,1,0:T(8,128)S(1)}) custom-call(f32[128,8,128]{2,1,0:T(8,128)S(1)} %all-to-all-done.refs_0_, f32[4,16,256]{2,1,0:T(8,128)S(1)} %copy-done.3, s32[4,16,256]{2,1,0:T(8,128)S(1)} %copy-done.4, ...), custom_call_target="tpu_custom_call" | custom-call | flops 4294967296 | bytes 2097152 | tf_op jit(solution)/shard_map/pallas_call | solution.py:487
  35.1 0.0 collective-permute-done.3.refs_8_.refs_4_
  35.1 0.2 collective-permute-done.4.refs_9_.refs_5_
  35.3 4.5 %shard_map.85 = (f32[2,16,32,384]{3,2,1,0:T(8,128)S(1)}, f32[64,256]{1,0:T(8,128)S(1)}, f32[16,32,384]{2,1,0:T(8,128)S(1)}, f32[16,32,384]{2,1,0:T(8,128)S(1)}, ...) custom-call(f32[2,16,16,256]{3,2,1,0:T(8,128)S(1)} %copy-done, f32[16,16,256]{2,1,0:T(8,128)S(1)} %copy-done.1, ...), custom_call_target="tpu_custom_call" | custom-call | flops 10000000 | bytes 16777216 | tf_op jit(solution)/shard_map/pallas_call | solution.py:487
  39.8 7.6 %collective-permute-start.5 = (f32[64,256]{1,0:T(8,128)S(1)}, f32[64,256]{1,0:T(8,128)S(1)}, u32[]{:S(2)}, u32[]{:S(2)}) collective-permute-start(f32[64,256]{1,0:T(8,128)S(1)} %get-tuple-element.51.refs_4_), channel_id=1, source_target_pairs={{15,127},{31,111},{47,95},{63,79},{79,63},{95,47},{111,31},{127,15}} | collective-permute-start | bytes 196616 | tf_op jit(solution)/shard_map/ppermute | solution.py:513
  47.4 2.5 %shard_map.86.refs_5_.refs_10_ = f32[2,4,256]{2,1,0:T(4,128)S(1)} custom-call(bf16[512,512]{1,0:T(8,128)(2,1)S(1)} %get-tuple-element.45.refs_0_, s32[4,32,256]{2,1,0:T(8,128)S(1)} %get-tuple-element.46.refs_1_, s32[4,32,256]{2,1,0:T(8,128)S(1)} %get-tuple-element.47.refs_2_, f32[4,32,256]{2,1,0:T(8,128)S(1)} %get-tuple-element.48.refs_3_, ...), custom_call_target="tpu_custom_call" | custom-call | flops 2147483648 | bytes 1048576 | tf_op jit(solution)/shard_map/pallas_call | solution.py:487
  49.9 0.7 collective-permute-start.6
  50.5 0.0 collective-permute-done.5.refs_4_.refs_5_
  50.5 2.5 %shard_map.87.refs_5_.refs_11_ = f32[2,4,256]{2,1,0:T(4,128)S(1)} custom-call(bf16[512,512]{1,0:T(8,128)(2,1)S(1)} %get-tuple-element.45.refs_0_, s32[4,32,256]{2,1,0:T(8,128)S(1)} %get-tuple-element.46.refs_1_, s32[4,32,256]{2,1,0:T(8,128)S(1)} %get-tuple-element.47.refs_2_, f32[4,32,256]{2,1,0:T(8,128)S(1)} %get-tuple-element.48.refs_3_, ...), custom_call_target="tpu_custom_call" | custom-call | flops 2147483648 | bytes 1048576 | tf_op jit(solution)/shard_map/pallas_call | solution.py:487
  53.0 4.1 %collective-permute-start.7 = (f32[64,256]{1,0:T(8,128)S(1)}, f32[64,256]{1,0:T(8,128)S(1)}, u32[]{:S(2)}, u32[]{:S(2)}) collective-permute-start(f32[64,256]{1,0:T(8,128)S(1)} %get-tuple-element.51.refs_4_), channel_id=1, source_target_pairs={{15,111},{31,95},{47,79},{63,63},{79,47},{95,31},{111,15},{127,127}} | collective-permute-start | bytes 196616 | tf_op jit(solution)/shard_map/ppermute | solution.py:513
  57.2 0.0 collective-permute-done.6.refs_4_.refs_6_
  57.2 2.5 %shard_map.88.refs_7_.refs_12_ = f32[2,4,256]{2,1,0:T(4,128)S(1)} custom-call(bf16[512,512]{1,0:T(8,128)(2,1)S(1)} %get-tuple-element.45.refs_0_, s32[4,32,256]{2,1,0:T(8,128)S(1)} %get-tuple-element.46.refs_1_, s32[4,32,256]{2,1,0:T(8,128)S(1)} %get-tuple-element.47.refs_2_, f32[4,32,256]{2,1,0:T(8,128)S(1)} %get-tuple-element.48.refs_3_, ...), custom_call_target="tpu_custom_call" | custom-call | flops 2147483648 | bytes 1048576 | tf_op jit(solution)/shard_map/pallas_call | solution.py:487
  59.7 1.9 %collective-permute-start.8 = (f32[64,256]{1,0:T(8,128)S(1)}, f32[64,256]{1,0:T(8,128)S(1)}, u32[]{:S(2)}, u32[]{:S(2)}) collective-permute-start(f32[64,256]{1,0:T(8,128)S(1)} %get-tuple-element.51.refs_4_), channel_id=1, source_target_pairs={{15,31},{31,15},{47,127},{63,111},{79,95},{95,79},{111,63},{127,47}} | collective-permute-start | bytes 196616 | tf_op jit(solution)/shard_map/ppermute | solution.py:513
  61.6 0.0 collective-permute-done.7.refs_6_.refs_7_
  61.6 3.0 %shard_map.89 = (f32[2,4,256]{2,1,0:T(4,128)S(1)}, f32[2,32,128]{2,1,0:T(8,128)S(1)}) custom-call(bf16[512,512]{1,0:T(8,128)(2,1)S(1)} %get-tuple-element.45.refs_0_, s32[4,32,256]{2,1,0:T(8,128)S(1)} %get-tuple-element.46.refs_1_, s32[4,32,256]{2,1,0:T(8,128)S(1)} %get-tuple-element.47.refs_2_, f32[4,32,256]{2,1,0:T(8,128)S(1)} %get-tuple-element.48.refs_3_, ...), custom_call_target="tpu_custom_call" | custom-call | flops 2147483648 | bytes 1048576 | tf_op jit(solution)/shard_map/pallas_call | solution.py:487
  64.5 0.1 collective-permute-done.8.refs_8_
  64.7 4.1 %shard_map.90 = (f32[2,16,32,384]{3,2,1,0:T(8,128)S(1)}, f32[64,256]{1,0:T(8,128)S(1)}, f32[2,32,384]{2,1,0:T(8,128)S(1)}) custom-call(f32[2,16,32,384]{3,2,1,0:T(8,128)S(1)} %get-tuple-element.39.refs_0_, f32[16,32,384]{2,1,0:T(8,128)S(1)} %get-tuple-element.40.refs_1_, f32[16,32,384]{2,1,0:T(8,128)S(1)} %get-tuple-element.41.refs_2_, ...), custom_call_target="tpu_custom_call" | custom-call | flops 10000000 | bytes 16777216 | tf_op jit(solution)/shard_map/pallas_call | solution.py:487
  68.8 3.3 %collective-permute-start.12 = (f32[64,256]{1,0:T(8,128)S(1)}, f32[64,256]{1,0:T(8,128)S(1)}, u32[]{:S(2)}, u32[]{:S(2)}) collective-permute-start(f32[64,256]{1,0:T(8,128)S(1)} %get-tuple-element.55), channel_id=1, source_target_pairs={{15,31},{31,15},{47,127},{63,111},{79,95},{95,79},{111,63},{127,47}} | collective-permute-start | bytes 196616 | tf_op jit(solution)/shard_map/ppermute | solution.py:513
  72.1 4.6 %collective-permute-start.11 = (f32[64,256]{1,0:T(8,128)S(1)}, f32[64,256]{1,0:T(8,128)S(1)}, u32[]{:S(2)}, u32[]{:S(2)}) collective-permute-start(f32[64,256]{1,0:T(8,128)S(1)} %get-tuple-element.55), channel_id=1, source_target_pairs={{15,111},{31,95},{47,79},{63,63},{79,47},{95,31},{111,15},{127,127}} | collective-permute-start | bytes 196616 | tf_op jit(solution)/shard_map/ppermute | solution.py:513
  76.7 0.7 collective-permute-start.10
  77.4 5.0 %collective-permute-start.9 = (f32[64,256]{1,0:T(8,128)S(1)}, f32[64,256]{1,0:T(8,128)S(1)}, u32[]{:S(2)}, u32[]{:S(2)}) collective-permute-start(f32[64,256]{1,0:T(8,128)S(1)} %get-tuple-element.55), channel_id=1, source_target_pairs={{15,127},{31,111},{47,95},{63,79},{79,63},{95,47},{111,31},{127,15}} | collective-permute-start | bytes 196616 | tf_op jit(solution)/shard_map/ppermute | solution.py:513
  82.3 0.0 collective-permute-done.12.refs_8_
  82.4 0.0 collective-permute-done.11.refs_7_
  82.4 0.0 collective-permute-done.10.refs_6_
  82.4 2.1 %collective-permute-done.9.refs_5_ = f32[64,256]{1,0:T(8,128)S(1)} collective-permute-done((f32[64,256]{1,0:T(8,128)S(1)}, f32[64,256]{1,0:T(8,128)S(1)}, u32[]{:S(2)}, u32[]{:S(2)}) %collective-permute-start.9) | collective-permute-done | bytes 65568 | tf_op jit(solution)/shard_map/ppermute | solution.py:513
  84.5 4.1 %shard_map.91 = f32[2,16,16,256]{3,2,1,0:T(8,128)} custom-call(f32[2,16,32,384]{3,2,1,0:T(8,128)S(1)} %get-tuple-element.54.refs_0_, f32[16,32,384]{2,1,0:T(8,128)S(1)} %get-tuple-element.40.refs_1_, f32[16,32,384]{2,1,0:T(8,128)S(1)} %get-tuple-element.41.refs_2_, f32[32,384]{1,0:T(8,128)S(1)} %get-tuple-element.42.refs_3_, ...), custom_call_target="tpu_custom_call" | custom-call | flops 10000000 | bytes 16777216 | tf_op jit(solution)/shard_map/pallas_call | solution.py:487
  (4 shorter events, 0.0 us)
Async XLA Ops:
  0.0 19.4 %copy-start.3 = (f32[4,16,256]{2,1,0:T(8,128)S(1)}, f32[4,16,256]{2,1,0:T(8,128)}, u32[]{:S(2)}) copy-start(f32[4,16,256]{2,1,0:T(8,128)} %refs_1_.6) | copy-start | bytes 196612
  0.0 19.4 %copy-start.4 = (s32[4,16,256]{2,1,0:T(8,128)S(1)}, s32[4,16,256]{2,1,0:T(8,128)}, u32[]{:S(2)}) copy-start(s32[4,16,256]{2,1,0:T(8,128)} %refs_2_.6) | copy-start | bytes 196612
  0.0 19.4 %copy-start.5 = (s32[16,256]{1,0:T(8,128)S(1)}, s32[16,256]{1,0:T(8,128)}, u32[]{:S(2)}) copy-start(s32[16,256]{1,0:T(8,128)} %refs_3_.5) | copy-start | bytes 49156
  0.0 19.4 %copy-start.2 = (f32[16,16,256]{2,1,0:T(8,128)S(1)}, f32[16,16,256]{2,1,0:T(8,128)}, u32[]{:S(2)}) copy-start(f32[16,16,256]{2,1,0:T(8,128)} %refs_2_.7) | copy-start | bytes 786436
  0.0 19.4 %copy-start.1 = (f32[16,16,256]{2,1,0:T(8,128)S(1)}, f32[16,16,256]{2,1,0:T(8,128)}, u32[]{:S(2)}) copy-start(f32[16,16,256]{2,1,0:T(8,128)} %refs_1_.7) | copy-start | bytes 786436
  0.0 19.4 %copy-start = (f32[2,16,16,256]{3,2,1,0:T(8,128)S(1)}, f32[2,16,16,256]{3,2,1,0:T(8,128)}, u32[]{:S(2)}) copy-start(f32[2,16,16,256]{3,2,1,0:T(8,128)} %refs_0_.5) | copy-start | bytes 1572868
  0.0 19.4 %copy-start.6 = (s32[256]{0:T(256)S(1)}, s32[256]{0:T(256)}, u32[]{:S(2)}) copy-start(s32[256]{0:T(256)} %param.12) | copy-start | bytes 3076
  3.0 14.7 %collective-permute-start = (f32[64,8,256]{2,1,0:T(8,128)}, f32[64,8,256]{2,1,0:T(8,128)S(1)}, u32[]{:S(2)}, u32[]{:S(2)}) collective-permute-start(f32[64,8,256]{2,1,0:T(8,128)} %get-tuple-element.31), channel_id=1, source_target_pairs={{0,1},{2,3},{4,5},{6,7},{8,9},{10,11},{12,13},{14,15},{1,0},{3,2},... | collective-permute-start | bytes 1572872 | tf_op jit(solution)/shard_map/ppermute | solution.py:530
  3.8 15.6 %collective-permute-start.1 = (f32[64,8,256]{2,1,0:T(8,128)}, f32[64,8,256]{2,1,0:T(8,128)S(1)}, u32[]{:S(2)}, u32[]{:S(2)}) collective-permute-start(f32[64,8,256]{2,1,0:T(8,128)} %get-tuple-element.32), channel_id=1, source_target_pairs={{1,2},{3,4},{5,6},{7,8},{9,10},{11,12},{13,14},{2,1},{4,3},{6,5},{... | collective-permute-start | bytes 1572872 | tf_op jit(solution)/shard_map/ppermute | solution.py:534
  8.0 22.0 %all-to-all-start = ((f32[128,8,128]{2,1,0:T(8,128)}), f32[128,8,128]{2,1,0:T(8,128)S(1)}, u32[]{:S(2)}, u32[]{:S(2)}) async-start(f32[128,8,128]{2,1,0:T(8,128)} %get-tuple-element.37), calls=%async_computation | async-start | bytes 1048576 | tf_op jit(solution)/shard_map/all_to_all | solution.py:537
  16.1 1.5 %collective-permute-start.2 = (f32[10,8,256]{2,1,0:T(8,128)}, f32[10,8,256]{2,1,0:T(8,128)S(1)}, u32[]{:S(2)}, u32[]{:S(2)}) collective-permute-start(f32[10,8,256]{2,1,0:T(8,128)} %get-tuple-element.33), channel_id=1, source_target_pairs={{15,15},{31,127},{47,111},{63,95},{79,79},{95,63},{111,47},{127,31}} | collective-permute-start | bytes 245768 | tf_op jit(solution)/shard_map/ppermute | solution.py:513
  20.3 14.8 %collective-permute-start.3 = (f32[5,32,128]{2,1,0:T(8,128)S(1)}, f32[5,32,128]{2,1,0:T(8,128)S(1)}, u32[]{:S(2)}, u32[]{:S(2)}) collective-permute-start(f32[5,32,128]{2,1,0:T(8,128)S(1)} %get-tuple-element.35), channel_id=1, source_target_pairs={{16,0},{32,16},{48,32},{64,48},{80,64},{96,80},{112,96},{0,112},{1... | collective-permute-start | bytes 245768 | tf_op jit(solution)/shard_map/ppermute | solution.py:545
  29.9 5.4 %collective-permute-start.4 = (f32[5,32,128]{2,1,0:T(8,128)S(1)}, f32[5,32,128]{2,1,0:T(8,128)S(1)}, u32[]{:S(2)}, u32[]{:S(2)}) collective-permute-start(f32[5,32,128]{2,1,0:T(8,128)S(1)} %get-tuple-element.36), channel_id=1, source_target_pairs={{0,16},{16,32},{32,48},{48,64},{64,80},{80,96},{96,112},{112,0},{1... | collective-permute-start | bytes 245768 | tf_op jit(solution)/shard_map/ppermute | solution.py:546
  39.8 10.7 %collective-permute-start.5 = (f32[64,256]{1,0:T(8,128)S(1)}, f32[64,256]{1,0:T(8,128)S(1)}, u32[]{:S(2)}, u32[]{:S(2)}) collective-permute-start(f32[64,256]{1,0:T(8,128)S(1)} %get-tuple-element.51.refs_4_), channel_id=1, source_target_pairs={{15,127},{31,111},{47,95},{63,79},{79,63},{95,47},{111,31},{127,15}} | collective-permute-start | bytes 196616 | tf_op jit(solution)/shard_map/ppermute | solution.py:513
  49.9 7.3 %collective-permute-start.6 = (f32[64,256]{1,0:T(8,128)S(1)}, f32[64,256]{1,0:T(8,128)S(1)}, u32[]{:S(2)}, u32[]{:S(2)}) collective-permute-start(f32[64,256]{1,0:T(8,128)S(1)} %get-tuple-element.51.refs_4_), channel_id=1, source_target_pairs={{15,15},{31,127},{47,111},{63,95},{79,79},{95,63},{111,47},{127,31}} | collective-permute-start | bytes 196616 | tf_op jit(solution)/shard_map/ppermute | solution.py:513
  53.0 8.6 %collective-permute-start.7 = (f32[64,256]{1,0:T(8,128)S(1)}, f32[64,256]{1,0:T(8,128)S(1)}, u32[]{:S(2)}, u32[]{:S(2)}) collective-permute-start(f32[64,256]{1,0:T(8,128)S(1)} %get-tuple-element.51.refs_4_), channel_id=1, source_target_pairs={{15,111},{31,95},{47,79},{63,63},{79,47},{95,31},{111,15},{127,127}} | collective-permute-start | bytes 196616 | tf_op jit(solution)/shard_map/ppermute | solution.py:513
  59.7 5.0 %collective-permute-start.8 = (f32[64,256]{1,0:T(8,128)S(1)}, f32[64,256]{1,0:T(8,128)S(1)}, u32[]{:S(2)}, u32[]{:S(2)}) collective-permute-start(f32[64,256]{1,0:T(8,128)S(1)} %get-tuple-element.51.refs_4_), channel_id=1, source_target_pairs={{15,31},{31,15},{47,127},{63,111},{79,95},{95,79},{111,63},{127,47}} | collective-permute-start | bytes 196616 | tf_op jit(solution)/shard_map/ppermute | solution.py:513
  68.8 13.5 %collective-permute-start.12 = (f32[64,256]{1,0:T(8,128)S(1)}, f32[64,256]{1,0:T(8,128)S(1)}, u32[]{:S(2)}, u32[]{:S(2)}) collective-permute-start(f32[64,256]{1,0:T(8,128)S(1)} %get-tuple-element.55), channel_id=1, source_target_pairs={{15,31},{31,15},{47,127},{63,111},{79,95},{95,79},{111,63},{127,47}} | collective-permute-start | bytes 196616 | tf_op jit(solution)/shard_map/ppermute | solution.py:513
  72.1 10.3 %collective-permute-start.11 = (f32[64,256]{1,0:T(8,128)S(1)}, f32[64,256]{1,0:T(8,128)S(1)}, u32[]{:S(2)}, u32[]{:S(2)}) collective-permute-start(f32[64,256]{1,0:T(8,128)S(1)} %get-tuple-element.55), channel_id=1, source_target_pairs={{15,111},{31,95},{47,79},{63,63},{79,47},{95,31},{111,15},{127,127}} | collective-permute-start | bytes 196616 | tf_op jit(solution)/shard_map/ppermute | solution.py:513
  76.7 5.7 %collective-permute-start.10 = (f32[64,256]{1,0:T(8,128)S(1)}, f32[64,256]{1,0:T(8,128)S(1)}, u32[]{:S(2)}, u32[]{:S(2)}) collective-permute-start(f32[64,256]{1,0:T(8,128)S(1)} %get-tuple-element.55), channel_id=1, source_target_pairs={{15,15},{31,127},{47,111},{63,95},{79,79},{95,63},{111,47},{127,31}} | collective-permute-start | bytes 196616 | tf_op jit(solution)/shard_map/ppermute | solution.py:513
  77.4 7.1 %collective-permute-start.9 = (f32[64,256]{1,0:T(8,128)S(1)}, f32[64,256]{1,0:T(8,128)S(1)}, u32[]{:S(2)}, u32[]{:S(2)}) collective-permute-start(f32[64,256]{1,0:T(8,128)S(1)} %get-tuple-element.55), channel_id=1, source_target_pairs={{15,127},{31,111},{47,95},{63,79},{79,63},{95,47},{111,31},{127,15}} | collective-permute-start | bytes 196616 | tf_op jit(solution)/shard_map/ppermute | solution.py:513
